TPU v7x, 32 devices: a whole 2x2x4 slice. The times are simulated.
32 devices in a mesh: layer: 4 (over y, x), lat: 8 (over z, core).
Axes of the slice: x: 2, y: 2, z: 4, core: 2. Of those that a mesh axis runs over, the one named last changes fastest.
Arguments:
- positions: float32 [3, 131072], P(None, ('layer', 'lat')), may hold values from 0 to 6
- velocities: float32 [3, 131072], P(None, ('layer', 'lat')), may hold values from -6 to 6
- types: int32 [131072], P(('layer', 'lat')), may hold values from 0 to 1
- counts: int32 [1024], P(('layer', 'lat')), may hold values from 0 to 128, as said below
- a_table: float32 [2, 2], replicated, may hold values from -60 to -20
- local_nbr: int32 [1024, 2], P(('layer', 'lat')), may hold values from -1 to 31, as said below
- face_nbr: int32 [1024, 2], P(('layer', 'lat')), may hold values from -1 to 7, as said below
- cross_send: int32 [32, 5, 12], P(('layer', 'lat')), may hold values from -1 to 15, as said below
- cross_pair: int32 [1024, 2], P(('layer', 'lat')), may hold values from -1 to 59, as said below
Outputs:
- new_positions: float32 [3, 131072], P(None, ('layer', 'lat'))
- new_velocities: float32 [3, 131072], P(None, ('layer', 'lat'))
Inputs may be any that keep to these rules, and one draw needn't show every extreme that they name: `counts`: some tile holds 128 beads and some none in every draw. `local_nbr`: each row lists distinct tiles of the same device, each with a higher index than the row's tile and within 8 of it, or -1. `face_nbr`: entries index the first 8 tiles of the device one place lower along lat (cyclically) in the same layer; distinct within a row, or -1. `cross_send`: entry [d, o, c] names a top tile (numbered among the last 16 tiles of device d) that device d offers to the device of the next layer at lateral offset o - 2, cyclically; -1 marks an empty slot; entries are distinct within [d, o]; for o = 2 every slot is used. `cross_pair`: entries are ghost slots o * 12 + c, distinct within a row, or -1.
All inputs are finite; a program needn't handle non-finite values.
Results may differ from a plain program's by a relative error of at most 0.0003.
Values sent between devices are 32-bit elements; how exact they have to be, the bound alone decides.
No kernel may reach another device: no remote copies, remote signals or barrier semaphores. Data moves between devices by JAX's collectives and lax.ppermute only.
A program may use at most 64 MiB of HBM per device.

v0:
```python
import functools
import math

import jax
import jax.numpy as jnp
from jax import lax
from jax.sharding import PartitionSpec as P

cutoff_force = 1.0
cutoff_density = 0.75
density_norm = 15.0 / (2.0 * math.pi * cutoff_density**3)
repulse = 25.0
friction = 4.5
time_step = 0.01
distance_floor = 0.01
far_away = 10000.0


def shifted(value, axis, by):
    length = lax.axis_size(axis)
    return lax.ppermute(value, axis, [(i, (i + by) % length) for i in range(length)])


def shifted_2(value, axis, steps):
    count = lax.axis_size(axis)
    leading, last = (max(0, -steps), min(count, count - steps))
    return lax.ppermute(value, axis, [(source, source + steps) for source in range(leading, last)])


def geometry(place_left, place_right):
    between = place_left[:, :, :, None] - place_right[:, :, None, :]
    distance = jnp.sqrt(jnp.maximum(jnp.sum(between * between, axis=1), distance_floor))
    return (between, distance)


def ordered_pairs(extent):
    rows_index = lax.broadcasted_iota(jnp.int32, (extent, extent), 0)
    cols_index = lax.broadcasted_iota(jnp.int32, (extent, extent), 1)
    return (rows_index < cols_index).astype(jnp.float32)


def density_terms(place_left, alive_left, place_right, alive_right, within):
    between, distance = geometry(place_left, place_right)
    weight = alive_left[:, :, None] * alive_right[:, None, :]
    if within:
        weight = weight * ordered_pairs(distance.shape[-1])[None]
    reach_term = jnp.maximum(1.0 - distance / cutoff_density, 0.0)
    weight = weight * density_norm * reach_term * reach_term
    return (jnp.sum(weight, axis=2), jnp.sum(weight, axis=1))


def force_terms(
    place_left,
    speed_left,
    density_left,
    species_left,
    alive_left,
    place_right,
    speed_right,
    density_right,
    strength_right,
    alive_right,
    within,
):
    between, distance = geometry(place_left, place_right)
    weight = alive_left[:, :, None] * alive_right[:, None, :]
    if within:
        weight = weight * ordered_pairs(distance.shape[-1])[None]
    conserve = jnp.maximum(1.0 - distance / cutoff_force, 0.0)
    crowding = jnp.maximum(1.0 - distance / cutoff_density, 0.0)
    amplitude = jnp.sum(species_left[:, :, :, None] * strength_right[:, :, None, :], axis=1)
    relative = speed_left[:, :, :, None] - speed_right[:, :, None, :]
    approach = jnp.sum(between * relative, axis=1) / distance
    scalar = (
        amplitude * conserve
        + repulse * (density_left[:, :, None] + density_right[:, None, :]) * crowding
    )
    scalar = scalar - friction * conserve * conserve * approach
    scalar = scalar * weight / distance
    pushed = between * scalar[:, None]
    return (jnp.sum(pushed, axis=3), -jnp.sum(pushed, axis=2))


def blocked_map(kernel, inputs):
    extent = inputs[0].shape[0]
    size_block = math.gcd(extent, 32)
    shaped = tuple(
        (
            element.reshape((extent // size_block, size_block) + element.shape[1:])
            for element in inputs
        )
    )
    results = lax.map(lambda group: kernel(*group), shaped)
    return tuple((element.reshape((extent,) + element.shape[2:]) for element in results))


def lateral_up(values):
    return shifted(values, "lat", 1)


def lateral_down(values):
    return shifted(values, "lat", -1)


def rise(values):
    return shifted_2(values, "layer", 1)


def sink(values):
    return shifted_2(values, "layer", -1)


def cross_forward(packed, offset_count, capacity):
    middle = offset_count // 2
    moved = []
    for offset in range(offset_count):
        block = packed[offset * capacity : (offset + 1) * capacity]
        if offset != middle:
            block = shifted(block, "lat", offset - middle)
        moved.append(block)
    return rise(jnp.concatenate(moved, axis=0))


def cross_backward(returned, offset_count, capacity):
    middle = offset_count // 2
    back = sink(returned)
    moved = []
    for offset in range(offset_count):
        block = back[offset * capacity : (offset + 1) * capacity]
        if offset != middle:
            block = shifted(block, "lat", middle - offset)
        moved.append(block)
    return jnp.concatenate(moved, axis=0)


def settle(total, spill, face_tiles, slot_tile, slot_used, offset_count, capacity):
    total = total.at[:face_tiles].add(lateral_down(spill[:face_tiles]))
    returned = cross_backward(spill[face_tiles:], offset_count, capacity)
    mask_shape = (slot_used.shape[0],) + (1,) * (returned.ndim - 1)
    return total.at[slot_tile].add(returned * slot_used.astype(jnp.float32).reshape(mask_shape))


def on_device(
    positions, velocities, types, counts, a_table, local_nbr, face_nbr, cross_send, cross_pair
):
    tile_count = counts.shape[0]
    tile_width = positions.shape[1] // tile_count
    face_tiles = tile_count // 4
    upper_tiles = tile_count // 2
    offset_count = cross_send.shape[1]
    capacity = cross_send.shape[2]
    ghost_slots = offset_count * capacity
    place = positions.reshape(3, tile_count, tile_width).transpose(1, 0, 2)
    speed = velocities.reshape(3, tile_count, tile_width).transpose(1, 0, 2)
    kinds_grid = types.reshape(tile_count, tile_width)
    species = (
        kinds_grid[:, None, :] == jnp.arange(a_table.shape[0], dtype=jnp.int32)[None, :, None]
    ).astype(jnp.float32)
    within_tile = lax.broadcasted_iota(jnp.int32, (tile_count, tile_width), 1)
    alive = (within_tile < counts[:, None]).astype(jnp.float32)
    symmetric = 0.5 * (a_table + a_table.T)
    strength = jnp.einsum("km,tmi->tki", symmetric, species, precision=lax.Precision.HIGHEST)
    shown = jnp.where(alive[:, None, :] > 0, place, far_away)
    payload = jnp.concatenate([shown, speed, strength], axis=1)
    offered = cross_send[0].reshape(-1)
    slot_used = offered >= 0
    slot_tile = tile_count - upper_tiles + jnp.maximum(offered, 0)
    packed = jnp.take(payload, slot_tile, axis=0)
    channel = lax.broadcasted_iota(jnp.int32, packed.shape, 1)
    packed = jnp.where((channel < 3) & jnp.logical_not(slot_used)[:, None, None], far_away, packed)
    face_ghosts = lateral_up(payload[:face_tiles])
    layer_ghosts = cross_forward(packed, offset_count, capacity)
    bottom = lax.axis_index("layer") == 0
    ghost_channel = lax.broadcasted_iota(jnp.int32, layer_ghosts.shape, 1)
    layer_ghosts = jnp.where(bottom & (ghost_channel < 3), far_away, layer_ghosts)
    union = jnp.concatenate([payload, face_ghosts, layer_ghosts], axis=0)
    union_alive = jnp.concatenate(
        [alive, jnp.ones((face_tiles + ghost_slots, tile_width), jnp.float32)], axis=0
    )
    partner = jnp.concatenate(
        [
            jnp.maximum(local_nbr, 0),
            tile_count + jnp.maximum(face_nbr, 0),
            tile_count + face_tiles + jnp.maximum(cross_pair, 0),
        ],
        axis=1,
    )
    listed = jnp.concatenate([local_nbr >= 0, face_nbr >= 0, cross_pair >= 0], axis=1)
    columns = partner.shape[1]
    flat = partner.reshape(-1)
    flat_used = listed.reshape(-1).astype(jnp.float32)

    def repeated(values):
        return jnp.repeat(values, columns, axis=0)

    right_payload = jnp.take(union, flat, axis=0)
    right_alive = jnp.take(union_alive, flat, axis=0) * flat_used[:, None]
    self_rows, self_cols = blocked_map(
        functools.partial(density_terms, within=True), (place, alive, place, alive)
    )
    pair_rows, pair_cols = blocked_map(
        functools.partial(density_terms, within=False),
        (repeated(place), repeated(alive), right_payload[:, 0:3], right_alive),
    )
    spill = jnp.zeros((union.shape[0], tile_width), jnp.float32).at[flat].add(pair_cols)
    density = (
        self_rows + self_cols + jnp.sum(pair_rows.reshape(tile_count, columns, tile_width), axis=1)
    )
    density = density + spill[:tile_count]
    density = settle(
        density, spill[tile_count:], face_tiles, slot_tile, slot_used, offset_count, capacity
    )
    face_density = lateral_up(density[:face_tiles])
    layer_density = cross_forward(jnp.take(density, slot_tile, axis=0), offset_count, capacity)
    union_density = jnp.concatenate([density, face_density, layer_density], axis=0)
    self_force, self_back = blocked_map(
        functools.partial(force_terms, within=True),
        (place, speed, density, species, alive, place, speed, density, strength, alive),
    )
    pair_force, pair_back = blocked_map(
        functools.partial(force_terms, within=False),
        (
            repeated(place),
            repeated(speed),
            repeated(density),
            repeated(species),
            repeated(alive),
            right_payload[:, 0:3],
            right_payload[:, 3:6],
            jnp.take(union_density, flat, axis=0),
            right_payload[:, 6:],
            right_alive,
        ),
    )
    spill_force = jnp.zeros((union.shape[0], 3, tile_width), jnp.float32).at[flat].add(pair_back)
    force = (
        self_force
        + self_back
        + jnp.sum(pair_force.reshape(tile_count, columns, 3, tile_width), axis=1)
    )
    force = force + spill_force[:tile_count]
    force = settle(
        force, spill_force[tile_count:], face_tiles, slot_tile, slot_used, offset_count, capacity
    )
    speed_next = (speed + time_step * force) * alive[:, None, :]
    place_next = (place + time_step * speed_next) * alive[:, None, :]
    new_positions = place_next.transpose(1, 0, 2).reshape(3, tile_count * tile_width)
    new_velocities = speed_next.transpose(1, 0, 2).reshape(3, tile_count * tile_width)
    return (new_positions, new_velocities)


def solution(mesh):
    placed = (
        P(None, ("layer", "lat")),
        P(None, ("layer", "lat")),
        P(("layer", "lat")),
        P(("layer", "lat")),
        P(),
        P(("layer", "lat"), None),
        P(("layer", "lat"), None),
        P(("layer", "lat"), None, None),
        P(("layer", "lat"), None),
    )
    return jax.shard_map(
        on_device,
        mesh=mesh,
        in_specs=placed,
        out_specs=(P(None, ("layer", "lat")), P(None, ("layer", "lat"))),
        check_vma=False,
    )
```

profile of v0, /device:TPU:4, one launch (start us, length us, event | category | flops | bytes accessed | tf_op | source)
XLA Modules:
  0.0 276.0 jit_solution(14007558690981432703)
XLA Ops:
  8.2 3.6 %collective-permute-start.2 = (f32[12,8,128]{2,1,0:T(8,128)S(1)}, f32[12,8,128]{2,1,0:T(8,128)S(1)}, u32[]{:S(2)}, u32[]{:S(2)}) collective-permute-start(f32[12,8,128]{2,1,0:T(8,128)S(1)} %get-tuple-element.300), channel_id=1, source_target_pairs={{0,7},{1,0},{2,1},{3,2},{4,3},{5,4},{6,5},{7,6},{8,15},{9,8},{10,9... | collective-permute-start | bytes 147464 | tf_op jit(solution)/shard_map/ppermute | solution.py:21
  18.8 5.5 %fusion.13 = (f32[32,128,128]{2,1,0:T(8,128)}, f32[32,128,128]{2,1,0:T(8,128)S(1)}) fusion(f32[32,3,128]{2,1,0:T(4,128)S(1)} %bitcast.117, f32[32,3,128]{2,1,0:T(4,128)S(1)} %bitcast.111), kind=kLoop, calls=%fused_computation.50 | loop fusion | flops 8388608 | bytes 4292608 | tf_op jit(solution)/shard_map/while/body/eval_jaxpr/reduce_sum | solution.py:73
  24.3 2.4 fusion.18
  27.1 5.0 %collective-permute-done.3 = f32[12,8,128]{2,1,0:T(8,128)S(1)} collective-permute-done((f32[12,8,128]{2,1,0:T(8,128)S(1)}, f32[12,8,128]{2,1,0:T(8,128)S(1)}, u32[]{:S(2)}, u32[]{:S(2)}) %collective-permute-start.3) | collective-permute-done | bytes 49184 | tf_op jit(solution)/shard_map/ppermute | solution.py:21
  33.2 3.4 %collective-permute-start.5 = (f32[60,8,128]{2,1,0:T(8,128)S(1)}, f32[60,8,128]{2,1,0:T(8,128)S(1)}, u32[]{:S(2)}, u32[]{:S(2)}) collective-permute-start(f32[60,8,128]{2,1,0:T(8,128)S(1)} %constant_dynamic-update-slice_fusion), channel_id=1, source_target_pairs={{0,8},{8,16},{16,24},{1,9},{9,17},{17,25},{2,10},{10,18},{18,26},{... | collective-permute-start | bytes 737288 | tf_op jit(solution)/shard_map/ppermute | solution.py:27
  39.0 4.9 %collective-permute-done.5 = f32[60,8,128]{2,1,0:T(8,128)S(1)} collective-permute-done((f32[60,8,128]{2,1,0:T(8,128)S(1)}, f32[60,8,128]{2,1,0:T(8,128)S(1)}, u32[]{:S(2)}, u32[]{:S(2)}) %collective-permute-start.5) | collective-permute-done | bytes 245792 | tf_op jit(solution)/shard_map/ppermute | solution.py:27
  49.7 40.0 %while.8 = (s32[]{:T(128)}, f32[6,32,128]{2,1,0:T(8,128)}, f32[6,32,128]{2,1,0:T(8,128)}, f32[6,32,128]{2,1,0:T(8,128)S(1)}, f32[6,32,128]{2,1,0:T(8,128)}, /*in...) while((s32[]{:T(128)}, f32[6,32,128]{2,1,0:T(8,128)}, f32[6,32,128]{2,1,0:T(8,128)}, ...), condition=%wide.region_8.10_spmd, body=%wide.region_4.9_spmd.sunk | while | flops 9428994 | bytes 4685933 | solution.py:93
  51.2 2.1 multiply_reduce_fusion.5
  57.9 2.1 multiply_reduce_fusion.5
  64.6 2.1 multiply_reduce_fusion.5
  71.3 2.1 multiply_reduce_fusion.5
  77.9 2.1 multiply_reduce_fusion.5
  84.6 2.1 multiply_reduce_fusion.5
  89.7 2.1 scatter_custom_fusion
  94.6 2.4 collective-permute-start.7
  108.5 5.2 %concatenate.40 = f32[60,128]{1,0:T(8,128)} concatenate(f32[12,128]{1,0:T(8,128)} %copy-done.12, f32[12,128]{1,0:T(8,128)} %copy-done.11, f32[12,128]{1,0:T(8,128)S(1)} %get-tuple-element.316, f32[12,128]{1,0:T(8,128)} %copy-done.10, f32[12,128]{1,0:T(8,128)S(1)} %collective-permute-done.11), dimensions={0} | concatenate | bytes 61440 | tf_op jit(solution)/shard_map/concatenate | solution.py:133
  117.9 3.4 %collective-permute-start.14 = (f32[12,128]{1,0:T(8,128)}, f32[12,128]{1,0:T(8,128)}, u32[]{:S(2)}, u32[]{:S(2)}) collective-permute-start(f32[12,128]{1,0:T(8,128)} %get-tuple-element.312), channel_id=1, source_target_pairs={{0,7},{1,0},{2,1},{3,2},{4,3},{5,4},{6,5},{7,6},{8,15},{9,8},{10,9... | collective-permute-start | bytes 18440 | tf_op jit(solution)/shard_map/ppermute | solution.py:21
  121.3 2.0 collective-permute-start.13
  123.3 3.4 %multiply_reduce_fusion.2 = f32[32,128,128]{2,1,0:T(8,128)} fusion(f32[32,2,128]{2,1,0:T(2,128)} %copy-done.6, f32[32,2,128]{2,1,0:T(2,128)} %fusion.23), kind=kLoop, calls=%fused_computation.51 | loop fusion | flops 1572864 | bytes 2162688 | tf_op jit(solution)/shard_map/while/body/eval_jaxpr/reduce_sum | solution.py:71
  127.5 2.9 %concatenate.41 = f32[60,128]{1,0:T(8,128)S(1)} concatenate(f32[12,128]{1,0:T(8,128)} %collective-permute-done.13, f32[12,128]{1,0:T(8,128)} %collective-permute-done.14, f32[12,128]{1,0:T(8,128)S(1)} %get-tuple-element.311, f32[12,128]{1,0:T(8,128)} %collective-permute-done.15, f32[12,128]{1,0:T(8,128)} %collective-permute-done.16), dimensions={0} | concatenate | bytes 61440 | tf_op jit(solution)/shard_map/concatenate | solution.py:121
  130.5 4.2 %collective-permute-start.17 = (f32[60,128]{1,0:T(8,128)S(1)}, f32[60,128]{1,0:T(8,128)S(1)}, u32[]{:S(2)}, u32[]{:S(2)}) collective-permute-start(f32[60,128]{1,0:T(8,128)S(1)} %concatenate.41), channel_id=1, source_target_pairs={{0,8},{8,16},{16,24},{1,9},{9,17},{17,25},{2,10},{10,18},{18,26},{... | collective-permute-start | bytes 92168 | tf_op jit(solution)/shard_map/ppermute | solution.py:27
  134.7 5.1 %fusion.17 = f32[32,128,128]{2,1,0:T(8,128)} fusion(f32[32,128,128]{2,1,0:T(8,128)} %get-tuple-element.245, f32[32,128,128]{2,1,0:T(8,128)} %multiply_reduce_fusion.2, f32[32,128,128]{2,1,0:T(8,128)S(1)} %get-tuple-element.246, f32[32,128]{1,0:T(8,128)S(1)} %scatter_custom_fusion.1, f32[128,128]{1,0:T(8,128)} %copy-done.3, f32[32,128]{1,0:T(8,128)S(1)} %get-tuple-element.320), kind=kLoop, calls=%fused_computation.57 | loop fusion | flops 10485760 | bytes 8486912 | tf_op jit(solution)/shard_map/while/body/eval_jaxpr/div | solution.py:79
  141.6 98.1 %while.9 = (s32[]{:T(128)}, f32[6,32,3,128]{3,2,1,0:T(4,128)}, f32[6,32,3,128]{3,2,1,0:T(4,128)}, f32[6,32,3,128]{3,2,1,0:T(4,128)}, f32[6,32,3,128]{3,2,1,0:T(4...) while((s32[]{:T(128)}, f32[6,32,3,128]{3,2,1,0:T(4,128)}, ...), condition=%wide.region_21.23_spmd, body=%wide.region_15.22_spmd.sunk | while | flops 26202112 | bytes 18186424 | solution.py:93
  147.1 4.1 %fusion.51 = (f32[32,128,128]{2,1,0:T(8,128)S(1)}, f32[32,128,128]{2,1,0:T(8,128)S(1)}) fusion(f32[32,3,128]{2,1,0:T(4,128)S(1)} %dynamic-slice_bitcast_fusion.28, f32[32,3,128]{2,1,0:T(4,128)S(1)} %dynamic-slice_bitcast_fusion.29, f32[32,3,128]{2,1,0:T(4,128)S(1)} %dynamic-slice_bitcast_fusion.30, f32[32,3,128]{2,1,0:T(4,128)S(1)} %dynamic-slice_bitcast_fusion.31), kind=kLoop, calls=%fused_computation.24.clone.1 | loop fusion | flops 8388608 | bytes 4390912 | tf_op jit(solution)/shard_map/while/body/eval_jaxpr/reduce_sum | solution.py:32
  151.2 2.0 fusion.52
  153.2 4.1 %fusion.53 = (f32[32,3,128]{2,1,0:T(4,128)S(1)}, f32[32,3,128]{2,1,0:T(4,128)S(1)}) fusion(f32[32,128,128]{2,1,0:T(8,128)S(1)} %fusion.52, f32[32,3,128]{2,1,0:T(4,128)S(1)} %dynamic-slice_bitcast_fusion.28, f32[32,3,128]{2,1,0:T(4,128)S(1)} %dynamic-slice_bitcast_fusion.29), kind=kLoop, calls=%fused_computation.22.clone.1 | loop fusion | flops 6266880 | bytes 2293760 | tf_op jit(solution)/shard_map/while/body/eval_jaxpr/reduce_sum | solution.py:81
  163.4 4.1 %fusion.51 = (f32[32,128,128]{2,1,0:T(8,128)S(1)}, f32[32,128,128]{2,1,0:T(8,128)S(1)}) fusion(f32[32,3,128]{2,1,0:T(4,128)S(1)} %dynamic-slice_bitcast_fusion.28, f32[32,3,128]{2,1,0:T(4,128)S(1)} %dynamic-slice_bitcast_fusion.29, f32[32,3,128]{2,1,0:T(4,128)S(1)} %dynamic-slice_bitcast_fusion.30, f32[32,3,128]{2,1,0:T(4,128)S(1)} %dynamic-slice_bitcast_fusion.31), kind=kLoop, calls=%fused_computation.24.clone.1 | loop fusion | flops 8388608 | bytes 4390912 | tf_op jit(solution)/shard_map/while/body/eval_jaxpr/reduce_sum | solution.py:32
  167.5 2.0 fusion.52
  169.6 4.1 %fusion.53 = (f32[32,3,128]{2,1,0:T(4,128)S(1)}, f32[32,3,128]{2,1,0:T(4,128)S(1)}) fusion(f32[32,128,128]{2,1,0:T(8,128)S(1)} %fusion.52, f32[32,3,128]{2,1,0:T(4,128)S(1)} %dynamic-slice_bitcast_fusion.28, f32[32,3,128]{2,1,0:T(4,128)S(1)} %dynamic-slice_bitcast_fusion.29), kind=kLoop, calls=%fused_computation.22.clone.1 | loop fusion | flops 6266880 | bytes 2293760 | tf_op jit(solution)/shard_map/while/body/eval_jaxpr/reduce_sum | solution.py:81
  179.7 4.1 %fusion.51 = (f32[32,128,128]{2,1,0:T(8,128)S(1)}, f32[32,128,128]{2,1,0:T(8,128)S(1)}) fusion(f32[32,3,128]{2,1,0:T(4,128)S(1)} %dynamic-slice_bitcast_fusion.28, f32[32,3,128]{2,1,0:T(4,128)S(1)} %dynamic-slice_bitcast_fusion.29, f32[32,3,128]{2,1,0:T(4,128)S(1)} %dynamic-slice_bitcast_fusion.30, f32[32,3,128]{2,1,0:T(4,128)S(1)} %dynamic-slice_bitcast_fusion.31), kind=kLoop, calls=%fused_computation.24.clone.1 | loop fusion | flops 8388608 | bytes 4390912 | tf_op jit(solution)/shard_map/while/body/eval_jaxpr/reduce_sum | solution.py:32
  183.8 2.0 fusion.52
  185.9 4.1 %fusion.53 = (f32[32,3,128]{2,1,0:T(4,128)S(1)}, f32[32,3,128]{2,1,0:T(4,128)S(1)}) fusion(f32[32,128,128]{2,1,0:T(8,128)S(1)} %fusion.52, f32[32,3,128]{2,1,0:T(4,128)S(1)} %dynamic-slice_bitcast_fusion.28, f32[32,3,128]{2,1,0:T(4,128)S(1)} %dynamic-slice_bitcast_fusion.29), kind=kLoop, calls=%fused_computation.22.clone.1 | loop fusion | flops 6266880 | bytes 2293760 | tf_op jit(solution)/shard_map/while/body/eval_jaxpr/reduce_sum | solution.py:81
  196.1 4.1 %fusion.51 = (f32[32,128,128]{2,1,0:T(8,128)S(1)}, f32[32,128,128]{2,1,0:T(8,128)S(1)}) fusion(f32[32,3,128]{2,1,0:T(4,128)S(1)} %dynamic-slice_bitcast_fusion.28, f32[32,3,128]{2,1,0:T(4,128)S(1)} %dynamic-slice_bitcast_fusion.29, f32[32,3,128]{2,1,0:T(4,128)S(1)} %dynamic-slice_bitcast_fusion.30, f32[32,3,128]{2,1,0:T(4,128)S(1)} %dynamic-slice_bitcast_fusion.31), kind=kLoop, calls=%fused_computation.24.clone.1 | loop fusion | flops 8388608 | bytes 4390912 | tf_op jit(solution)/shard_map/while/body/eval_jaxpr/reduce_sum | solution.py:32
  200.2 2.0 fusion.52
  202.2 4.1 %fusion.53 = (f32[32,3,128]{2,1,0:T(4,128)S(1)}, f32[32,3,128]{2,1,0:T(4,128)S(1)}) fusion(f32[32,128,128]{2,1,0:T(8,128)S(1)} %fusion.52, f32[32,3,128]{2,1,0:T(4,128)S(1)} %dynamic-slice_bitcast_fusion.28, f32[32,3,128]{2,1,0:T(4,128)S(1)} %dynamic-slice_bitcast_fusion.29), kind=kLoop, calls=%fused_computation.22.clone.1 | loop fusion | flops 6266880 | bytes 2293760 | tf_op jit(solution)/shard_map/while/body/eval_jaxpr/reduce_sum | solution.py:81
  212.4 4.1 %fusion.51 = (f32[32,128,128]{2,1,0:T(8,128)S(1)}, f32[32,128,128]{2,1,0:T(8,128)S(1)}) fusion(f32[32,3,128]{2,1,0:T(4,128)S(1)} %dynamic-slice_bitcast_fusion.28, f32[32,3,128]{2,1,0:T(4,128)S(1)} %dynamic-slice_bitcast_fusion.29, f32[32,3,128]{2,1,0:T(4,128)S(1)} %dynamic-slice_bitcast_fusion.30, f32[32,3,128]{2,1,0:T(4,128)S(1)} %dynamic-slice_bitcast_fusion.31), kind=kLoop, calls=%fused_computation.24.clone.1 | loop fusion | flops 8388608 | bytes 4390912 | tf_op jit(solution)/shard_map/while/body/eval_jaxpr/reduce_sum | solution.py:32
  216.5 2.0 fusion.52
  218.5 4.1 %fusion.53 = (f32[32,3,128]{2,1,0:T(4,128)S(1)}, f32[32,3,128]{2,1,0:T(4,128)S(1)}) fusion(f32[32,128,128]{2,1,0:T(8,128)S(1)} %fusion.52, f32[32,3,128]{2,1,0:T(4,128)S(1)} %dynamic-slice_bitcast_fusion.28, f32[32,3,128]{2,1,0:T(4,128)S(1)} %dynamic-slice_bitcast_fusion.29), kind=kLoop, calls=%fused_computation.22.clone.1 | loop fusion | flops 6266880 | bytes 2293760 | tf_op jit(solution)/shard_map/while/body/eval_jaxpr/reduce_sum | solution.py:81
  228.7 4.1 %fusion.51 = (f32[32,128,128]{2,1,0:T(8,128)S(1)}, f32[32,128,128]{2,1,0:T(8,128)S(1)}) fusion(f32[32,3,128]{2,1,0:T(4,128)S(1)} %dynamic-slice_bitcast_fusion.28, f32[32,3,128]{2,1,0:T(4,128)S(1)} %dynamic-slice_bitcast_fusion.29, f32[32,3,128]{2,1,0:T(4,128)S(1)} %dynamic-slice_bitcast_fusion.30, f32[32,3,128]{2,1,0:T(4,128)S(1)} %dynamic-slice_bitcast_fusion.31), kind=kLoop, calls=%fused_computation.24.clone.1 | loop fusion | flops 8388608 | bytes 4390912 | tf_op jit(solution)/shard_map/while/body/eval_jaxpr/reduce_sum | solution.py:32
  232.8 2.0 fusion.52
  234.9 4.1 %fusion.53 = (f32[32,3,128]{2,1,0:T(4,128)S(1)}, f32[32,3,128]{2,1,0:T(4,128)S(1)}) fusion(f32[32,128,128]{2,1,0:T(8,128)S(1)} %fusion.52, f32[32,3,128]{2,1,0:T(4,128)S(1)} %dynamic-slice_bitcast_fusion.28, f32[32,3,128]{2,1,0:T(4,128)S(1)} %dynamic-slice_bitcast_fusion.29), kind=kLoop, calls=%fused_computation.22.clone.1 | loop fusion | flops 6266880 | bytes 2293760 | tf_op jit(solution)/shard_map/while/body/eval_jaxpr/reduce_sum | solution.py:81
  239.7 13.1 %scatter_fusion = f32[100,3,128]{2,1,0:T(4,128)S(1)} fusion(f32[100,3,128]{2,1,0:T(4,128)S(1)} %broadcast_in_dim.180, s32[192]{0:T(256)S(1)} %bitcast.132, f32[192,3,128]{2,1,0:T(4,128)} %bitcast.126), kind=kCustom, calls=%fused_computation.7 | custom fusion | flops 73728 | bytes 885504 | tf_op jit(solution)/shard_map/scatter-add | solution.py:235
  252.9 2.8 %collective-permute-start.19 = (f32[60,3,128]{2,1,0:T(4,128)S(1)}, f32[60,3,128]{2,1,0:T(4,128)S(1)}, u32[]{:S(2)}, u32[]{:S(2)}) collective-permute-start(f32[60,3,128]{2,1,0:T(4,128)S(1)} %slice.213), channel_id=1, source_target_pairs={{8,0},{16,8},{24,16},{9,1},{17,9},{25,17},{10,2},{18,10},{26,18},{... | collective-permute-start | bytes 276488 | tf_op jit(solution)/shard_map/ppermute | solution.py:27
  255.7 3.8 %fusion.10 = (f32[32,3,128]{2,1,0:T(4,128)S(1)}, f32[32,3,128]{2,1,0:T(4,128)S(1)}) fusion(f32[32,128,128]{2,1,0:T(8,128)S(1)} %copy-done, f32[32,3,128]{2,1,0:T(4,128)S(1)} %bitcast.113), kind=kLoop, calls=%fused_computation.47 | loop fusion | flops 6266880 | bytes 2244608 | tf_op jit(solution)/shard_map/while/body/eval_jaxpr/reduce_sum | solution.py:81
  259.6 3.0 %collective-permute-start.18 = (f32[8,3,128]{2,1,0:T(4,128)S(1)}, f32[8,3,128]{2,1,0:T(4,128)S(1)}, u32[]{:S(2)}, u32[]{:S(2)}) collective-permute-start(f32[8,3,128]{2,1,0:T(4,128)S(1)} %slice.212), channel_id=1, source_target_pairs={{0,7},{1,0},{2,1},{3,2},{4,3},{5,4},{6,5},{7,6},{8,15},{9,8},{10,9... | collective-permute-start | bytes 36872 | tf_op jit(solution)/shard_map/ppermute | solution.py:21
  262.8 5.5 %collective-permute-done.20 = f32[12,3,128]{2,1,0:T(4,128)S(1)} collective-permute-done((f32[12,3,128]{2,1,0:T(4,128)S(1)}, f32[12,3,128]{2,1,0:T(4,128)S(1)}, u32[]{:S(2)}, u32[]{:S(2)}) %collective-permute-start.20) | collective-permute-done | bytes 18464 | tf_op jit(solution)/shard_map/ppermute | solution.py:21
  270.0 2.3 collective-permute-done.23
  272.5 2.9 %scatter_fusion.1 = f32[32,3,128]{2,1,0:T(4,128)S(1)} fusion(f32[32,3,128]{2,1,0:T(4,128)S(1)} %fusion.26, s32[60]{0:T(128)S(1)} %copy-done.19, f32[60,3,128]{2,1,0:T(4,128)S(1)} %broadcast_multiply_fusion), kind=kCustom, calls=%fused_computation.8 | custom fusion | flops 23040 | bytes 276720 | tf_op jit(solution)/shard_map/scatter-add | solution.py:140
  (273 shorter events, 111.6 us)
Async XLA Ops:
  0.6 18.2 %copy-start.1 = (f32[3,4096]{1,0:T(4,128)S(1)}, f32[3,4096]{1,0:T(4,128)}, u32[]{:S(2)}) copy-start(f32[3,4096]{1,0:T(4,128)} %param.19) | copy-start | bytes 147460
  0.6 18.2 %copy-start.2 = (f32[3,4096]{1,0:T(4,128)S(1)}, f32[3,4096]{1,0:T(4,128)}, u32[]{:S(2)}) copy-start(f32[3,4096]{1,0:T(4,128)} %param.20) | copy-start | bytes 147460
  3.1 40.8 %copy-start.6 = (f32[32,2,128]{2,1,0:T(2,128)}, f32[32,2,128]{2,1,0:T(2,128)S(1)}, u32[]{:S(2)}) copy-start(f32[32,2,128]{2,1,0:T(2,128)S(1)} %convolution_bitcast_fusion) | copy-start | bytes 98308
  4.9 39.0 %collective-permute-start = (f32[8,8,128]{2,1,0:T(8,128)S(1)}, f32[8,8,128]{2,1,0:T(8,128)}, u32[]{:S(2)}, u32[]{:S(2)}) collective-permute-start(f32[8,8,128]{2,1,0:T(8,128)S(1)} %slice.186), channel_id=1, source_target_pairs={{0,1},{1,2},{2,3},{3,4},{4,5},{5,6},{6,7},{7,0},{8,9},{9,10},{10,1... | collective-permute-start | bytes 98312 | tf_op jit(solution)/shard_map/ppermute | solution.py:21
  6.8 0.5 copy-start.18
  7.3 9.7 %copy-start.13 = (s32[1024]{0:T(1024)}, s32[1024]{0:T(1024)S(1)}, u32[]{:S(2)}) copy-start(s32[1024]{0:T(1024)S(1)} %pad_clamp_fusion.1) | copy-start | bytes 12292
  8.0 5.6 %copy-start.17 = (pred[60]{0:T(512)(128)(4,1)}, pred[60]{0:T(512)(128)(4,1)S(1)}, u32[]{:S(2)}) copy-start(pred[60]{0:T(512)(128)(4,1)S(1)} %compare_and_fusion.1) | copy-start | bytes 184
  8.2 18.5 %collective-permute-start.2 = (f32[12,8,128]{2,1,0:T(8,128)S(1)}, f32[12,8,128]{2,1,0:T(8,128)S(1)}, u32[]{:S(2)}, u32[]{:S(2)}) collective-permute-start(f32[12,8,128]{2,1,0:T(8,128)S(1)} %get-tuple-element.300), channel_id=1, source_target_pairs={{0,7},{1,0},{2,1},{3,2},{4,3},{5,4},{6,5},{7,6},{8,15},{9,8},{10,9... | collective-permute-start | bytes 147464 | tf_op jit(solution)/shard_map/ppermute | solution.py:21
  11.8 14.9 %collective-permute-start.1 = (f32[12,8,128]{2,1,0:T(8,128)S(1)}, f32[12,8,128]{2,1,0:T(8,128)S(1)}, u32[]{:S(2)}, u32[]{:S(2)}) collective-permute-start(f32[12,8,128]{2,1,0:T(8,128)S(1)} %get-tuple-element.301), channel_id=1, source_target_pairs={{0,6},{1,7},{2,0},{3,1},{4,2},{5,3},{6,4},{7,5},{8,14},{9,15},{10,... | collective-permute-start | bytes 147464 | tf_op jit(solution)/shard_map/ppermute | solution.py:21
  17.4 29.2 %copy-start.14 = (pred[192]{0:T(512)(128)(4,1)}, pred[192]{0:T(512)(128)(4,1)S(1)}, u32[]{:S(2)}) copy-start(pred[192]{0:T(512)(128)(4,1)S(1)} %compare_and_fusion) | copy-start | bytes 580
  18.8 5.5 %copy-start.3 = (f32[128,128]{1,0:T(8,128)}, f32[128,128]{1,0:T(8,128)S(1)}, u32[]{:S(2)}) copy-start(f32[128,128]{1,0:T(8,128)S(1)} %fusion.20) | copy-start | bytes 196612
  18.8 7.9 %copy-start.8 = (s32[192,1]{0,1:T(1,128)}, s32[192,1]{0,1:T(1,128)S(1)}, u32[]{:S(2)}) copy-start(s32[192,1]{0,1:T(1,128)S(1)} %compare_select_fusion) | copy-start | bytes 2308
  18.8 18.7 %copy-start.7 = (s32[1024]{0:T(1024)}, s32[1024]{0:T(1024)S(1)}, u32[]{:S(2)}) copy-start(s32[1024]{0:T(1024)S(1)} %pad_clamp_fusion.2) | copy-start | bytes 12292
  26.7 5.4 %collective-permute-start.3 = (f32[12,8,128]{2,1,0:T(8,128)S(1)}, f32[12,8,128]{2,1,0:T(8,128)S(1)}, u32[]{:S(2)}, u32[]{:S(2)}) collective-permute-start(f32[12,8,128]{2,1,0:T(8,128)S(1)} %get-tuple-element.298), channel_id=1, source_target_pairs={{0,1},{1,2},{2,3},{3,4},{4,5},{5,6},{6,7},{7,0},{8,9},{9,10},{10,1... | collective-permute-start | bytes 147464 | tf_op jit(solution)/shard_map/ppermute | solution.py:21
  26.8 6.3 %collective-permute-start.4 = (f32[12,8,128]{2,1,0:T(8,128)S(1)}, f32[12,8,128]{2,1,0:T(8,128)S(1)}, u32[]{:S(2)}, u32[]{:S(2)}) collective-permute-start(f32[12,8,128]{2,1,0:T(8,128)S(1)} %get-tuple-element.297), channel_id=1, source_target_pairs={{0,2},{1,3},{2,4},{3,5},{4,6},{5,7},{6,0},{7,1},{8,10},{9,11},{10,... | collective-permute-start | bytes 147464 | tf_op jit(solution)/shard_map/ppermute | solution.py:21
  33.2 10.7 %collective-permute-start.5 = (f32[60,8,128]{2,1,0:T(8,128)S(1)}, f32[60,8,128]{2,1,0:T(8,128)S(1)}, u32[]{:S(2)}, u32[]{:S(2)}) collective-permute-start(f32[60,8,128]{2,1,0:T(8,128)S(1)} %constant_dynamic-update-slice_fusion), channel_id=1, source_target_pairs={{0,8},{8,16},{16,24},{1,9},{9,17},{17,25},{2,10},{10,18},{18,26},{... | collective-permute-start | bytes 737288 | tf_op jit(solution)/shard_map/ppermute | solution.py:27
  94.5 9.8 %collective-permute-start.6 = (f32[8,128]{1,0:T(8,128)}, f32[8,128]{1,0:T(8,128)}, u32[]{:S(2)}, u32[]{:S(2)}) collective-permute-start(f32[8,128]{1,0:T(8,128)} %slice.195), channel_id=1, source_target_pairs={{0,7},{1,0},{2,1},{3,2},{4,3},{5,4},{6,5},{7,6},{8,15},{9,8},{10,9... | collective-permute-start | bytes 12296 | tf_op jit(solution)/shard_map/ppermute | solution.py:21
  94.6 6.3 %collective-permute-start.7 = (f32[60,128]{1,0:T(8,128)}, f32[60,128]{1,0:T(8,128)}, u32[]{:S(2)}, u32[]{:S(2)}) collective-permute-start(f32[60,128]{1,0:T(8,128)} %slice.196), channel_id=1, source_target_pairs={{8,0},{16,8},{24,16},{9,1},{17,9},{25,17},{10,2},{18,10},{26,18},{... | collective-permute-start | bytes 92168 | tf_op jit(solution)/shard_map/ppermute | solution.py:27
  101.7 3.7 %collective-permute-start.11 = (f32[12,128]{1,0:T(8,128)S(1)}, f32[12,128]{1,0:T(8,128)S(1)}, u32[]{:S(2)}, u32[]{:S(2)}) collective-permute-start(f32[12,128]{1,0:T(8,128)S(1)} %get-tuple-element.314), channel_id=1, source_target_pairs={{0,6},{1,7},{2,0},{3,1},{4,2},{5,3},{6,4},{7,5},{8,14},{9,15},{10,... | collective-permute-start | bytes 18440 | tf_op jit(solution)/shard_map/ppermute | solution.py:21
  102.0 3.4 %collective-permute-start.10 = (f32[12,128]{1,0:T(8,128)S(1)}, f32[12,128]{1,0:T(8,128)S(1)}, u32[]{:S(2)}, u32[]{:S(2)}) collective-permute-start(f32[12,128]{1,0:T(8,128)S(1)} %get-tuple-element.315), channel_id=1, source_target_pairs={{0,7},{1,0},{2,1},{3,2},{4,3},{5,4},{6,5},{7,6},{8,15},{9,8},{10,9... | collective-permute-start | bytes 18440 | tf_op jit(solution)/shard_map/ppermute | solution.py:21
  102.0 4.9 %collective-permute-start.9 = (f32[12,128]{1,0:T(8,128)S(1)}, f32[12,128]{1,0:T(8,128)S(1)}, u32[]{:S(2)}, u32[]{:S(2)}) collective-permute-start(f32[12,128]{1,0:T(8,128)S(1)} %get-tuple-element.317), channel_id=1, source_target_pairs={{0,1},{1,2},{2,3},{3,4},{4,5},{5,6},{6,7},{7,0},{8,9},{9,10},{10,1... | collective-permute-start | bytes 18440 | tf_op jit(solution)/shard_map/ppermute | solution.py:21
  102.5 5.4 %collective-permute-start.8 = (f32[12,128]{1,0:T(8,128)S(1)}, f32[12,128]{1,0:T(8,128)S(1)}, u32[]{:S(2)}, u32[]{:S(2)}) collective-permute-start(f32[12,128]{1,0:T(8,128)S(1)} %get-tuple-element.318), channel_id=1, source_target_pairs={{0,2},{1,3},{2,4},{3,5},{4,6},{5,7},{6,0},{7,1},{8,10},{9,11},{10,... | collective-permute-start | bytes 18440 | tf_op jit(solution)/shard_map/ppermute | solution.py:21
  105.3 2.6 copy-start.10
  106.8 1.1 copy-start.11
  107.9 0.6 copy-start.12
  117.7 9.8 %collective-permute-start.16 = (f32[12,128]{1,0:T(8,128)}, f32[12,128]{1,0:T(8,128)}, u32[]{:S(2)}, u32[]{:S(2)}) collective-permute-start(f32[12,128]{1,0:T(8,128)} %get-tuple-element.309), channel_id=1, source_target_pairs={{0,2},{1,3},{2,4},{3,5},{4,6},{5,7},{6,0},{7,1},{8,10},{9,11},{10,... | collective-permute-start | bytes 18440 | tf_op jit(solution)/shard_map/ppermute | solution.py:21
  117.7 9.8 %collective-permute-start.15 = (f32[12,128]{1,0:T(8,128)}, f32[12,128]{1,0:T(8,128)}, u32[]{:S(2)}, u32[]{:S(2)}) collective-permute-start(f32[12,128]{1,0:T(8,128)} %get-tuple-element.310), channel_id=1, source_target_pairs={{0,1},{1,2},{2,3},{3,4},{4,5},{5,6},{6,7},{7,0},{8,9},{9,10},{10,1... | collective-permute-start | bytes 18440 | tf_op jit(solution)/shard_map/ppermute | solution.py:21
  117.9 9.6 %collective-permute-start.14 = (f32[12,128]{1,0:T(8,128)}, f32[12,128]{1,0:T(8,128)}, u32[]{:S(2)}, u32[]{:S(2)}) collective-permute-start(f32[12,128]{1,0:T(8,128)} %get-tuple-element.312), channel_id=1, source_target_pairs={{0,7},{1,0},{2,1},{3,2},{4,3},{5,4},{6,5},{7,6},{8,15},{9,8},{10,9... | collective-permute-start | bytes 18440 | tf_op jit(solution)/shard_map/ppermute | solution.py:21
  121.3 6.2 %collective-permute-start.13 = (f32[12,128]{1,0:T(8,128)S(1)}, f32[12,128]{1,0:T(8,128)}, u32[]{:S(2)}, u32[]{:S(2)}) collective-permute-start(f32[12,128]{1,0:T(8,128)S(1)} %get-tuple-element.313), channel_id=1, source_target_pairs={{0,6},{1,7},{2,0},{3,1},{4,2},{5,3},{6,4},{7,5},{8,14},{9,15},{10,... | collective-permute-start | bytes 18440 | tf_op jit(solution)/shard_map/ppermute | solution.py:21
  127.5 12.3 %collective-permute-start.12 = (f32[8,128]{1,0:T(8,128)S(1)}, f32[8,128]{1,0:T(8,128)S(1)}, u32[]{:S(2)}, u32[]{:S(2)}) collective-permute-start(f32[8,128]{1,0:T(8,128)S(1)} %slice.203), channel_id=1, source_target_pairs={{0,1},{1,2},{2,3},{3,4},{4,5},{5,6},{6,7},{7,0},{8,9},{9,10},{10,1... | collective-permute-start | bytes 12296 | tf_op jit(solution)/shard_map/ppermute | solution.py:21
  130.5 9.4 %collective-permute-start.17 = (f32[60,128]{1,0:T(8,128)S(1)}, f32[60,128]{1,0:T(8,128)S(1)}, u32[]{:S(2)}, u32[]{:S(2)}) collective-permute-start(f32[60,128]{1,0:T(8,128)S(1)} %concatenate.41), channel_id=1, source_target_pairs={{0,8},{8,16},{16,24},{1,9},{9,17},{17,25},{2,10},{10,18},{18,26},{... | collective-permute-start | bytes 92168 | tf_op jit(solution)/shard_map/ppermute | solution.py:27
  134.6 6.0 %copy-start.15 = (pred[192]{0:T(512)(128)(4,1)S(1)}, pred[192]{0:T(512)(128)(4,1)}, u32[]{:S(2)}) copy-start(pred[192]{0:T(512)(128)(4,1)} %copy-done.14) | copy-start | bytes 580
  134.7 6.8 %copy-start.5 = (f32[32,2,128]{2,1,0:T(2,128)S(1)}, f32[32,2,128]{2,1,0:T(2,128)}, u32[]{:S(2)}) copy-start(f32[32,2,128]{2,1,0:T(2,128)} %fusion.23) | copy-start | bytes 98308
  141.5 98.2 %copy-start.9 = (s32[192,1]{0,1:T(1,128)S(1)}, s32[192,1]{0,1:T(1,128)}, u32[]{:S(2)}) copy-start(s32[192,1]{0,1:T(1,128)} %copy-done.8) | copy-start | bytes 2308
  141.5 114.1 %copy-start = (f32[32,128,128]{2,1,0:T(8,128)S(1)}, f32[32,128,128]{2,1,0:T(8,128)}, u32[]{:S(2)}) copy-start(f32[32,128,128]{2,1,0:T(8,128)} %fusion.17) | copy-start | bytes 6291460
  239.7 19.8 %copy-start.4 = (f32[6,32,3,128]{3,2,1,0:T(4,128)S(1)}, f32[6,32,3,128]{3,2,1,0:T(4,128)}, u32[]{:S(2)}) copy-start(f32[6,32,3,128]{3,2,1,0:T(4,128)} %get-tuple-element.233) | copy-start | bytes 884740
  252.8 19.5 %copy-start.16 = (f32[60]{0:T(128)S(1)}, f32[60]{0:T(128)}, u32[]{:S(2)}) copy-start(f32[60]{0:T(128)} %reshape.431) | copy-start | bytes 724
  252.8 19.6 %copy-start.19 = (s32[60]{0:T(128)S(1)}, s32[60]{0:T(128)}, u32[]{:S(2)}) copy-start(s32[60]{0:T(128)} %copy-done.18) | copy-start | bytes 724
  252.9 9.7 %collective-permute-start.19 = (f32[60,3,128]{2,1,0:T(4,128)S(1)}, f32[60,3,128]{2,1,0:T(4,128)S(1)}, u32[]{:S(2)}, u32[]{:S(2)}) collective-permute-start(f32[60,3,128]{2,1,0:T(4,128)S(1)} %slice.213), channel_id=1, source_target_pairs={{8,0},{16,8},{24,16},{9,1},{17,9},{25,17},{10,2},{18,10},{26,18},{... | collective-permute-start | bytes 276488 | tf_op jit(solution)/shard_map/ppermute | solution.py:27
  259.6 8.8 %collective-permute-start.18 = (f32[8,3,128]{2,1,0:T(4,128)S(1)}, f32[8,3,128]{2,1,0:T(4,128)S(1)}, u32[]{:S(2)}, u32[]{:S(2)}) collective-permute-start(f32[8,3,128]{2,1,0:T(4,128)S(1)} %slice.212), channel_id=1, source_target_pairs={{0,7},{1,0},{2,1},{3,2},{4,3},{5,4},{6,5},{7,6},{8,15},{9,8},{10,9... | collective-permute-start | bytes 36872 | tf_op jit(solution)/shard_map/ppermute | solution.py:21
  262.6 5.7 %collective-permute-start.20 = (f32[12,3,128]{2,1,0:T(4,128)S(1)}, f32[12,3,128]{2,1,0:T(4,128)S(1)}, u32[]{:S(2)}, u32[]{:S(2)}) collective-permute-start(f32[12,3,128]{2,1,0:T(4,128)S(1)} %get-tuple-element.308), channel_id=1, source_target_pairs={{0,2},{1,3},{2,4},{3,5},{4,6},{5,7},{6,0},{7,1},{8,10},{9,11},{10,... | collective-permute-start | bytes 55304 | tf_op jit(solution)/shard_map/ppermute | solution.py:21
  262.7 5.6 %collective-permute-start.21 = (f32[12,3,128]{2,1,0:T(4,128)S(1)}, f32[12,3,128]{2,1,0:T(4,128)S(1)}, u32[]{:S(2)}, u32[]{:S(2)}) collective-permute-start(f32[12,3,128]{2,1,0:T(4,128)S(1)} %get-tuple-element.307), channel_id=1, source_target_pairs={{0,1},{1,2},{2,3},{3,4},{4,5},{5,6},{6,7},{7,0},{8,9},{9,10},{10,1... | collective-permute-start | bytes 55304 | tf_op jit(solution)/shard_map/ppermute | solution.py:21
  268.3 1.7 collective-permute-start.22
  268.4 3.9 %collective-permute-start.23 = (f32[12,3,128]{2,1,0:T(4,128)S(1)}, f32[12,3,128]{2,1,0:T(4,128)S(1)}, u32[]{:S(2)}, u32[]{:S(2)}) collective-permute-start(f32[12,3,128]{2,1,0:T(4,128)S(1)} %get-tuple-element.304), channel_id=1, source_target_pairs={{0,6},{1,7},{2,0},{3,1},{4,2},{5,3},{6,4},{7,5},{8,14},{9,15},{10,... | collective-permute-start | bytes 55304 | tf_op jit(solution)/shard_map/ppermute | solution.py:21
where the time goes:
time: 281 us; the launch traced here: 276 us
  other arithmetic  154 us (55%)
  local copies, waits for them, and re-layouts  65.9 us (23%)
  starting transfers between devices  31.5 us (11%)
  waiting for transfers between devices  21.7 us (8%)
    reduce_sum x12, other arithmetic, geometry(): jnp.sum(between * between, axis=1)  37 us
    reduce_sum x7, other arithmetic, force_terms(): return (jnp.sum(pushed, axis=3), -jnp.sum(pushed, axis=2))  28.4 us
    ppermute x20, starting transfers between devices, shifted(): lax.ppermute(value, axis, [(i, (i + by) % length) for i in range(length)])  18.8 us
    div x7, other arithmetic, force_terms(): scalar = scalar * weight / distance  17.4 us
    ppermute x20, waiting for transfers between devices, shifted(): lax.ppermute(value, axis, [(i, (i + by) % length) for i in range(length)])  16.9 us
    reduce_sum x7, other arithmetic, density_terms(): return (jnp.sum(weight, axis=2), jnp.sum(weight, axis=1))  13.1 us
    scatter-add x1, other arithmetic, on_device(): jnp.zeros((union.shape[0], 3, tile_width), jnp.float32).at[flat]  13.1 us
    ppermute x4, starting transfers between devices, shifted_2(): lax.ppermute(value, axis, [(source, source + steps) for source in range(l...  12.8 us
  transfers between devices with their start and end apart: 24, of which 8 were waited for; matrix products, arithmetic and copies ran while one was open for 14% of the time, Pallas kernels for 0%

commit v1 on v0

v1 whole, which is shorter than its diff:
```python
import functools
import math

import jax
import jax.numpy as jnp
from jax import lax
from jax.experimental import pallas as pl
from jax.experimental.pallas import tpu as pltpu
from jax.sharding import PartitionSpec as P

cutoff_density = 0.75
density_norm = 15.0 / (2.0 * math.pi * cutoff_density**3)
repulse = 25.0
friction = 4.5
time_step = 0.01
distance_floor = 0.01
far_away = 10000.0
density_scale = density_norm / (cutoff_density * cutoff_density)
crowd_scale = repulse / cutoff_density
STEP = 16
VMEM = pl.BlockSpec(memory_space=pltpu.VMEM)
SMEM = pl.BlockSpec(memory_space=pltpu.SMEM)
f32 = jnp.float32


def sds(*shape):
    return jax.ShapeDtypeStruct(shape, f32)


def params():
    return pltpu.CompilerParams(vmem_limit_bytes=32 * 1024 * 1024)


def pack_kernel(pos, vel, typ, counts, send, out, top, face):
    tiles = out.shape[0]
    width = out.shape[2]
    lane = lax.broadcasted_iota(jnp.int32, (1, width), 1)
    upper = top.shape[0]
    offsets, cap = send.shape[1], send.shape[2]
    for g in range(tiles):
        cols = pl.ds(g * width, width)
        live = lane < counts[g]
        for c in range(3):
            out[g, pl.ds(c, 1), :] = jnp.where(live, pos[pl.ds(c, 1), cols], far_away)
            out[g, pl.ds(3 + c, 1), :] = vel[pl.ds(c, 1), cols]
        out[g, pl.ds(6, 1), :] = typ[pl.ds(g, 1), :].astype(f32)
        meta = jnp.full((1, width), counts[g], jnp.int32)
        o = g - (tiles - upper)
        if 0 <= o < offsets:
            for c in range(cap):
                meta = jnp.where(lane == c, send[0, o, c], meta)
        out[g, pl.ds(7, 1), :] = meta.astype(f32)
    top[...] = out[pl.ds(tiles - upper, upper)]
    face[...] = out[pl.ds(0, face.shape[0])]


def spread_rows(tile, rows, channels):
    width = tile.shape[1]
    turned = tile.T
    for c in range(channels):
        rows[c] = jnp.broadcast_to(turned[:, c : c + 1], (width, width))


def sized(count, width, body):
    steps = (count + (STEP - 1)) // STEP

    def case(k):
        @pl.when(steps == k)
        def _():
            body(k * STEP)

    for k in range(1, width // STEP + 1):
        case(k)


def density_block(rows, other, r):
    at = pl.ds(r, 8)
    dx = rows[0, at, :] - other[0]
    dy = rows[1, at, :] - other[1]
    dz = rows[2, at, :] - other[2]
    d2 = jnp.maximum(dx * dx + dy * dy + dz * dz, distance_floor)
    w = jnp.maximum(cutoff_density - d2 * lax.rsqrt(d2), 0.0)
    return w * w


def column(ref, h, c):
    return jnp.broadcast_to(ref[h, pl.ds(c, 1), :], (8, ref.shape[2]))


def density_pair(rows, union, h, count, acc_cols, acc_rows):
    width = union.shape[2]

    def body(n):
        other = [column(union, h, c) for c in range(3)]
        total = None
        for r in range(0, n, 8):
            w = density_block(rows, other, r)
            total = w if total is None else total + w
            if acc_rows is not None:
                acc_rows[0, pl.ds(r, 8), :] += w
        acc_cols[h] += total

    sized(count, width, body)


def force_pair(rows, union, h, count, table, acc_cols, acc_rows):
    width = union.shape[2]
    a00, a01, a11 = table

    def body(n):
        other = [column(union, h, c) for c in range(8)]
        first = a00 + other[6] * (a01 - a00)
        slope = (a01 + other[6] * (a11 - a01)) - first
        total = [None] * 3
        for r in range(0, n, 8):
            mine = [rows[c, pl.ds(r, 8), :] for c in range(8)]
            d = [mine[c] - other[c] for c in range(3)]
            d2 = jnp.maximum(d[0] * d[0] + d[1] * d[1] + d[2] * d[2], distance_floor)
            inverse = lax.rsqrt(d2)
            dist = d2 * inverse
            wc = jnp.maximum(1.0 - dist, 0.0)
            wd = jnp.maximum(cutoff_density - dist, 0.0)
            dv = [mine[3 + c] - other[3 + c] for c in range(3)]
            approach = (d[0] * dv[0] + d[1] * dv[1] + d[2] * dv[2]) * inverse
            scalar = (first + mine[6] * slope) - approach * wc
            scalar = scalar * wc + (mine[7] + other[7]) * wd
            scalar = scalar * inverse
            for c in range(3):
                push = d[c] * scalar
                total[c] = push if total[c] is None else total[c] + push
                if acc_rows is not None:
                    acc_rows[c, pl.ds(r, 8), :] += push
        for c in range(3):
            acc_cols[c, h] -= total[c]

    sized(count, width, body)


def row_sums(acc):
    first = (lax.broadcasted_iota(jnp.int32, (8, acc.shape[1]), 0) == 0).astype(f32)
    return lax.dot_general(
        first,
        acc,
        (((1,), (1,)), ((), ())),
        precision=lax.Precision.HIGHEST,
        preferred_element_type=f32,
    )


def fold(ref, tiles, out, scale=None):
    def one(t, carry):
        value = jnp.sum(ref[t], axis=0, keepdims=True)
        out[pl.ds(t, 1), :] = value
        return carry

    lax.fori_loop(0, tiles, one, 0)


def local_density_kernel(counts, nbr, union, acc, rows, acc_rows):
    tiles, width = union.shape[0], union.shape[2]
    acc[...] = jnp.zeros_like(acc)

    def tile(g, carry):
        count = counts[g]

        @pl.when(count > 0)
        def _():
            spread_rows(union[g], rows, 3)
            density_pair(rows, union, g, count, acc, None)
            acc_rows[0] = jnp.zeros((width, width), f32)

            def partner(k, carry):
                h = nbr[g, k]

                @pl.when((h >= 0) & (counts[jnp.maximum(h, 0)] > 0))
                def _():
                    density_pair(rows, union, h, count, acc, acc_rows)

                return carry

            lax.fori_loop(0, nbr.shape[1], partner, 0)
            acc[g] += row_sums(acc_rows[0])

        return carry

    lax.fori_loop(0, tiles, tile, 0)


def gather_ghosts(ghosts, face, near, flip, below, above):
    at = 0
    for ref in (face, near, flip, below, above):
        ghosts[pl.ds(at, ref.shape[0])] = ref[...]
        at += ref.shape[0]


def ghost_meta(ghosts, faces, upper, meta, meta_smem, sem):
    total = ghosts.shape[0]
    for t in range(total):
        meta[pl.ds(t, 1), :] = ghosts[t, pl.ds(7, 1), :].astype(jnp.int32)
    copy = pltpu.make_async_copy(meta, meta_smem, sem)
    copy.start()
    copy.wait()


def ghost_partner(k, g, face_nbr, cross_pair, where, meta, faces, upper, cap, reach):
    columns = face_nbr.shape[1]
    is_face = k < columns
    f = face_nbr[g, jnp.minimum(k, columns - 1)]
    s = cross_pair[g, jnp.maximum(k - columns, 0)]
    layer, core = where[0], where[1]
    slot = jnp.maximum(s, 0)
    o = slot // cap
    c = slot - o * cap
    place = core - o + 2 * reach
    hop = place // 2 - 1
    flipped = jnp.where(lax.rem(place, 2) == core, 0, 1)
    hops = jnp.where(hop == 0, 0, jnp.where(hop < 0, 1, 2))
    base = faces + (hops * 2 + flipped) * upper
    u = meta[base + o, c]
    ok = (s >= 0) & (layer > 0) & (u >= 0)
    h = jnp.where(is_face, jnp.maximum(f, 0), base + jnp.maximum(u, 0))
    ok = jnp.where(is_face, f >= 0, ok)
    return h, ok & (meta[h, meta.shape[1] - 1] > 0)


def ghost_density_kernel(
    faces,
    upper,
    cap,
    reach,
    where,
    counts,
    face_nbr,
    cross_pair,
    union,
    local_acc,
    face,
    near,
    flip,
    below,
    above,
    own_out,
    top_out,
    face_out,
    pair_out,
    below_out,
    above_out,
    ghosts,
    acc,
    acc_own,
    rows,
    acc_rows,
    reduced,
    meta,
    meta_smem,
    sem,
):
    tiles, width = union.shape[0], union.shape[2]
    gather_ghosts(ghosts, face, near, flip, below, above)
    ghost_meta(ghosts, faces, upper, meta, meta_smem, sem)
    acc[...] = jnp.zeros_like(acc)
    columns = face_nbr.shape[1] + cross_pair.shape[1]

    def tile(g, carry):
        count = counts[g]
        acc_own[g] = local_acc[g]

        @pl.when(count > 0)
        def _():
            spread_rows(union[g], rows, 3)
            acc_rows[0] = jnp.zeros((width, width), f32)

            def partner(k, carry):
                h, ok = ghost_partner(
                    k, g, face_nbr, cross_pair, where, meta_smem, faces, upper, cap, reach
                )

                @pl.when(ok)
                def _():
                    density_pair(rows, ghosts, h, count, acc, acc_rows)

                return carry

            lax.fori_loop(0, columns, partner, 0)
            acc_own[g] += row_sums(acc_rows[0])

        return carry

    lax.fori_loop(0, tiles, tile, 0)
    self_term = (cutoff_density - math.sqrt(distance_floor)) ** 2
    for t in range(tiles):
        lane = lax.broadcasted_iota(jnp.int32, (1, width), 1)
        value = jnp.sum(acc_own[t], axis=0, keepdims=True)
        own_out[pl.ds(t, 1), :] = value - jnp.where(lane < counts[t], self_term, 0.0)
    top_out[...] = own_out[pl.ds(tiles - upper, upper)]
    for t in range(acc.shape[0]):
        reduced[pl.ds(t, 1), :] = jnp.sum(acc[t], axis=0, keepdims=True)
    face_out[...] = reduced[pl.ds(0, faces)]
    pair_out[...] = reduced[pl.ds(faces, 2 * upper)]
    below_out[...] = reduced[pl.ds(faces + 2 * upper, 2 * upper)]
    above_out[...] = reduced[pl.ds(faces + 4 * upper, 2 * upper)]


def force_tile(union, density, t):
    tile = union[t]
    channel = lax.broadcasted_iota(jnp.int32, tile.shape, 0)
    tile = jnp.where((channel >= 3) & (channel < 6), tile * friction, tile)
    return jnp.where(channel == 7, density * (crowd_scale * density_scale), tile)


def amplitudes(a_table):
    return (a_table[0, 0], 0.5 * (a_table[0, 1] + a_table[1, 0]), a_table[1, 1])


def local_force_kernel(counts, nbr, a_table, union, density, acc, beads, rows, acc_rows):
    tiles, width = union.shape[0], union.shape[2]
    table = amplitudes(a_table)
    acc[...] = jnp.zeros_like(acc)
    for t in range(tiles):
        beads[t] = force_tile(union, density[pl.ds(t, 1), :], t)

    def tile(g, carry):
        count = counts[g]

        @pl.when(count > 0)
        def _():
            spread_rows(beads[g], rows, 8)
            force_pair(rows, beads, g, count, table, acc, None)
            acc_rows[...] = jnp.zeros_like(acc_rows)

            def partner(k, carry):
                h = nbr[g, k]

                @pl.when((h >= 0) & (counts[jnp.maximum(h, 0)] > 0))
                def _():
                    force_pair(rows, beads, h, count, table, acc, acc_rows)

                return carry

            lax.fori_loop(0, nbr.shape[1], partner, 0)
            for c in range(3):
                acc[c, g] += row_sums(acc_rows[c])

        return carry

    lax.fori_loop(0, tiles, tile, 0)


def ghost_force_kernel(
    faces,
    upper,
    cap,
    reach,
    where,
    counts,
    face_nbr,
    cross_pair,
    a_table,
    union,
    density,
    face,
    near,
    flip,
    below,
    above,
    face_rho,
    pair_rho,
    below_rho,
    above_rho,
    own_out,
    face_out,
    pair_out,
    below_out,
    above_out,
    ghosts,
    beads,
    acc,
    rho,
    rows,
    acc_rows,
    reduced,
    meta,
    meta_smem,
    sem,
):
    tiles, width = union.shape[0], union.shape[2]
    gather_ghosts(ghosts, face, near, flip, below, above)
    ghost_meta(ghosts, faces, upper, meta, meta_smem, sem)
    acc[...] = jnp.zeros_like(acc)
    own_out[...] = jnp.zeros_like(own_out)
    table = amplitudes(a_table)
    columns = face_nbr.shape[1] + cross_pair.shape[1]
    at = 0
    for ref in (face_rho, pair_rho, below_rho, above_rho):
        rho[pl.ds(at, ref.shape[0]), :] = ref[...]
        at += ref.shape[0]
    for t in range(ghosts.shape[0]):
        ghosts[t] = force_tile(ghosts, rho[pl.ds(t, 1), :], t)
    for t in range(tiles):
        beads[t] = force_tile(union, density[pl.ds(t, 1), :], t)

    def tile(g, carry):
        count = counts[g]

        @pl.when(count > 0)
        def _():
            spread_rows(beads[g], rows, 8)
            acc_rows[...] = jnp.zeros_like(acc_rows)

            def partner(k, carry):
                h, ok = ghost_partner(
                    k, g, face_nbr, cross_pair, where, meta_smem, faces, upper, cap, reach
                )

                @pl.when(ok)
                def _():
                    force_pair(rows, ghosts, h, count, table, acc, acc_rows)

                return carry

            lax.fori_loop(0, columns, partner, 0)
            for c in range(3):
                own_out[c, g] = row_sums(acc_rows[c])

        return carry

    lax.fori_loop(0, tiles, tile, 0)
    for c in range(3):
        for t in range(acc.shape[1]):
            reduced[pl.ds(t, 1), :] = jnp.sum(acc[c, t], axis=0, keepdims=True)
        face_out[c] = reduced[pl.ds(0, faces)]
        pair_out[c] = reduced[pl.ds(faces, 2 * upper)]
        below_out[c] = reduced[pl.ds(faces + 2 * upper, 2 * upper)]
        above_out[c] = reduced[pl.ds(faces + 4 * upper, 2 * upper)]


def finish_kernel(counts, pos, vel, local_acc, ghost_acc, face_back, top_back, pos_out, vel_out):
    tiles, width = local_acc.shape[1], local_acc.shape[3]
    faces, upper = face_back.shape[1], top_back.shape[1]
    lane = lax.broadcasted_iota(jnp.int32, (1, width), 1)
    for g in range(tiles):
        cols = pl.ds(g * width, width)
        live = lane < counts[g]
        for c in range(3):
            force = jnp.sum(local_acc[c, g] + ghost_acc[c, g], axis=0, keepdims=True)
            if g < faces:
                force = force + face_back[c, pl.ds(g, 1), :]
            if g >= tiles - upper:
                force = force + top_back[c, pl.ds(g - (tiles - upper), 1), :]
            speed = jnp.where(live, vel[pl.ds(c, 1), cols] + time_step * force, 0.0)
            vel_out[pl.ds(c, 1), cols] = speed
            place = jnp.where(live, pos[pl.ds(c, 1), cols] + time_step * speed, 0.0)
            pos_out[pl.ds(c, 1), cols] = place


def on_device(
    layers,
    places,
    positions,
    velocities,
    types,
    counts,
    a_table,
    local_nbr,
    face_nbr,
    cross_send,
    cross_pair,
):
    tiles = counts.shape[0]
    width = positions.shape[1] // tiles
    faces, upper = tiles // 4, tiles // 2
    offsets, cap = cross_send.shape[1], cross_send.shape[2]
    reach = offsets // 2
    total = faces + 6 * upper
    both = ("layer", "lat")

    def lateral(value, by):
        return lax.ppermute(value, "lat", [(m, (m + by) % places) for m in range(places)])

    def swap(value):
        return lax.ppermute(value, "lat", [(m, m ^ 1) for m in range(places)])

    def climb(value, by, flip=0):
        return lax.ppermute(
            value,
            both,
            [
                (l * places + m, ((l + by) % layers) * places + (m ^ flip))
                for l in range(layers)
                for m in range(places)
            ],
        )

    kinds = types.reshape(tiles, width)
    payload, top, face = pl.pallas_call(
        pack_kernel,
        out_shape=(sds(tiles, 8, width), sds(upper, 8, width), sds(faces, 8, width)),
        in_specs=[VMEM, VMEM, VMEM, SMEM, SMEM],
        out_specs=[VMEM] * 3,
        compiler_params=params(),
    )(positions, velocities, kinds, counts, cross_send)
    near = climb(top, 1)
    flip = climb(top, 1, 1)
    face_ghosts = lateral(face, 1)
    chip_ghosts = jnp.concatenate([near, flip], axis=0)
    below = lateral(chip_ghosts, 2)
    above = lateral(chip_ghosts, -2)
    where = jnp.stack([lax.axis_index("layer"), lax.axis_index("lat") % 2]).astype(jnp.int32)

    local_acc = pl.pallas_call(
        local_density_kernel,
        out_shape=sds(tiles, 8, width),
        in_specs=[SMEM, SMEM, VMEM],
        out_specs=VMEM,
        scratch_shapes=[pltpu.VMEM((3, width, width), f32), pltpu.VMEM((1, width, width), f32)],
        cost_estimate=pl.CostEstimate(flops=200 * 10**6, bytes_accessed=10**6, transcendentals=0),
        compiler_params=params(),
    )(counts, local_nbr, payload)

    sizes = (faces, upper, cap, reach)
    meta_scratch = [
        pltpu.VMEM((total, width), jnp.int32),
        pltpu.SMEM((total, width), jnp.int32),
        pltpu.SemaphoreType.DMA,
    ]
    own, own_top, face_part, pair_part, below_part, above_part = pl.pallas_call(
        functools.partial(ghost_density_kernel, *sizes),
        out_shape=(
            sds(tiles, width),
            sds(upper, width),
            sds(faces, width),
            sds(2 * upper, width),
            sds(2 * upper, width),
            sds(2 * upper, width),
        ),
        in_specs=[SMEM] * 4 + [VMEM] * 7,
        out_specs=[VMEM] * 6,
        scratch_shapes=[
            pltpu.VMEM((total, 8, width), f32),
            pltpu.VMEM((total, 8, width), f32),
            pltpu.VMEM((tiles, 8, width), f32),
            pltpu.VMEM((3, width, width), f32),
            pltpu.VMEM((1, width, width), f32),
            pltpu.VMEM((total, width), f32),
        ]
        + meta_scratch,
        compiler_params=params(),
    )(
        where,
        counts,
        face_nbr,
        cross_pair,
        payload,
        local_acc,
        face_ghosts,
        near,
        flip,
        below,
        above,
    )

    owner_part = climb(own_top, 1)
    from_above = lateral(below_part, -2)
    from_below = lateral(above_part, 2)
    face_back = lateral(face_part, -1)
    met = pair_part + from_above + from_below
    met = jnp.concatenate([met[:upper] + owner_part, met[upper:]], axis=0)
    other = swap(met)
    pair_rho = met + jnp.concatenate([other[upper:], other[:upper]], axis=0)
    top_rho = climb(pair_rho[:upper], -1)
    below_rho = lateral(pair_rho, 2)
    above_rho = lateral(pair_rho, -2)
    bottom_rho = own[:faces] + face_back
    face_rho = lateral(bottom_rho, 1)
    density = jnp.concatenate([bottom_rho, own[faces : tiles - upper], top_rho], axis=0)

    ghost_acc, face_force, pair_force, below_force, above_force = pl.pallas_call(
        functools.partial(ghost_force_kernel, *sizes),
        out_shape=(
            sds(3, tiles, 8, width),
            sds(3, faces, width),
            sds(3, 2 * upper, width),
            sds(3, 2 * upper, width),
            sds(3, 2 * upper, width),
        ),
        in_specs=[SMEM] * 5 + [VMEM] * 11,
        out_specs=[VMEM] * 5,
        scratch_shapes=[
            pltpu.VMEM((total, 8, width), f32),
            pltpu.VMEM((tiles, 8, width), f32),
            pltpu.VMEM((3, total, 8, width), f32),
            pltpu.VMEM((total, width), f32),
            pltpu.VMEM((8, width, width), f32),
            pltpu.VMEM((3, width, width), f32),
            pltpu.VMEM((total, width), f32),
        ]
        + meta_scratch,
        compiler_params=params(),
    )(
        where,
        counts,
        face_nbr,
        cross_pair,
        a_table,
        payload,
        density,
        face_ghosts,
        near,
        flip,
        below,
        above,
        face_rho,
        pair_rho,
        below_rho,
        above_rho,
    )

    force_face = lateral(face_force, -1)
    force_met = pair_force + lateral(below_force, -2) + lateral(above_force, 2)
    force_other = swap(force_met[:, upper:])
    force_top = climb(force_met[:, :upper] + force_other, -1)

    local_force = pl.pallas_call(
        local_force_kernel,
        out_shape=sds(3, tiles, 8, width),
        in_specs=[SMEM, SMEM, SMEM, VMEM, VMEM],
        out_specs=VMEM,
        scratch_shapes=[
            pltpu.VMEM((tiles, 8, width), f32),
            pltpu.VMEM((8, width, width), f32),
            pltpu.VMEM((3, width, width), f32),
        ],
        cost_estimate=pl.CostEstimate(flops=400 * 10**6, bytes_accessed=10**6, transcendentals=0),
        compiler_params=params(),
    )(counts, local_nbr, a_table, payload, density)

    return pl.pallas_call(
        finish_kernel,
        out_shape=(sds(*positions.shape), sds(*velocities.shape)),
        in_specs=[SMEM] + [VMEM] * 6,
        out_specs=[VMEM] * 2,
        compiler_params=params(),
    )(counts, positions, velocities, local_force, ghost_acc, force_face, force_top)


def solution(mesh):
    placed = (
        P(None, ("layer", "lat")),
        P(None, ("layer", "lat")),
        P(("layer", "lat")),
        P(("layer", "lat")),
        P(),
        P(("layer", "lat"), None),
        P(("layer", "lat"), None),
        P(("layer", "lat"), None, None),
        P(("layer", "lat"), None),
    )
    return jax.shard_map(
        functools.partial(on_device, mesh.shape["layer"], mesh.shape["lat"]),
        mesh=mesh,
        in_specs=placed,
        out_specs=(P(None, ("layer", "lat")), P(None, ("layer", "lat"))),
        check_vma=False,
    )
```

time: 281 us -> 177 us (0.63); the launches traced: 276 us -> 177 us
  other arithmetic: 154 us -> 0.12 us
  Pallas kernels: 0 us -> 128 us
  local copies, waits for them, and re-layouts: 65.9 us -> 5.81 us
  starting transfers between devices: 31.5 us -> 19.5 us
    pallas_call x0 -> x6, Pallas kernels: none -> 128 us  [the longest x1 42.5 us: on_device(): pl.pallas_call(functools.partial(ghost_force_kernel, *sizes), out_shape=(...]
    reduce_sum x36 -> x0, other arithmetic: 97.4 us -> none  [the longest x12 37 us: geometry(): jnp.sum(between * between, axis=1)]
    scatter-add x6 -> x0, other arithmetic: 20 us -> none  [the longest x1 13.1 us: on_device(): jnp.zeros((union.shape[0], 3, tile_width), jnp.float32).at[flat]]
    div x7 -> x0, other arithmetic: 17.4 us -> none  [force_terms(): scalar = scalar * weight / distance]
    sub x30 -> x0, local copies, waits for them, and re-layouts: 15.7 us -> none  [the longest x18 10.4 us: geometry(): between = place_left[:, :, :, None] - place_right[:, :, None, :]]
    mul x30 -> x0, local copies, waits for them, and re-layouts: 13.4 us -> none  [the longest x12 4.58 us: force_terms(): species_left[:, :, :, None] * strength_right[:, :, None, :]]
    ppermute x24 -> x19, starting transfers between devices: 31.5 us -> 19.5 us  [the longest x12 17.7 us: lateral(): lax.ppermute(value, 'lat', [(m, (m + by) % places) for m in range(places)])]
    concatenate x6 -> x1, local copies, waits for them, and re-layouts: 8.29 us -> 0.01 us  [on_device(): chip_ghosts = jnp.concatenate([near, flip], axis=0)]
  transfers between devices with their start and end apart: 24 -> 19, of which waited for: 8 -> 11; matrix products, arithmetic and copies ran while one was open for 14% -> 0% of each run, Pallas kernels for 0% -> 30%
where the time goes in v1:
time: 177 us
  Pallas kernels  128 us (72%)
  waiting for transfers between devices  23.4 us (13%)
  starting transfers between devices  19.5 us (11%)
  local copies, waits for them, and re-layouts  5.81 us (3%)
    pallas_call x1, Pallas kernels, on_device(): pl.pallas_call(functools.partial(ghost_force_kernel, *sizes), out_shape=(...  42.5 us
    pallas_call x1, Pallas kernels, on_device(): pl.pallas_call(local_force_kernel, out_shape=sds(3, tiles, 8, width), in_...  32.9 us
    pallas_call x1, Pallas kernels, on_device(): pl.pallas_call(functools.partial(ghost_density_kernel, *sizes), out_shape...  29.7 us
    pallas_call x1, Pallas kernels, on_device(): pl.pallas_call(local_density_kernel, out_shape=sds(tiles, 8, width), in_s...  20.5 us
    ppermute x12, starting transfers between devices, lateral(): lax.ppermute(value, 'lat', [(m, (m + by) % places) for m in range(places)])  17.7 us
    ppermute x12, waiting for transfers between devices, lateral(): lax.ppermute(value, 'lat', [(m, (m + by) % places) for m in range(places)])  17.4 us
    unnamed x25, local copies, waits for them, and re-layouts  5.8 us
    ppermute x5, waiting for transfers between devices, climb(): lax.ppermute(value, both, [(l * places + m, (l + by) % layers * places +...  4.92 us
  transfers between devices with their start and end apart: 19, of which 11 were waited for; matrix products, arithmetic and copies ran while one was open for 0% of the time, Pallas kernels for 30%

profile of v1, /device:TPU:4, one launch (start us, length us, event | category | flops | bytes accessed | tf_op | source)
XLA Modules:
  0.0 177.3 jit_solution(1974471187422211318)
XLA Ops:
  0.6 0.7 copy.11.send
  1.3 0.7 copy-done.5
  2.0 0.8 copy-done
  2.8 0.8 copy-done.2
  3.7 0.7 copy-done.4
  4.4 0.7 shard_map.104
  5.1 1.5 collective-permute-start.1
  6.6 0.0 collective-permute-start.2
  6.6 0.2 collective-permute-start
  6.8 3.5 %collective-permute-done.1.near = f32[16,8,128]{2,1,0:T(8,128)S(1)} collective-permute-done((f32[16,8,128]{2,1,0:T(8,128)S(1)}, f32[16,8,128]{2,1,0:T(8,128)S(1)}, u32[]{:S(2)}, u32[]{:S(2)}) %collective-permute-start.1) | collective-permute-done | bytes 65568 | tf_op jit(solution)/shard_map/ppermute | solution.py:484
  10.3 1.4 collective-permute-done.2.flip
  11.7 3.6 %collective-permute-start.4 = (f32[32,8,128]{2,1,0:T(8,128)S(1)}, f32[32,8,128]{2,1,0:T(8,128)S(1)}, u32[]{:S(2)}, u32[]{:S(2)}) collective-permute-start(f32[32,8,128]{2,1,0:T(8,128)S(1)} %constant_dynamic-update-slice_fusion), channel_id=1, source_target_pairs={{0,6},{1,7},{2,0},{3,1},{4,2},{5,3},{6,4},{7,5},{8,14},{9,15},{10,... | collective-permute-start | bytes 393224 | tf_op jit(solution)/shard_map/ppermute | solution.py:478
  15.3 0.0 collective-permute-start.3
  15.3 0.1 pad_add_fusion.where
  15.4 0.6 copy-done.7
  16.0 0.1 copy.15.nbr
  16.1 0.6 copy-done.8
  16.7 0.1 copy.13.face_nbr
  16.8 0.6 copy-done.9
  17.3 0.1 copy.14.cross_pair
  17.4 20.5 %shard_map.105.local_acc = f32[32,8,128]{2,1,0:T(8,128)S(1)} custom-call(s32[32]{0:T(128)S(1)} %copy-done.5, s32[32,2]{1,0:T(8,128)S(1)} %copy.15.nbr, f32[32,8,128]{2,1,0:T(8,128)S(1)} %get-tuple-element.16.union), custom_call_target="tpu_custom_call" | custom-call | flops 200000000 | bytes 1000000 | tf_op jit(solution)/shard_map/pallas_call | solution.py:510
  37.9 0.0 collective-permute-done.face
  37.9 0.0 collective-permute-done.4.above
  38.0 0.0 collective-permute-done.3.below
  38.0 29.7 %shard_map.106 = (f32[32,128]{1,0:T(8,128)S(1)}, f32[16,128]{1,0:T(8,128)S(1)}, f32[8,128]{1,0:T(8,128)S(1)}, f32[32,128]{1,0:T(8,128)S(1)}, f32[32,128]{1,0:T(8,128)S(1)}, /*index=5*/f32[32,128]{1,0:T(8,128)S(1)}) custom-call(s32[2]{0:T(128)S(1)} %pad_add_fusion.where, s32[32]{0:T(128)S(1)} %copy-done.5, s32[32,2]{1,0:T(8,128)S(1)} %copy.13.face_nbr, ...), custom_call_target="tpu_custom_call" | custom-call | tf_op jit(solution)/shard_map/pallas_call | solution.py:526
  67.7 5.0 %collective-permute-start.6 = (f32[32,128]{1,0:T(8,128)S(1)}, f32[32,128]{1,0:T(8,128)S(1)}, u32[]{:S(2)}, u32[]{:S(2)}) collective-permute-start(f32[32,128]{1,0:T(8,128)S(1)} %get-tuple-element.22), channel_id=1, source_target_pairs={{0,6},{1,7},{2,0},{3,1},{4,2},{5,3},{6,4},{7,5},{8,14},{9,15},{10,... | collective-permute-start | bytes 49160 | tf_op jit(solution)/shard_map/ppermute | solution.py:478
  72.7 1.4 collective-permute-done.6
  74.1 4.1 %collective-permute-done.7 = f32[32,128]{1,0:T(8,128)S(1)} collective-permute-done((f32[32,128]{1,0:T(8,128)S(1)}, f32[32,128]{1,0:T(8,128)S(1)}, u32[]{:S(2)}, u32[]{:S(2)}) %collective-permute-start.7) | collective-permute-done | bytes 16416 | tf_op jit(solution)/shard_map/ppermute | solution.py:478
  78.2 0.1 collective-permute-start.9
  78.3 2.8 %collective-permute-start.5 = (f32[8,128]{1,0:T(8,128)S(1)}, f32[8,128]{1,0:T(8,128)S(1)}, u32[]{:S(2)}, u32[]{:S(2)}) collective-permute-start(f32[8,128]{1,0:T(8,128)S(1)} %get-tuple-element.20), channel_id=1, source_target_pairs={{0,7},{1,0},{2,1},{3,2},{4,3},{5,4},{6,5},{7,6},{8,15},{9,8},{10,9... | collective-permute-start | bytes 12296 | tf_op jit(solution)/shard_map/ppermute | solution.py:478
  81.2 0.1 collective-permute-start.10
  81.3 1.2 collective-permute-done.5
  82.5 3.9 %collective-permute-start.13 = (f32[32,128]{1,0:T(8,128)S(1)}, f32[32,128]{1,0:T(8,128)S(1)}, u32[]{:S(2)}, u32[]{:S(2)}) collective-permute-start(f32[32,128]{1,0:T(8,128)S(1)} %maximum_add_fusion.pair_rho), channel_id=1, source_target_pairs={{0,6},{1,7},{2,0},{3,1},{4,2},{5,3},{6,4},{7,5},{8,14},{9,15},{10,... | collective-permute-start | bytes 49160 | tf_op jit(solution)/shard_map/ppermute | solution.py:478
  86.4 0.9 collective-permute-done.11.face_rho
  87.3 0.5 collective-permute-done.13.above_rho
  87.8 4.1 %collective-permute-done.12.below_rho = f32[32,128]{1,0:T(8,128)S(1)} collective-permute-done((f32[32,128]{1,0:T(8,128)S(1)}, f32[32,128]{1,0:T(8,128)S(1)}, u32[]{:S(2)}, u32[]{:S(2)}) %collective-permute-start.12) | collective-permute-done | bytes 16416 | tf_op jit(solution)/shard_map/ppermute | solution.py:478
  91.9 42.5 %shard_map.108 = (f32[3,32,8,128]{3,2,1,0:T(8,128)S(1)}, f32[3,8,128]{2,1,0:T(8,128)S(1)}, f32[3,32,128]{2,1,0:T(8,128)S(1)}, f32[3,32,128]{2,1,0:T(8,128)S(1)}, f32[3,32,128]{2,1,0:T(8,128)S(1)}) custom-call(s32[2]{0:T(128)S(1)} %pad_add_fusion.where, s32[32]{0:T(128)S(1)} %copy-done.5, s32[32,2]{1,0:T(8,128)S(1)} %copy.13.face_nbr, ...), custom_call_target="tpu_custom_call" | custom-call | tf_op jit(solution)/shard_map/pallas_call | solution.py:577
  134.5 1.2 collective-permute-start.15
  135.7 0.8 collective-permute-start.16
  136.6 2.6 %collective-permute-done.15 = f32[3,32,128]{2,1,0:T(8,128)S(1)} collective-permute-done((f32[3,32,128]{2,1,0:T(8,128)S(1)}, f32[3,32,128]{2,1,0:T(8,128)S(1)}, u32[]{:S(2)}, u32[]{:S(2)}) %collective-permute-start.15) | collective-permute-done | bytes 49184 | tf_op jit(solution)/shard_map/ppermute | solution.py:478
  139.1 2.5 %collective-permute-done.16 = f32[3,32,128]{2,1,0:T(8,128)S(1)} collective-permute-done((f32[3,32,128]{2,1,0:T(8,128)S(1)}, f32[3,32,128]{2,1,0:T(8,128)S(1)}, u32[]{:S(2)}, u32[]{:S(2)}) %collective-permute-start.16) | collective-permute-done | bytes 49184 | tf_op jit(solution)/shard_map/ppermute | solution.py:478
  141.6 0.1 collective-permute-start.17
  141.7 0.1 collective-permute-start.14
  141.8 1.1 collective-permute-done.17
  142.9 0.1 collective-permute-start.18
  143.0 32.9 %shard_map.107.local_acc = f32[3,32,8,128]{3,2,1,0:T(8,128)S(1)} custom-call(s32[32]{0:T(128)S(1)} %copy-done.5, s32[32,2]{1,0:T(8,128)S(1)} %copy.15.nbr, f32[2,2]{1,0:T(2,128)S(1)} %copy-done.6, f32[32,8,128]{2,1,0:T(8,128)S(1)} %get-tuple-element.16.union, f32[32,128]{1,0:T(8,128)S(1)} %pad_maximum_fusion.1.density), custom_call_target="tpu_custom_call" | custom-call | flops 400000000 | bytes 1000000 | tf_op jit(solution)/shard_map/pallas_call | solution.py:623
  175.9 0.0 collective-permute-done.18.top_back
  175.9 1.4 shard_map.109
  (34 shorter events, 0.1 us)
Async XLA Ops:
  1.3 0.7 copy-start.5
  2.0 0.8 copy-start
  2.8 0.8 copy-start.2
  3.7 0.7 copy-start.4
  5.1 5.2 %collective-permute-start.1 = (f32[16,8,128]{2,1,0:T(8,128)S(1)}, f32[16,8,128]{2,1,0:T(8,128)S(1)}, u32[]{:S(2)}, u32[]{:S(2)}) collective-permute-start(f32[16,8,128]{2,1,0:T(8,128)S(1)} %get-tuple-element.18), channel_id=1, source_target_pairs={{0,8},{1,9},{2,10},{3,11},{4,12},{5,13},{6,14},{7,15},{8,16},{9,17... | collective-permute-start | bytes 196616 | tf_op jit(solution)/shard_map/ppermute | solution.py:484
  6.6 5.1 %collective-permute-start.2 = (f32[16,8,128]{2,1,0:T(8,128)S(1)}, f32[16,8,128]{2,1,0:T(8,128)S(1)}, u32[]{:S(2)}, u32[]{:S(2)}) collective-permute-start(f32[16,8,128]{2,1,0:T(8,128)S(1)} %get-tuple-element.18), channel_id=1, source_target_pairs={{0,9},{1,8},{2,11},{3,10},{4,13},{5,12},{6,15},{7,14},{8,17},{9,16... | collective-permute-start | bytes 196616 | tf_op jit(solution)/shard_map/ppermute | solution.py:484
  6.6 31.3 %collective-permute-start = (f32[8,8,128]{2,1,0:T(8,128)S(1)}, f32[8,8,128]{2,1,0:T(8,128)S(1)}, u32[]{:S(2)}, u32[]{:S(2)}) collective-permute-start(f32[8,8,128]{2,1,0:T(8,128)S(1)} %get-tuple-element.17), channel_id=1, source_target_pairs={{0,1},{1,2},{2,3},{3,4},{4,5},{5,6},{6,7},{7,0},{8,9},{9,10},{10,1... | collective-permute-start | bytes 98312 | tf_op jit(solution)/shard_map/ppermute | solution.py:478
  11.7 26.2 %collective-permute-start.4 = (f32[32,8,128]{2,1,0:T(8,128)S(1)}, f32[32,8,128]{2,1,0:T(8,128)S(1)}, u32[]{:S(2)}, u32[]{:S(2)}) collective-permute-start(f32[32,8,128]{2,1,0:T(8,128)S(1)} %constant_dynamic-update-slice_fusion), channel_id=1, source_target_pairs={{0,6},{1,7},{2,0},{3,1},{4,2},{5,3},{6,4},{7,5},{8,14},{9,15},{10,... | collective-permute-start | bytes 393224 | tf_op jit(solution)/shard_map/ppermute | solution.py:478
  15.3 22.7 %collective-permute-start.3 = (f32[32,8,128]{2,1,0:T(8,128)S(1)}, f32[32,8,128]{2,1,0:T(8,128)S(1)}, u32[]{:S(2)}, u32[]{:S(2)}) collective-permute-start(f32[32,8,128]{2,1,0:T(8,128)S(1)} %constant_dynamic-update-slice_fusion), channel_id=1, source_target_pairs={{0,2},{1,3},{2,4},{3,5},{4,6},{5,7},{6,0},{7,1},{8,10},{9,11},{10,... | collective-permute-start | bytes 393224 | tf_op jit(solution)/shard_map/ppermute | solution.py:478
  15.3 0.7 copy-start.7
  16.0 0.7 copy-start.8
  16.7 0.7 copy-start.9
  67.7 6.4 %collective-permute-start.6 = (f32[32,128]{1,0:T(8,128)S(1)}, f32[32,128]{1,0:T(8,128)S(1)}, u32[]{:S(2)}, u32[]{:S(2)}) collective-permute-start(f32[32,128]{1,0:T(8,128)S(1)} %get-tuple-element.22), channel_id=1, source_target_pairs={{0,6},{1,7},{2,0},{3,1},{4,2},{5,3},{6,4},{7,5},{8,14},{9,15},{10,... | collective-permute-start | bytes 49160 | tf_op jit(solution)/shard_map/ppermute | solution.py:478
  72.7 5.5 %collective-permute-start.7 = (f32[32,128]{1,0:T(8,128)S(1)}, f32[32,128]{1,0:T(8,128)S(1)}, u32[]{:S(2)}, u32[]{:S(2)}) collective-permute-start(f32[32,128]{1,0:T(8,128)S(1)} %get-tuple-element.23), channel_id=1, source_target_pairs={{0,2},{1,3},{2,4},{3,5},{4,6},{5,7},{6,0},{7,1},{8,10},{9,11},{10,... | collective-permute-start | bytes 49160 | tf_op jit(solution)/shard_map/ppermute | solution.py:478
  72.7 5.5 %collective-permute-start.8 = (f32[16,128]{1,0:T(8,128)S(1)}, f32[16,128]{1,0:T(8,128)S(1)}, u32[]{:S(2)}, u32[]{:S(2)}) collective-permute-start(f32[16,128]{1,0:T(8,128)S(1)} %get-tuple-element.24), channel_id=1, source_target_pairs={{0,8},{1,9},{2,10},{3,11},{4,12},{5,13},{6,14},{7,15},{8,16},{9,17... | collective-permute-start | bytes 24584 | tf_op jit(solution)/shard_map/ppermute | solution.py:484
  78.2 2.9 %collective-permute-start.9 = (f32[32,128]{1,0:T(8,128)S(1)}, f32[32,128]{1,0:T(8,128)S(1)}, u32[]{:S(2)}, u32[]{:S(2)}) collective-permute-start(f32[32,128]{1,0:T(8,128)S(1)} %pad_maximum_fusion), channel_id=1, source_target_pairs={{0,1},{1,0},{2,3},{3,2},{4,5},{5,4},{6,7},{7,6},{8,9},{9,8},{10,11... | collective-permute-start | bytes 49160 | tf_op jit(solution)/shard_map/ppermute | solution.py:481
  78.3 4.2 %collective-permute-start.5 = (f32[8,128]{1,0:T(8,128)S(1)}, f32[8,128]{1,0:T(8,128)S(1)}, u32[]{:S(2)}, u32[]{:S(2)}) collective-permute-start(f32[8,128]{1,0:T(8,128)S(1)} %get-tuple-element.20), channel_id=1, source_target_pairs={{0,7},{1,0},{2,1},{3,2},{4,3},{5,4},{6,5},{7,6},{8,15},{9,8},{10,9... | collective-permute-start | bytes 12296 | tf_op jit(solution)/shard_map/ppermute | solution.py:478
  81.2 5.2 %collective-permute-start.10 = (f32[16,128]{1,0:T(8,128)S(1)}, f32[16,128]{1,0:T(8,128)S(1)}, u32[]{:S(2)}, u32[]{:S(2)}) collective-permute-start(f32[16,128]{1,0:T(8,128)S(1)} %slice.40), channel_id=1, source_target_pairs={{0,24},{1,25},{2,26},{3,27},{4,28},{5,29},{6,30},{7,31},{8,0},{9,1... | collective-permute-start | bytes 24584 | tf_op jit(solution)/shard_map/ppermute | solution.py:484
  82.5 4.8 %collective-permute-start.11 = (f32[8,128]{1,0:T(8,128)S(1)}, f32[8,128]{1,0:T(8,128)S(1)}, u32[]{:S(2)}, u32[]{:S(2)}) collective-permute-start(f32[8,128]{1,0:T(8,128)S(1)} %get-tuple-element.30), channel_id=1, source_target_pairs={{0,1},{1,2},{2,3},{3,4},{4,5},{5,6},{6,7},{7,0},{8,9},{9,10},{10,1... | collective-permute-start | bytes 12296 | tf_op jit(solution)/shard_map/ppermute | solution.py:478
  82.5 5.3 %collective-permute-start.13 = (f32[32,128]{1,0:T(8,128)S(1)}, f32[32,128]{1,0:T(8,128)S(1)}, u32[]{:S(2)}, u32[]{:S(2)}) collective-permute-start(f32[32,128]{1,0:T(8,128)S(1)} %maximum_add_fusion.pair_rho), channel_id=1, source_target_pairs={{0,6},{1,7},{2,0},{3,1},{4,2},{5,3},{6,4},{7,5},{8,14},{9,15},{10,... | collective-permute-start | bytes 49160 | tf_op jit(solution)/shard_map/ppermute | solution.py:478
  86.4 5.5 %collective-permute-start.12 = (f32[32,128]{1,0:T(8,128)S(1)}, f32[32,128]{1,0:T(8,128)S(1)}, u32[]{:S(2)}, u32[]{:S(2)}) collective-permute-start(f32[32,128]{1,0:T(8,128)S(1)} %maximum_add_fusion.pair_rho), channel_id=1, source_target_pairs={{0,2},{1,3},{2,4},{3,5},{4,6},{5,7},{6,0},{7,1},{8,10},{9,11},{10,... | collective-permute-start | bytes 49160 | tf_op jit(solution)/shard_map/ppermute | solution.py:478
  86.4 5.5 %copy-start.6 = (f32[2,2]{1,0:T(2,128)S(1)}, f32[2,2]{1,0:T(2,128)}, u32[]{:S(2)}) copy-start(f32[2,2]{1,0:T(2,128)} %a_table.3) | copy-start | bytes 52
  134.5 4.7 %collective-permute-start.15 = (f32[3,32,128]{2,1,0:T(8,128)S(1)}, f32[3,32,128]{2,1,0:T(8,128)S(1)}, u32[]{:S(2)}, u32[]{:S(2)}) collective-permute-start(f32[3,32,128]{2,1,0:T(8,128)S(1)} %get-tuple-element.28), channel_id=1, source_target_pairs={{0,6},{1,7},{2,0},{3,1},{4,2},{5,3},{6,4},{7,5},{8,14},{9,15},{10,... | collective-permute-start | bytes 147464 | tf_op jit(solution)/shard_map/ppermute | solution.py:478
  135.7 5.9 %collective-permute-start.16 = (f32[3,32,128]{2,1,0:T(8,128)S(1)}, f32[3,32,128]{2,1,0:T(8,128)S(1)}, u32[]{:S(2)}, u32[]{:S(2)}) collective-permute-start(f32[3,32,128]{2,1,0:T(8,128)S(1)} %get-tuple-element.29), channel_id=1, source_target_pairs={{0,2},{1,3},{2,4},{3,5},{4,6},{5,7},{6,0},{7,1},{8,10},{9,11},{10,... | collective-permute-start | bytes 147464 | tf_op jit(solution)/shard_map/ppermute | solution.py:478
  141.6 1.3 collective-permute-start.17
  141.7 34.2 %collective-permute-start.14 = (f32[3,8,128]{2,1,0:T(8,128)S(1)}, f32[3,8,128]{2,1,0:T(8,128)S(1)}, u32[]{:S(2)}, u32[]{:S(2)}) collective-permute-start(f32[3,8,128]{2,1,0:T(8,128)S(1)} %get-tuple-element.26), channel_id=1, source_target_pairs={{0,7},{1,0},{2,1},{3,2},{4,3},{5,4},{6,5},{7,6},{8,15},{9,8},{10,9... | collective-permute-start | bytes 36872 | tf_op jit(solution)/shard_map/ppermute | solution.py:478
  142.9 33.0 %copy-start.1 = (f32[3,4096]{1,0:T(4,128)S(1)}, f32[3,4096]{1,0:T(4,128)}, u32[]{:S(2)}) copy-start(f32[3,4096]{1,0:T(4,128)} %pos.3) | copy-start | bytes 147460
  142.9 33.0 %copy-start.3 = (f32[3,4096]{1,0:T(4,128)S(1)}, f32[3,4096]{1,0:T(4,128)}, u32[]{:S(2)}) copy-start(f32[3,4096]{1,0:T(4,128)} %vel.3) | copy-start | bytes 147460
  142.9 33.0 %collective-permute-start.18 = (f32[3,16,128]{2,1,0:T(8,128)S(1)}, f32[3,16,128]{2,1,0:T(8,128)S(1)}, u32[]{:S(2)}, u32[]{:S(2)}) collective-permute-start(f32[3,16,128]{2,1,0:T(8,128)S(1)} %slice_add_fusion), channel_id=1, source_target_pairs={{0,24},{1,25},{2,26},{3,27},{4,28},{5,29},{6,30},{7,31},{8,0},{9,1... | collective-permute-start | bytes 73736 | tf_op jit(solution)/shard_map/ppermute | solution.py:484

commit v2 on v1

--- a/solution.py
+++ b/solution.py
@@ -17,7 +17,6 @@
 far_away = 10000.0
 density_scale = density_norm / (cutoff_density * cutoff_density)
 crowd_scale = repulse / cutoff_density
-STEP = 16
 VMEM = pl.BlockSpec(memory_space=pltpu.VMEM)
 SMEM = pl.BlockSpec(memory_space=pltpu.SMEM)
 f32 = jnp.float32
@@ -54,136 +53,161 @@
     face[...] = out[pl.ds(0, face.shape[0])]
 
 
-def spread_rows(tile, rows, channels):
-    width = tile.shape[1]
-    turned = tile.T
-    for c in range(channels):
-        rows[c] = jnp.broadcast_to(turned[:, c : c + 1], (width, width))
-
-
-def sized(count, width, body):
-    steps = (count + (STEP - 1)) // STEP
-
-    def case(k):
-        @pl.when(steps == k)
+def diagonal(width):
+    lane = lax.broadcasted_iota(jnp.int32, (8, width), 1)
+    return lane - lax.broadcasted_iota(jnp.int32, (8, width), 0)
+
+
+def spread_row(row, store):
+    width = row.shape[1]
+    diff = diagonal(width)
+    row = jnp.broadcast_to(row, (8, width))
+    for r in range(0, width, 8):
+        one = jnp.sum(jnp.where(diff == r, row, 0.0), axis=1, keepdims=True)
+        store(r, jnp.broadcast_to(one, (8, width)))
+
+
+def row_sums(acc, c):
+    width = acc.shape[2]
+    diff = diagonal(width)
+    out = jnp.zeros((8, width), f32)
+    for r in range(0, width, 8):
+        out = jnp.where(diff == r, jnp.sum(acc[c, pl.ds(r, 8), :], axis=1, keepdims=True), out)
+        acc[c, pl.ds(r, 8), :] = jnp.zeros((8, width), f32)
+    return out
+
+
+def branch(used, count, width, body):
+    sizes = (0,) + tuple(width * e // 8 for e in (4, 6, 8))
+    index = jnp.where(used, 1, 0)
+    for n in sizes[1:-1]:
+        index += jnp.where(used & (count > n), 1, 0)
+
+    def pick(low, high):
+        if low == high:
+            body(sizes[low])
+            return
+        middle = (low + high) // 2
+
+        @pl.when(index <= middle)
         def _():
-            body(k * STEP)
-
-    for k in range(1, width // STEP + 1):
-        case(k)
-
-
-def density_block(rows, other, r):
-    at = pl.ds(r, 8)
-    dx = rows[0, at, :] - other[0]
-    dy = rows[1, at, :] - other[1]
-    dz = rows[2, at, :] - other[2]
-    d2 = jnp.maximum(dx * dx + dy * dy + dz * dz, distance_floor)
-    w = jnp.maximum(cutoff_density - d2 * lax.rsqrt(d2), 0.0)
-    return w * w
+            pick(low, middle)
+
+        @pl.when(index > middle)
+        def _():
+            pick(middle + 1, high)
+
+    pick(0, len(sizes) - 1)
+
+
+def tile_loop(tiles, width, counts, slots, partner, pair, tasks):
+    def step(i, carry):
+        for half in range(2):
+            g = 2 * i + half
+            count = counts[g]
+            work = tasks(g, half)
+            for k in range(slots):
+                h, used = partner(g, k)
+
+                def body(n, k=k, h=h):
+                    if n:
+                        pair(g, half, k, h, n)
+                    for task in work[k::slots]:
+                        task()
+
+                branch(used & (count > 0), count, width, body)
+        return carry
+
+    lax.fori_loop(0, tiles // 2, step, 0)
 
 
 def column(ref, h, c):
     return jnp.broadcast_to(ref[h, pl.ds(c, 1), :], (8, ref.shape[2]))
 
 
-def density_pair(rows, union, h, count, acc_cols, acc_rows):
-    width = union.shape[2]
-
-    def body(n):
-        other = [column(union, h, c) for c in range(3)]
-        total = None
-        for r in range(0, n, 8):
-            w = density_block(rows, other, r)
-            total = w if total is None else total + w
+def density_pair(mine, union, h, n, acc_cols, acc_rows):
+    other = [column(union, h, c) for c in range(3)]
+    total = None
+    for r in range(0, n, 8):
+        d = [mine(c, r) - other[c] for c in range(3)]
+        d2 = jnp.maximum(d[0] * d[0] + d[1] * d[1] + d[2] * d[2], distance_floor)
+        w = jnp.maximum(cutoff_density - d2 * lax.rsqrt(d2), 0.0)
+        w = w * w
+        total = w if total is None else total + w
+        if acc_rows is not None:
+            acc_rows[0, pl.ds(r, 8), :] += w
+    acc_cols[h] += total
+
+
+def force_pair(mine, union, h, n, table, acc_cols, acc_rows):
+    a00, a01, a11 = table
+    other = [column(union, h, c) for c in range(8)]
+    first = a00 + other[6] * (a01 - a00)
+    slope = (a01 + other[6] * (a11 - a01)) - first
+    total = [None] * 3
+    for r in range(0, n, 8):
+        d = [mine(c, r) - other[c] for c in range(3)]
+        d2 = jnp.maximum(d[0] * d[0] + d[1] * d[1] + d[2] * d[2], distance_floor)
+        inverse = lax.rsqrt(d2)
+        dist = d2 * inverse
+        wc = jnp.maximum(1.0 - dist, 0.0)
+        wd = jnp.maximum(cutoff_density - dist, 0.0)
+        dv = [mine(3 + c, r) - other[3 + c] for c in range(3)]
+        approach = (d[0] * dv[0] + d[1] * dv[1] + d[2] * dv[2]) * inverse
+        scalar = (first + mine(6, r) * slope) - approach * wc
+        scalar = scalar * wc + (mine(7, r) + other[7]) * wd
+        scalar = scalar * inverse
+        for c in range(3):
+            push = d[c] * scalar
+            total[c] = push if total[c] is None else total[c] + push
             if acc_rows is not None:
-                acc_rows[0, pl.ds(r, 8), :] += w
-        acc_cols[h] += total
-
-    sized(count, width, body)
-
-
-def force_pair(rows, union, h, count, table, acc_cols, acc_rows):
-    width = union.shape[2]
-    a00, a01, a11 = table
-
-    def body(n):
-        other = [column(union, h, c) for c in range(8)]
-        first = a00 + other[6] * (a01 - a00)
-        slope = (a01 + other[6] * (a11 - a01)) - first
-        total = [None] * 3
-        for r in range(0, n, 8):
-            mine = [rows[c, pl.ds(r, 8), :] for c in range(8)]
-            d = [mine[c] - other[c] for c in range(3)]
-            d2 = jnp.maximum(d[0] * d[0] + d[1] * d[1] + d[2] * d[2], distance_floor)
-            inverse = lax.rsqrt(d2)
-            dist = d2 * inverse
-            wc = jnp.maximum(1.0 - dist, 0.0)
-            wd = jnp.maximum(cutoff_density - dist, 0.0)
-            dv = [mine[3 + c] - other[3 + c] for c in range(3)]
-            approach = (d[0] * dv[0] + d[1] * dv[1] + d[2] * dv[2]) * inverse
-            scalar = (first + mine[6] * slope) - approach * wc
-            scalar = scalar * wc + (mine[7] + other[7]) * wd
-            scalar = scalar * inverse
-            for c in range(3):
-                push = d[c] * scalar
-                total[c] = push if total[c] is None else total[c] + push
-                if acc_rows is not None:
-                    acc_rows[c, pl.ds(r, 8), :] += push
-        for c in range(3):
-            acc_cols[c, h] -= total[c]
-
-    sized(count, width, body)
-
-
-def row_sums(acc):
-    first = (lax.broadcasted_iota(jnp.int32, (8, acc.shape[1]), 0) == 0).astype(f32)
-    return lax.dot_general(
-        first,
-        acc,
-        (((1,), (1,)), ((), ())),
-        precision=lax.Precision.HIGHEST,
-        preferred_element_type=f32,
-    )
-
-
-def fold(ref, tiles, out, scale=None):
-    def one(t, carry):
-        value = jnp.sum(ref[t], axis=0, keepdims=True)
-        out[pl.ds(t, 1), :] = value
-        return carry
-
-    lax.fori_loop(0, tiles, one, 0)
-
-
-def local_density_kernel(counts, nbr, union, acc, rows, acc_rows):
+                acc_rows[c, pl.ds(r, 8), :] += push
+    for c in range(3):
+        acc_cols[c, h] -= total[c]
+
+
+def zero(*refs):
+    for ref in refs:
+        ref[...] = jnp.zeros_like(ref)
+
+
+def local_density_kernel(counts, nbr, union, acc, spread, rows_0, rows_1, sums_0, sums_1):
     tiles, width = union.shape[0], union.shape[2]
-    acc[...] = jnp.zeros_like(acc)
-
-    def tile(g, carry):
-        count = counts[g]
-
-        @pl.when(count > 0)
-        def _():
-            spread_rows(union[g], rows, 3)
-            density_pair(rows, union, g, count, acc, None)
-            acc_rows[0] = jnp.zeros((width, width), f32)
-
-            def partner(k, carry):
-                h = nbr[g, k]
-
-                @pl.when((h >= 0) & (counts[jnp.maximum(h, 0)] > 0))
-                def _():
-                    density_pair(rows, union, h, count, acc, acc_rows)
-
-                return carry
-
-            lax.fori_loop(0, nbr.shape[1], partner, 0)
-            acc[g] += row_sums(acc_rows[0])
-
-        return carry
-
-    lax.fori_loop(0, tiles, tile, 0)
+    rows, sums = (rows_0, rows_1), (sums_0, sums_1)
+    zero(acc, *sums)
+
+    def fill(g, c, half):
+        def store(r, value):
+            spread[g, c, pl.ds(r, 8), :] = value
+            if c < 3:
+                rows[half][c, pl.ds(r, 8), :] = value
+
+        row = union[g, pl.ds(c, 1), :]
+        spread_row(row * friction if 3 <= c < 6 else row, store)
+
+    def tasks(g, half):
+        after, before = jnp.minimum(g + 1, tiles - 1), jnp.maximum(g - 1, 0)
+
+        def collect():
+            acc[before] += row_sums(sums[1 - half], 0)
+
+        work = [functools.partial(fill, after, c, 1 - half) for c in range(spread.shape[1])]
+        return work[:6] + [collect] + work[6:]
+
+    def partner(g, k):
+        if k == 0:
+            return g, True
+        h = nbr[g, k - 1]
+        return jnp.maximum(h, 0), (h >= 0) & (counts[jnp.maximum(h, 0)] > 0)
+
+    def pair(g, half, k, h, n):
+        mine = lambda c, r: rows[half][c, pl.ds(r, 8), :]
+        density_pair(mine, union, h, n, acc, sums[half] if k else None)
+
+    for c in range(spread.shape[1]):
+        fill(0, c, 0)
+    tile_loop(tiles, width, counts, 1 + nbr.shape[1], partner, pair, tasks)
+    acc[tiles - 1] += row_sums(sums[1], 0)
 
 
 def gather_ghosts(ghosts, face, near, flip, below, above):
@@ -204,9 +228,11 @@
 
 def ghost_partner(k, g, face_nbr, cross_pair, where, meta, faces, upper, cap, reach):
     columns = face_nbr.shape[1]
-    is_face = k < columns
-    f = face_nbr[g, jnp.minimum(k, columns - 1)]
-    s = cross_pair[g, jnp.maximum(k - columns, 0)]
+    if k < columns:
+        f = face_nbr[g, k]
+        h = jnp.maximum(f, 0)
+        return h, (f >= 0) & (meta[h, meta.shape[1] - 1] > 0)
+    s = cross_pair[g, k - columns]
     layer, core = where[0], where[1]
     slot = jnp.maximum(s, 0)
     o = slot // cap
@@ -217,10 +243,8 @@
     hops = jnp.where(hop == 0, 0, jnp.where(hop < 0, 1, 2))
     base = faces + (hops * 2 + flipped) * upper
     u = meta[base + o, c]
-    ok = (s >= 0) & (layer > 0) & (u >= 0)
-    h = jnp.where(is_face, jnp.maximum(f, 0), base + jnp.maximum(u, 0))
-    ok = jnp.where(is_face, f >= 0, ok)
-    return h, ok & (meta[h, meta.shape[1] - 1] > 0)
+    h = base + jnp.maximum(u, 0)
+    return h, (s >= 0) & (layer > 0) & (u >= 0) & (meta[h, meta.shape[1] - 1] > 0)
 
 
 def ghost_density_kernel(
@@ -232,7 +256,7 @@
     counts,
     face_nbr,
     cross_pair,
-    union,
+    spread,
     local_acc,
     face,
     near,
@@ -248,45 +272,40 @@
     ghosts,
     acc,
     acc_own,
-    rows,
-    acc_rows,
+    sums_0,
+    sums_1,
     reduced,
     meta,
     meta_smem,
     sem,
 ):
-    tiles, width = union.shape[0], union.shape[2]
+    tiles, width = spread.shape[0], spread.shape[2]
+    sums = (sums_0, sums_1)
     gather_ghosts(ghosts, face, near, flip, below, above)
     ghost_meta(ghosts, faces, upper, meta, meta_smem, sem)
-    acc[...] = jnp.zeros_like(acc)
+    zero(acc, *sums)
+    acc_own[...] = local_acc[...]
     columns = face_nbr.shape[1] + cross_pair.shape[1]
 
-    def tile(g, carry):
-        count = counts[g]
-        acc_own[g] = local_acc[g]
-
-        @pl.when(count > 0)
-        def _():
-            spread_rows(union[g], rows, 3)
-            acc_rows[0] = jnp.zeros((width, width), f32)
-
-            def partner(k, carry):
-                h, ok = ghost_partner(
-                    k, g, face_nbr, cross_pair, where, meta_smem, faces, upper, cap, reach
-                )
-
-                @pl.when(ok)
-                def _():
-                    density_pair(rows, ghosts, h, count, acc, acc_rows)
-
-                return carry
-
-            lax.fori_loop(0, columns, partner, 0)
-            acc_own[g] += row_sums(acc_rows[0])
-
-        return carry
-
-    lax.fori_loop(0, tiles, tile, 0)
+    def tasks(g, half):
+        before = jnp.maximum(g - 1, 0)
+
+        def collect():
+            acc_own[before] += row_sums(sums[1 - half], 0)
+
+        return [collect]
+
+    def partner(g, k):
+        return ghost_partner(
+            k, g, face_nbr, cross_pair, where, meta_smem, faces, upper, cap, reach
+        )
+
+    def pair(g, half, k, h, n):
+        mine = lambda c, r: spread[g, c, pl.ds(r, 8), :]
+        density_pair(mine, ghosts, h, n, acc, sums[half])
+
+    tile_loop(tiles, width, counts, columns, partner, pair, tasks)
+    acc_own[tiles - 1] += row_sums(sums[1], 0)
     self_term = (cutoff_density - math.sqrt(distance_floor)) ** 2
     for t in range(tiles):
         lane = lax.broadcasted_iota(jnp.int32, (1, width), 1)
@@ -312,38 +331,60 @@
     return (a_table[0, 0], 0.5 * (a_table[0, 1] + a_table[1, 0]), a_table[1, 1])
 
 
-def local_force_kernel(counts, nbr, a_table, union, density, acc, beads, rows, acc_rows):
+def force_tasks(tiles, beads, rows, sums, acc):
+    def fill(g, half):
+        def store(r, value):
+            rows[half][pl.ds(r, 8), :] = value
+
+        spread_row(beads[g, pl.ds(7, 1), :], store)
+
+    def tasks(g, half):
+        after, before = jnp.minimum(g + 1, tiles - 1), jnp.maximum(g - 1, 0)
+
+        def collect(c):
+            acc[c, before] += row_sums(sums[1 - half], c)
+
+        work = [functools.partial(collect, c) for c in range(3)]
+        return [functools.partial(fill, after, 1 - half)] + work
+
+    def last():
+        for c in range(3):
+            acc[c, tiles - 1] += row_sums(sums[1], c)
+
+    return lambda: fill(0, 0), tasks, last
+
+
+def force_mine(spread, rows, g, half):
+    def mine(c, r):
+        return rows[half][pl.ds(r, 8), :] if c == 7 else spread[g, c, pl.ds(r, 8), :]
+
+    return mine
+
+
+def local_force_kernel(
+    counts, nbr, a_table, union, spread, density, acc, beads, rows_0, rows_1, sums_0, sums_1
+):
     tiles, width = union.shape[0], union.shape[2]
+    rows, sums = (rows_0, rows_1), (sums_0, sums_1)
     table = amplitudes(a_table)
-    acc[...] = jnp.zeros_like(acc)
+    zero(acc, *sums)
     for t in range(tiles):
         beads[t] = force_tile(union, density[pl.ds(t, 1), :], t)
-
-    def tile(g, carry):
-        count = counts[g]
-
-        @pl.when(count > 0)
-        def _():
-            spread_rows(beads[g], rows, 8)
-            force_pair(rows, beads, g, count, table, acc, None)
-            acc_rows[...] = jnp.zeros_like(acc_rows)
-
-            def partner(k, carry):
-                h = nbr[g, k]
-
-                @pl.when((h >= 0) & (counts[jnp.maximum(h, 0)] > 0))
-                def _():
-                    force_pair(rows, beads, h, count, table, acc, acc_rows)
-
-                return carry
-
-            lax.fori_loop(0, nbr.shape[1], partner, 0)
-            for c in range(3):
-                acc[c, g] += row_sums(acc_rows[c])
-
-        return carry
-
-    lax.fori_loop(0, tiles, tile, 0)
+    first, tasks, last = force_tasks(tiles, beads, rows, sums, acc)
+
+    def partner(g, k):
+        if k == 0:
+            return g, True
+        h = nbr[g, k - 1]
+        return jnp.maximum(h, 0), (h >= 0) & (counts[jnp.maximum(h, 0)] > 0)
+
+    def pair(g, half, k, h, n):
+        mine = force_mine(spread, rows, g, half)
+        force_pair(mine, beads, h, n, table, acc, sums[half] if k else None)
+
+    first()
+    tile_loop(tiles, width, counts, 1 + nbr.shape[1], partner, pair, tasks)
+    last()
 
 
 def ghost_force_kernel(
@@ -357,6 +398,7 @@
     cross_pair,
     a_table,
     union,
+    spread,
     density,
     face,
     near,
@@ -376,18 +418,20 @@
     beads,
     acc,
     rho,
-    rows,
-    acc_rows,
+    rows_0,
+    rows_1,
+    sums_0,
+    sums_1,
     reduced,
     meta,
     meta_smem,
     sem,
 ):
     tiles, width = union.shape[0], union.shape[2]
+    rows, sums = (rows_0, rows_1), (sums_0, sums_1)
     gather_ghosts(ghosts, face, near, flip, below, above)
     ghost_meta(ghosts, faces, upper, meta, meta_smem, sem)
-    acc[...] = jnp.zeros_like(acc)
-    own_out[...] = jnp.zeros_like(own_out)
+    zero(acc, own_out, *sums)
     table = amplitudes(a_table)
     columns = face_nbr.shape[1] + cross_pair.shape[1]
     at = 0
@@ -399,32 +443,20 @@
     for t in range(tiles):
         beads[t] = force_tile(union, density[pl.ds(t, 1), :], t)
 
-    def tile(g, carry):
-        count = counts[g]
-
-        @pl.when(count > 0)
-        def _():
-            spread_rows(beads[g], rows, 8)
-            acc_rows[...] = jnp.zeros_like(acc_rows)
-
-            def partner(k, carry):
-                h, ok = ghost_partner(
-                    k, g, face_nbr, cross_pair, where, meta_smem, faces, upper, cap, reach
-                )
-
-                @pl.when(ok)
-                def _():
-                    force_pair(rows, ghosts, h, count, table, acc, acc_rows)
-
-                return carry
-
-            lax.fori_loop(0, columns, partner, 0)
-            for c in range(3):
-                own_out[c, g] = row_sums(acc_rows[c])
-
-        return carry
-
-    lax.fori_loop(0, tiles, tile, 0)
+    first, tasks, last = force_tasks(tiles, beads, rows, sums, own_out)
+
+    def partner(g, k):
+        return ghost_partner(
+            k, g, face_nbr, cross_pair, where, meta_smem, faces, upper, cap, reach
+        )
+
+    def pair(g, half, k, h, n):
+        mine = force_mine(spread, rows, g, half)
+        force_pair(mine, ghosts, h, n, table, acc, sums[half])
+
+    first()
+    tile_loop(tiles, width, counts, columns, partner, pair, tasks)
+    last()
     for c in range(3):
         for t in range(acc.shape[1]):
             reduced[pl.ds(t, 1), :] = jnp.sum(acc[c, t], axis=0, keepdims=True)
@@ -507,12 +539,15 @@
     above = lateral(chip_ghosts, -2)
     where = jnp.stack([lax.axis_index("layer"), lax.axis_index("lat") % 2]).astype(jnp.int32)
 
-    local_acc = pl.pallas_call(
+    square = pltpu.VMEM((width, width), f32)
+    square_1 = pltpu.VMEM((1, width, width), f32)
+    square_3 = pltpu.VMEM((3, width, width), f32)
+    local_acc, spread = pl.pallas_call(
         local_density_kernel,
-        out_shape=sds(tiles, 8, width),
+        out_shape=(sds(tiles, 8, width), sds(tiles, 7, width, width)),
         in_specs=[SMEM, SMEM, VMEM],
-        out_specs=VMEM,
-        scratch_shapes=[pltpu.VMEM((3, width, width), f32), pltpu.VMEM((1, width, width), f32)],
+        out_specs=[VMEM] * 2,
+        scratch_shapes=[square_3, square_3, square_1, square_1],
         cost_estimate=pl.CostEstimate(flops=200 * 10**6, bytes_accessed=10**6, transcendentals=0),
         compiler_params=params(),
     )(counts, local_nbr, payload)
@@ -539,8 +574,8 @@
             pltpu.VMEM((total, 8, width), f32),
             pltpu.VMEM((total, 8, width), f32),
             pltpu.VMEM((tiles, 8, width), f32),
-            pltpu.VMEM((3, width, width), f32),
-            pltpu.VMEM((1, width, width), f32),
+            square_1,
+            square_1,
             pltpu.VMEM((total, width), f32),
         ]
         + meta_scratch,
@@ -550,7 +585,7 @@
         counts,
         face_nbr,
         cross_pair,
-        payload,
+        spread,
         local_acc,
         face_ghosts,
         near,
@@ -583,15 +618,17 @@
             sds(3, 2 * upper, width),
             sds(3, 2 * upper, width),
         ),
-        in_specs=[SMEM] * 5 + [VMEM] * 11,
+        in_specs=[SMEM] * 5 + [VMEM] * 12,
         out_specs=[VMEM] * 5,
         scratch_shapes=[
             pltpu.VMEM((total, 8, width), f32),
             pltpu.VMEM((tiles, 8, width), f32),
             pltpu.VMEM((3, total, 8, width), f32),
             pltpu.VMEM((total, width), f32),
-            pltpu.VMEM((8, width, width), f32),
-            pltpu.VMEM((3, width, width), f32),
+            square,
+            square,
+            square_3,
+            square_3,
             pltpu.VMEM((total, width), f32),
         ]
         + meta_scratch,
@@ -603,6 +640,7 @@
         cross_pair,
         a_table,
         payload,
+        spread,
         density,
         face_ghosts,
         near,
@@ -623,16 +661,18 @@
     local_force = pl.pallas_call(
         local_force_kernel,
         out_shape=sds(3, tiles, 8, width),
-        in_specs=[SMEM, SMEM, SMEM, VMEM, VMEM],
+        in_specs=[SMEM, SMEM, SMEM, VMEM, VMEM, VMEM],
         out_specs=VMEM,
         scratch_shapes=[
             pltpu.VMEM((tiles, 8, width), f32),
-            pltpu.VMEM((8, width, width), f32),
-            pltpu.VMEM((3, width, width), f32),
+            square,
+            square,
+            square_3,
+            square_3,
         ],
         cost_estimate=pl.CostEstimate(flops=400 * 10**6, bytes_accessed=10**6, transcendentals=0),
         compiler_params=params(),
-    )(counts, local_nbr, a_table, payload, density)
+    )(counts, local_nbr, a_table, payload, spread, density)
 
     return pl.pallas_call(
         finish_kernel,

time: 177 us -> 112 us (0.63); the launches traced: 177 us -> 110 us
  Pallas kernels: 128 us -> 62.2 us
    pallas_call x1, Pallas kernels: 42.5 us -> 20.1 us  [on_device(): pl.pallas_call(functools.partial(ghost_force_kernel, *sizes), out_shape=(...]
    pallas_call x1, Pallas kernels: 32.9 us -> 12.8 us  [on_device(): pl.pallas_call(local_force_kernel, out_shape=sds(3, tiles, 8, width), in_...]
    pallas_call x1, Pallas kernels: 29.7 us -> 13 us  [on_device(): pl.pallas_call(functools.partial(ghost_density_kernel, *sizes), out_shape...]
    pallas_call x1, Pallas kernels: 20.5 us -> 14.1 us  [on_device(): pl.pallas_call(local_density_kernel, out_shape=(sds(tiles, 8, width), sds...]
    unnamed x25 -> x21, local copies, waits for them, and re-layouts: 5.8 us -> 6.69 us
  transfers between devices with their start and end apart: 19 -> 19, of which waited for: 11 -> 11; matrix products, arithmetic and copies ran while one was open for 0% -> 2% of each run, Pallas kernels for 30% -> 24%
where the time goes in v2:
time: 112 us; the launch traced here: 110 us
  Pallas kernels  62.2 us (56%)
  waiting for transfers between devices  22.2 us (20%)
  starting transfers between devices  18.3 us (16%)
  local copies, waits for them, and re-layouts  6.71 us (6%)
    pallas_call x1, Pallas kernels, on_device(): pl.pallas_call(functools.partial(ghost_force_kernel, *sizes), out_shape=(...  20.1 us
    ppermute x12, starting transfers between devices, lateral(): lax.ppermute(value, 'lat', [(m, (m + by) % places) for m in range(places)])  16.6 us
    ppermute x12, waiting for transfers between devices, lateral(): lax.ppermute(value, 'lat', [(m, (m + by) % places) for m in range(places)])  16.2 us
    pallas_call x1, Pallas kernels, on_device(): pl.pallas_call(local_density_kernel, out_shape=(sds(tiles, 8, width), sds...  14.1 us
    pallas_call x1, Pallas kernels, on_device(): pl.pallas_call(functools.partial(ghost_density_kernel, *sizes), out_shape...  13 us
    pallas_call x1, Pallas kernels, on_device(): pl.pallas_call(local_force_kernel, out_shape=sds(3, tiles, 8, width), in_...  12.8 us
    unnamed x21, local copies, waits for them, and re-layouts  6.69 us
    ppermute x5, waiting for transfers between devices, climb(): lax.ppermute(value, both, [(l * places + m, (l + by) % layers * places +...  4.9 us
  transfers between devices with their start and end apart: 19, of which 11 were waited for; matrix products, arithmetic and copies ran while one was open for 2% of the time, Pallas kernels for 24%

profile of v2, /device:TPU:4, one launch (start us, length us, event | category | flops | bytes accessed | tf_op | source)
XLA Modules:
  0.0 110.3 jit_solution(11664587049415635322)
XLA Ops:
  0.6 0.7 copy.11.send
  1.3 0.8 copy-done
  2.2 0.8 copy-done.2
  3.0 0.7 copy-done.4
  3.7 0.7 copy-done.5
  4.4 0.7 shard_map.104
  5.1 1.5 %collective-permute-start.1 = (f32[16,8,128]{2,1,0:T(8,128)S(1)}, f32[16,8,128]{2,1,0:T(8,128)S(1)}, u32[]{:S(2)}, u32[]{:S(2)}) collective-permute-start(f32[16,8,128]{2,1,0:T(8,128)S(1)} %get-tuple-element.22), channel_id=1, source_target_pairs={{0,8},{1,9},{2,10},{3,11},{4,12},{5,13},{6,14},{7,15},{8,16},{9,17... | collective-permute-start | bytes 196616 | tf_op jit(solution)/shard_map/ppermute | solution.py:516
  6.6 0.0 collective-permute-start.2
  6.6 0.2 collective-permute-start
  6.8 3.5 %collective-permute-done.1.near = f32[16,8,128]{2,1,0:T(8,128)S(1)} collective-permute-done((f32[16,8,128]{2,1,0:T(8,128)S(1)}, f32[16,8,128]{2,1,0:T(8,128)S(1)}, u32[]{:S(2)}, u32[]{:S(2)}) %collective-permute-start.1) | collective-permute-done | bytes 65568 | tf_op jit(solution)/shard_map/ppermute | solution.py:516
  10.3 1.4 %collective-permute-done.2.flip = f32[16,8,128]{2,1,0:T(8,128)S(1)} collective-permute-done((f32[16,8,128]{2,1,0:T(8,128)S(1)}, f32[16,8,128]{2,1,0:T(8,128)S(1)}, u32[]{:S(2)}, u32[]{:S(2)}) %collective-permute-start.2) | collective-permute-done | bytes 65568 | tf_op jit(solution)/shard_map/ppermute | solution.py:516
  11.7 3.6 %collective-permute-start.4 = (f32[32,8,128]{2,1,0:T(8,128)S(1)}, f32[32,8,128]{2,1,0:T(8,128)S(1)}, u32[]{:S(2)}, u32[]{:S(2)}) collective-permute-start(f32[32,8,128]{2,1,0:T(8,128)S(1)} %constant_dynamic-update-slice_fusion), channel_id=1, source_target_pairs={{0,6},{1,7},{2,0},{3,1},{4,2},{5,3},{6,4},{7,5},{8,14},{9,15},{10,... | collective-permute-start | bytes 393224 | tf_op jit(solution)/shard_map/ppermute | solution.py:510
  15.3 0.1 pad_add_fusion.where
  15.4 0.8 copy.15.nbr
  16.2 0.8 copy.13.face_nbr
  16.9 0.8 copy.14.cross_pair
  17.7 0.7 copy-done.6
  18.3 14.1 %shard_map.105 = (f32[32,8,128]{2,1,0:T(8,128)S(1)}, f32[32,7,128,128]{3,2,1,0:T(8,128)S(1)}) custom-call(s32[32]{0:T(128)S(1)} %copy-done.6, s32[32,2]{1,0:T(8,128)S(1)} %copy.15.nbr, f32[32,8,128]{2,1,0:T(8,128)S(1)} %get-tuple-element.18.union), custom_call_target="tpu_custom_call" | custom-call | flops 200000000 | bytes 1000000 | tf_op jit(solution)/shard_map/pallas_call | solution.py:545
  32.4 0.0 collective-permute-done.4.above
  32.5 0.0 collective-permute-done.3.below
  32.5 13.0 %shard_map.106 = (f32[32,128]{1,0:T(8,128)S(1)}, f32[16,128]{1,0:T(8,128)S(1)}, f32[8,128]{1,0:T(8,128)S(1)}, f32[32,128]{1,0:T(8,128)S(1)}, f32[32,128]{1,0:T(8,128)S(1)}, /*index=5*/f32[32,128]{1,0:T(8,128)S(1)}) custom-call(s32[2]{0:T(128)S(1)} %pad_add_fusion.where, s32[32]{0:T(128)S(1)} %copy-done.6, s32[32,2]{1,0:T(8,128)S(1)} %copy.13.face_nbr, ...), custom_call_target="tpu_custom_call" | custom-call | tf_op jit(solution)/shard_map/pallas_call | solution.py:561
  45.5 3.8 %collective-permute-start.6 = (f32[32,128]{1,0:T(8,128)S(1)}, f32[32,128]{1,0:T(8,128)S(1)}, u32[]{:S(2)}, u32[]{:S(2)}) collective-permute-start(f32[32,128]{1,0:T(8,128)S(1)} %get-tuple-element.26), channel_id=1, source_target_pairs={{0,6},{1,7},{2,0},{3,1},{4,2},{5,3},{6,4},{7,5},{8,14},{9,15},{10,... | collective-permute-start | bytes 49160 | tf_op jit(solution)/shard_map/ppermute | solution.py:510
  49.4 1.4 %collective-permute-done.6 = f32[32,128]{1,0:T(8,128)S(1)} collective-permute-done((f32[32,128]{1,0:T(8,128)S(1)}, f32[32,128]{1,0:T(8,128)S(1)}, u32[]{:S(2)}, u32[]{:S(2)}) %collective-permute-start.6) | collective-permute-done | bytes 16416 | tf_op jit(solution)/shard_map/ppermute | solution.py:510
  50.8 4.1 %collective-permute-done.7 = f32[32,128]{1,0:T(8,128)S(1)} collective-permute-done((f32[32,128]{1,0:T(8,128)S(1)}, f32[32,128]{1,0:T(8,128)S(1)}, u32[]{:S(2)}, u32[]{:S(2)}) %collective-permute-start.7) | collective-permute-done | bytes 16416 | tf_op jit(solution)/shard_map/ppermute | solution.py:510
  54.9 0.0 collective-permute-done.8
  54.9 0.1 collective-permute-start.9
  55.0 2.8 %collective-permute-start.5 = (f32[8,128]{1,0:T(8,128)S(1)}, f32[8,128]{1,0:T(8,128)S(1)}, u32[]{:S(2)}, u32[]{:S(2)}) collective-permute-start(f32[8,128]{1,0:T(8,128)S(1)} %get-tuple-element.24), channel_id=1, source_target_pairs={{0,7},{1,0},{2,1},{3,2},{4,3},{5,4},{6,5},{7,6},{8,15},{9,8},{10,9... | collective-permute-start | bytes 12296 | tf_op jit(solution)/shard_map/ppermute | solution.py:510
  57.9 0.0 collective-permute-done.9
  57.9 0.1 collective-permute-start.10
  57.9 1.2 %collective-permute-done.5 = f32[8,128]{1,0:T(8,128)S(1)} collective-permute-done((f32[8,128]{1,0:T(8,128)S(1)}, f32[8,128]{1,0:T(8,128)S(1)}, u32[]{:S(2)}, u32[]{:S(2)}) %collective-permute-start.5) | collective-permute-done | bytes 4128 | tf_op jit(solution)/shard_map/ppermute | solution.py:510
  59.2 0.0 collective-permute-start.11
  59.2 3.9 %collective-permute-start.13 = (f32[32,128]{1,0:T(8,128)S(1)}, f32[32,128]{1,0:T(8,128)S(1)}, u32[]{:S(2)}, u32[]{:S(2)}) collective-permute-start(f32[32,128]{1,0:T(8,128)S(1)} %maximum_add_fusion.pair_rho), channel_id=1, source_target_pairs={{0,6},{1,7},{2,0},{3,1},{4,2},{5,3},{6,4},{7,5},{8,14},{9,15},{10,... | collective-permute-start | bytes 49160 | tf_op jit(solution)/shard_map/ppermute | solution.py:510
  63.1 0.0 copy-start.1
  63.1 0.0 copy-start.3
  63.1 0.9 collective-permute-done.11.face_rho
  64.0 0.5 collective-permute-done.13.above_rho
  64.5 4.1 %collective-permute-done.12.below_rho = f32[32,128]{1,0:T(8,128)S(1)} collective-permute-done((f32[32,128]{1,0:T(8,128)S(1)}, f32[32,128]{1,0:T(8,128)S(1)}, u32[]{:S(2)}, u32[]{:S(2)}) %collective-permute-start.12) | collective-permute-done | bytes 16416 | tf_op jit(solution)/shard_map/ppermute | solution.py:510
  68.6 20.1 %shard_map.108 = (f32[3,32,8,128]{3,2,1,0:T(8,128)S(1)}, f32[3,8,128]{2,1,0:T(8,128)S(1)}, f32[3,32,128]{2,1,0:T(8,128)S(1)}, f32[3,32,128]{2,1,0:T(8,128)S(1)}, f32[3,32,128]{2,1,0:T(8,128)S(1)}) custom-call(s32[2]{0:T(128)S(1)} %pad_add_fusion.where, s32[32]{0:T(128)S(1)} %copy-done.6, s32[32,2]{1,0:T(8,128)S(1)} %copy.13.face_nbr, ...), custom_call_target="tpu_custom_call" | custom-call | tf_op jit(solution)/shard_map/pallas_call | solution.py:612
  88.7 0.1 collective-permute-start.15
  88.9 1.9 %collective-permute-start.16 = (f32[3,32,128]{2,1,0:T(8,128)S(1)}, f32[3,32,128]{2,1,0:T(8,128)S(1)}, u32[]{:S(2)}, u32[]{:S(2)}) collective-permute-start(f32[3,32,128]{2,1,0:T(8,128)S(1)} %get-tuple-element.33), channel_id=1, source_target_pairs={{0,2},{1,3},{2,4},{3,5},{4,6},{5,7},{6,0},{7,1},{8,10},{9,11},{10,... | collective-permute-start | bytes 147464 | tf_op jit(solution)/shard_map/ppermute | solution.py:510
  90.8 2.2 %collective-permute-done.15 = f32[3,32,128]{2,1,0:T(8,128)S(1)} collective-permute-done((f32[3,32,128]{2,1,0:T(8,128)S(1)}, f32[3,32,128]{2,1,0:T(8,128)S(1)}, u32[]{:S(2)}, u32[]{:S(2)}) %collective-permute-start.15) | collective-permute-done | bytes 49184 | tf_op jit(solution)/shard_map/ppermute | solution.py:510
  93.0 1.7 %collective-permute-done.16 = f32[3,32,128]{2,1,0:T(8,128)S(1)} collective-permute-done((f32[3,32,128]{2,1,0:T(8,128)S(1)}, f32[3,32,128]{2,1,0:T(8,128)S(1)}, u32[]{:S(2)}, u32[]{:S(2)}) %collective-permute-start.16) | collective-permute-done | bytes 49184 | tf_op jit(solution)/shard_map/ppermute | solution.py:510
  94.8 0.1 collective-permute-start.17
  94.9 0.1 collective-permute-start.14
  95.0 1.1 collective-permute-done.17
  96.1 12.8 %shard_map.107.local_acc = f32[3,32,8,128]{3,2,1,0:T(8,128)S(1)} custom-call(s32[32]{0:T(128)S(1)} %copy-done.6, s32[32,2]{1,0:T(8,128)S(1)} %copy.15.nbr, f32[2,2]{1,0:T(2,128)S(1)} %copy-done.7, f32[32,8,128]{2,1,0:T(8,128)S(1)} %get-tuple-element.18.union, f32[32,7,128,128]{3,2,1,0:T(8,128)S(1)} %get-tuple-element.19.spread, ...), custom_call_target="tpu_custom_call" | custom-call | flops 400000000 | bytes 1000000 | tf_op jit(solution)/shard_map/pallas_call | solution.py:661
  108.9 0.0 collective-permute-done.18.top_back
  108.9 1.4 %shard_map.109 = (f32[3,4096]{1,0:T(4,128)}, f32[3,4096]{1,0:T(4,128)}) custom-call(s32[32]{0:T(128)S(1)} %copy-done.6, f32[3,4096]{1,0:T(4,128)S(1)} %copy-done.1, f32[3,4096]{1,0:T(4,128)S(1)} %copy-done.3, f32[3,32,8,128]{3,2,1,0:T(8,128)S(1)} %shard_map.107.local_acc, f32[3,32,8,128]{3,2,1,0:T(8,128)S(1)} %get-tuple-element.29.ghost_acc, ...), custom_call_target="tpu_custom_call" | custom-call | tf_op jit(solution)/shard_map/pallas_call | solution.py:677
  (30 shorter events, 0.1 us)
Async XLA Ops:
  0.6 68.0 %copy-start.7 = (f32[2,2]{1,0:T(2,128)S(1)}, f32[2,2]{1,0:T(2,128)}, u32[]{:S(2)}) copy-start(f32[2,2]{1,0:T(2,128)} %a_table.3) | copy-start | bytes 52
  1.3 0.8 copy-start
  2.2 0.8 copy-start.2
  3.0 0.7 copy-start.4
  3.7 0.7 copy-start.5
  5.1 5.2 %collective-permute-start.1 = (f32[16,8,128]{2,1,0:T(8,128)S(1)}, f32[16,8,128]{2,1,0:T(8,128)S(1)}, u32[]{:S(2)}, u32[]{:S(2)}) collective-permute-start(f32[16,8,128]{2,1,0:T(8,128)S(1)} %get-tuple-element.22), channel_id=1, source_target_pairs={{0,8},{1,9},{2,10},{3,11},{4,12},{5,13},{6,14},{7,15},{8,16},{9,17... | collective-permute-start | bytes 196616 | tf_op jit(solution)/shard_map/ppermute | solution.py:516
  6.6 5.1 %collective-permute-start.2 = (f32[16,8,128]{2,1,0:T(8,128)S(1)}, f32[16,8,128]{2,1,0:T(8,128)S(1)}, u32[]{:S(2)}, u32[]{:S(2)}) collective-permute-start(f32[16,8,128]{2,1,0:T(8,128)S(1)} %get-tuple-element.22), channel_id=1, source_target_pairs={{0,9},{1,8},{2,11},{3,10},{4,13},{5,12},{6,15},{7,14},{8,17},{9,16... | collective-permute-start | bytes 196616 | tf_op jit(solution)/shard_map/ppermute | solution.py:516
  6.6 25.8 %collective-permute-start = (f32[8,8,128]{2,1,0:T(8,128)S(1)}, f32[8,8,128]{2,1,0:T(8,128)S(1)}, u32[]{:S(2)}, u32[]{:S(2)}) collective-permute-start(f32[8,8,128]{2,1,0:T(8,128)S(1)} %get-tuple-element.21), channel_id=1, source_target_pairs={{0,1},{1,2},{2,3},{3,4},{4,5},{5,6},{6,7},{7,0},{8,9},{9,10},{10,1... | collective-permute-start | bytes 98312 | tf_op jit(solution)/shard_map/ppermute | solution.py:510
  11.7 20.7 %collective-permute-start.4 = (f32[32,8,128]{2,1,0:T(8,128)S(1)}, f32[32,8,128]{2,1,0:T(8,128)S(1)}, u32[]{:S(2)}, u32[]{:S(2)}) collective-permute-start(f32[32,8,128]{2,1,0:T(8,128)S(1)} %constant_dynamic-update-slice_fusion), channel_id=1, source_target_pairs={{0,6},{1,7},{2,0},{3,1},{4,2},{5,3},{6,4},{7,5},{8,14},{9,15},{10,... | collective-permute-start | bytes 393224 | tf_op jit(solution)/shard_map/ppermute | solution.py:510
  15.3 17.1 %collective-permute-start.3 = (f32[32,8,128]{2,1,0:T(8,128)S(1)}, f32[32,8,128]{2,1,0:T(8,128)S(1)}, u32[]{:S(2)}, u32[]{:S(2)}) collective-permute-start(f32[32,8,128]{2,1,0:T(8,128)S(1)} %constant_dynamic-update-slice_fusion), channel_id=1, source_target_pairs={{0,2},{1,3},{2,4},{3,5},{4,6},{5,7},{6,0},{7,1},{8,10},{9,11},{10,... | collective-permute-start | bytes 393224 | tf_op jit(solution)/shard_map/ppermute | solution.py:510
  17.7 0.7 copy-start.6
  45.5 5.3 %collective-permute-start.6 = (f32[32,128]{1,0:T(8,128)S(1)}, f32[32,128]{1,0:T(8,128)S(1)}, u32[]{:S(2)}, u32[]{:S(2)}) collective-permute-start(f32[32,128]{1,0:T(8,128)S(1)} %get-tuple-element.26), channel_id=1, source_target_pairs={{0,6},{1,7},{2,0},{3,1},{4,2},{5,3},{6,4},{7,5},{8,14},{9,15},{10,... | collective-permute-start | bytes 49160 | tf_op jit(solution)/shard_map/ppermute | solution.py:510
  49.4 5.5 %collective-permute-start.7 = (f32[32,128]{1,0:T(8,128)S(1)}, f32[32,128]{1,0:T(8,128)S(1)}, u32[]{:S(2)}, u32[]{:S(2)}) collective-permute-start(f32[32,128]{1,0:T(8,128)S(1)} %get-tuple-element.27), channel_id=1, source_target_pairs={{0,2},{1,3},{2,4},{3,5},{4,6},{5,7},{6,0},{7,1},{8,10},{9,11},{10,... | collective-permute-start | bytes 49160 | tf_op jit(solution)/shard_map/ppermute | solution.py:510
  49.4 5.5 %collective-permute-start.8 = (f32[16,128]{1,0:T(8,128)S(1)}, f32[16,128]{1,0:T(8,128)S(1)}, u32[]{:S(2)}, u32[]{:S(2)}) collective-permute-start(f32[16,128]{1,0:T(8,128)S(1)} %get-tuple-element.28), channel_id=1, source_target_pairs={{0,8},{1,9},{2,10},{3,11},{4,12},{5,13},{6,14},{7,15},{8,16},{9,17... | collective-permute-start | bytes 24584 | tf_op jit(solution)/shard_map/ppermute | solution.py:516
  54.9 2.9 %collective-permute-start.9 = (f32[32,128]{1,0:T(8,128)S(1)}, f32[32,128]{1,0:T(8,128)S(1)}, u32[]{:S(2)}, u32[]{:S(2)}) collective-permute-start(f32[32,128]{1,0:T(8,128)S(1)} %pad_maximum_fusion), channel_id=1, source_target_pairs={{0,1},{1,0},{2,3},{3,2},{4,5},{5,4},{6,7},{7,6},{8,9},{9,8},{10,11... | collective-permute-start | bytes 49160 | tf_op jit(solution)/shard_map/ppermute | solution.py:513
  55.0 4.2 %collective-permute-start.5 = (f32[8,128]{1,0:T(8,128)S(1)}, f32[8,128]{1,0:T(8,128)S(1)}, u32[]{:S(2)}, u32[]{:S(2)}) collective-permute-start(f32[8,128]{1,0:T(8,128)S(1)} %get-tuple-element.24), channel_id=1, source_target_pairs={{0,7},{1,0},{2,1},{3,2},{4,3},{5,4},{6,5},{7,6},{8,15},{9,8},{10,9... | collective-permute-start | bytes 12296 | tf_op jit(solution)/shard_map/ppermute | solution.py:510
  57.9 5.2 %collective-permute-start.10 = (f32[16,128]{1,0:T(8,128)S(1)}, f32[16,128]{1,0:T(8,128)S(1)}, u32[]{:S(2)}, u32[]{:S(2)}) collective-permute-start(f32[16,128]{1,0:T(8,128)S(1)} %slice.40), channel_id=1, source_target_pairs={{0,24},{1,25},{2,26},{3,27},{4,28},{5,29},{6,30},{7,31},{8,0},{9,1... | collective-permute-start | bytes 24584 | tf_op jit(solution)/shard_map/ppermute | solution.py:516
  59.2 4.8 %collective-permute-start.11 = (f32[8,128]{1,0:T(8,128)S(1)}, f32[8,128]{1,0:T(8,128)S(1)}, u32[]{:S(2)}, u32[]{:S(2)}) collective-permute-start(f32[8,128]{1,0:T(8,128)S(1)} %get-tuple-element.34), channel_id=1, source_target_pairs={{0,1},{1,2},{2,3},{3,4},{4,5},{5,6},{6,7},{7,0},{8,9},{9,10},{10,1... | collective-permute-start | bytes 12296 | tf_op jit(solution)/shard_map/ppermute | solution.py:510
  59.2 5.3 %collective-permute-start.13 = (f32[32,128]{1,0:T(8,128)S(1)}, f32[32,128]{1,0:T(8,128)S(1)}, u32[]{:S(2)}, u32[]{:S(2)}) collective-permute-start(f32[32,128]{1,0:T(8,128)S(1)} %maximum_add_fusion.pair_rho), channel_id=1, source_target_pairs={{0,6},{1,7},{2,0},{3,1},{4,2},{5,3},{6,4},{7,5},{8,14},{9,15},{10,... | collective-permute-start | bytes 49160 | tf_op jit(solution)/shard_map/ppermute | solution.py:510
  63.1 5.5 %collective-permute-start.12 = (f32[32,128]{1,0:T(8,128)S(1)}, f32[32,128]{1,0:T(8,128)S(1)}, u32[]{:S(2)}, u32[]{:S(2)}) collective-permute-start(f32[32,128]{1,0:T(8,128)S(1)} %maximum_add_fusion.pair_rho), channel_id=1, source_target_pairs={{0,2},{1,3},{2,4},{3,5},{4,6},{5,7},{6,0},{7,1},{8,10},{9,11},{10,... | collective-permute-start | bytes 49160 | tf_op jit(solution)/shard_map/ppermute | solution.py:510
  63.1 45.8 %copy-start.1 = (f32[3,4096]{1,0:T(4,128)S(1)}, f32[3,4096]{1,0:T(4,128)}, u32[]{:S(2)}) copy-start(f32[3,4096]{1,0:T(4,128)} %pos.3) | copy-start | bytes 147460
  63.1 45.8 %copy-start.3 = (f32[3,4096]{1,0:T(4,128)S(1)}, f32[3,4096]{1,0:T(4,128)}, u32[]{:S(2)}) copy-start(f32[3,4096]{1,0:T(4,128)} %vel.3) | copy-start | bytes 147460
  88.7 4.3 %collective-permute-start.15 = (f32[3,32,128]{2,1,0:T(8,128)S(1)}, f32[3,32,128]{2,1,0:T(8,128)S(1)}, u32[]{:S(2)}, u32[]{:S(2)}) collective-permute-start(f32[3,32,128]{2,1,0:T(8,128)S(1)} %get-tuple-element.32), channel_id=1, source_target_pairs={{0,6},{1,7},{2,0},{3,1},{4,2},{5,3},{6,4},{7,5},{8,14},{9,15},{10,... | collective-permute-start | bytes 147464 | tf_op jit(solution)/shard_map/ppermute | solution.py:510
  88.9 5.9 %collective-permute-start.16 = (f32[3,32,128]{2,1,0:T(8,128)S(1)}, f32[3,32,128]{2,1,0:T(8,128)S(1)}, u32[]{:S(2)}, u32[]{:S(2)}) collective-permute-start(f32[3,32,128]{2,1,0:T(8,128)S(1)} %get-tuple-element.33), channel_id=1, source_target_pairs={{0,2},{1,3},{2,4},{3,5},{4,6},{5,7},{6,0},{7,1},{8,10},{9,11},{10,... | collective-permute-start | bytes 147464 | tf_op jit(solution)/shard_map/ppermute | solution.py:510
  94.8 1.3 %collective-permute-start.17 = (f32[3,16,128]{2,1,0:T(8,128)S(1)}, f32[3,16,128]{2,1,0:T(8,128)S(1)}, u32[]{:S(2)}, u32[]{:S(2)}) collective-permute-start(f32[3,16,128]{2,1,0:T(8,128)S(1)} %slice.42), channel_id=1, source_target_pairs={{0,1},{1,0},{2,3},{3,2},{4,5},{5,4},{6,7},{7,6},{8,9},{9,8},{10,11... | collective-permute-start | bytes 73736 | tf_op jit(solution)/shard_map/ppermute | solution.py:513
  94.9 14.0 %collective-permute-start.14 = (f32[3,8,128]{2,1,0:T(8,128)S(1)}, f32[3,8,128]{2,1,0:T(8,128)S(1)}, u32[]{:S(2)}, u32[]{:S(2)}) collective-permute-start(f32[3,8,128]{2,1,0:T(8,128)S(1)} %get-tuple-element.30), channel_id=1, source_target_pairs={{0,7},{1,0},{2,1},{3,2},{4,3},{5,4},{6,5},{7,6},{8,15},{9,8},{10,9... | collective-permute-start | bytes 36872 | tf_op jit(solution)/shard_map/ppermute | solution.py:510
  96.1 12.9 %collective-permute-start.18 = (f32[3,16,128]{2,1,0:T(8,128)S(1)}, f32[3,16,128]{2,1,0:T(8,128)S(1)}, u32[]{:S(2)}, u32[]{:S(2)}) collective-permute-start(f32[3,16,128]{2,1,0:T(8,128)S(1)} %slice_add_fusion), channel_id=1, source_target_pairs={{0,24},{1,25},{2,26},{3,27},{4,28},{5,29},{6,30},{7,31},{8,0},{9,1... | collective-permute-start | bytes 73736 | tf_op jit(solution)/shard_map/ppermute | solution.py:516

commit v3 on v2

v3 whole, which is shorter than its diff:
```python
import functools
import math

import jax
import jax.numpy as jnp
from jax import lax
from jax.experimental import pallas as pl
from jax.experimental.pallas import tpu as pltpu
from jax.sharding import PartitionSpec as P

cutoff_density = 0.75
density_norm = 15.0 / (2.0 * math.pi * cutoff_density**3)
repulse = 25.0
friction = 4.5
time_step = 0.01
distance_floor = 0.01
far_away = 10000.0
density_scale = density_norm / (cutoff_density * cutoff_density)
crowd_scale = repulse / cutoff_density
VMEM = pl.BlockSpec(memory_space=pltpu.VMEM)
SMEM = pl.BlockSpec(memory_space=pltpu.SMEM)
HBM = pl.BlockSpec(memory_space=pltpu.HBM)
f32 = jnp.float32


def sds(*shape):
    return jax.ShapeDtypeStruct(shape, f32)


def params():
    return pltpu.CompilerParams(vmem_limit_bytes=32 * 1024 * 1024)


def fetch(sems, *copies):
    started = [pltpu.make_async_copy(a, b, sems.at[i]) for i, (a, b) in enumerate(copies)]
    for copy in started:
        copy.start()

    def wait():
        for copy in started:
            copy.wait()

    return wait


def pack_kernel(
    pos_hbm, vel_hbm, typ_hbm, counts_hbm, send_hbm, out, top, face, pos, vel, typ, counts, send, sems
):
    fetch(
        sems, (pos_hbm, pos), (vel_hbm, vel), (typ_hbm, typ), (counts_hbm, counts), (send_hbm, send)
    )()
    tiles = out.shape[0]
    width = out.shape[2]
    lane = lax.broadcasted_iota(jnp.int32, (1, width), 1)
    upper = top.shape[0]
    offsets, cap = send.shape[0], send.shape[2]
    for g in range(tiles):
        cols = pl.ds(g * width, width)
        live = lane < counts[g]
        for c in range(3):
            out[g, pl.ds(c, 1), :] = jnp.where(live, pos[pl.ds(c, 1), cols], far_away)
            out[g, pl.ds(3 + c, 1), :] = vel[pl.ds(c, 1), cols]
        out[g, pl.ds(6, 1), :] = typ[pl.ds(g, 1), :].astype(f32)
        meta = jnp.full((1, width), counts[g], jnp.int32)
        o = g - (tiles - upper)
        if 0 <= o < offsets:
            for c in range(cap):
                meta = jnp.where(lane == c, send[o, 0, c], meta)
        out[g, pl.ds(7, 1), :] = meta.astype(f32)
    top[...] = out[pl.ds(tiles - upper, upper)]
    face[...] = out[pl.ds(0, face.shape[0])]


def diagonal(width):
    lane = lax.broadcasted_iota(jnp.int32, (8, width), 1)
    return lane - lax.broadcasted_iota(jnp.int32, (8, width), 0)


def spread_row(row, store):
    width = row.shape[1]
    diff = diagonal(width)
    row = jnp.broadcast_to(row, (8, width))
    for r in range(0, width, 8):
        one = jnp.sum(jnp.where(diff == r, row, 0.0), axis=1, keepdims=True)
        store(r, jnp.broadcast_to(one, (8, width)))


def row_sums(acc, *at):
    width = acc.shape[-1]
    diff = diagonal(width)
    out = jnp.zeros((8, width), f32)
    for r in range(0, width, 8):
        out = jnp.where(diff == r, jnp.sum(acc[*at, pl.ds(r, 8), :], axis=1, keepdims=True), out)
    return out


def by_fours(tiles, body):
    def step(i, carry):
        for t in range(4):
            body(4 * i + t)
        return carry

    lax.fori_loop(0, tiles // 4, step, 0)


def fold(ref, first, *at):
    width = ref.shape[-1]
    sub = lax.broadcasted_iota(jnp.int32, (8, width), 0)
    parts = [ref[*at, first + t] for t in range(8)]
    for step in (4, 2, 1):
        low = sub % (2 * step) < step
        parts = [
            jnp.where(low, a, b) + pltpu.roll(jnp.where(low, b, a), step, 0)
            if step == 4
            else jnp.where(low, a, b)
            + jnp.where(
                low,
                pltpu.roll(jnp.where(low, b, a), 8 - step, 0),
                pltpu.roll(jnp.where(low, b, a), step, 0),
            )
            for a, b in zip(parts[:step], parts[step:])
        ]
    return parts[0]


def branch(used, count, width, body):
    sizes = (0,) + tuple(width * e // 8 for e in (4, 6, 8))
    index = jnp.where(used, 1, 0)
    for n in sizes[1:-1]:
        index += jnp.where(used & (count > n), 1, 0)

    def pick(low, high):
        if low == high:
            body(sizes[low])
            return
        middle = (low + high) // 2

        @pl.when(index <= middle)
        def _():
            pick(low, middle)

        @pl.when(index > middle)
        def _():
            pick(middle + 1, high)

    pick(0, len(sizes) - 1)


def tile_loop(tiles, width, counts, slots, partner, pair):
    def step(g, carry):
        count = counts[g]
        listed = [partner(g, k) for k in range(slots)]
        for k, (h, used) in enumerate(listed):

            def body(n, k=k, h=h):
                if n:
                    pair(g, k, h, n)

            branch(used & (count > 0), count, width, body)
        return carry

    lax.fori_loop(0, tiles, step, 0)


def column(ref, h, c):
    return jnp.broadcast_to(ref[h, pl.ds(c, 1), :], (8, ref.shape[2]))


def density_pair(mine, union, h, n, acc_cols, acc_rows, g):
    other = [column(union, h, c) for c in range(3)]
    total = None
    for r in range(0, n, 8):
        d = [mine(c, r) - other[c] for c in range(3)]
        d2 = jnp.maximum(d[0] * d[0] + d[1] * d[1] + d[2] * d[2], distance_floor)
        w = jnp.maximum(cutoff_density - d2 * lax.rsqrt(d2), 0.0)
        w = w * w
        total = w if total is None else total + w
        if acc_rows is not None:
            acc_rows[g, pl.ds(r, 8), :] += w
    acc_cols[h] += total


def force_pair(mine, union, h, n, table, acc_cols, acc_rows, g):
    a00, a01, a11 = table
    other = [column(union, h, c) for c in range(8)]
    first = a00 + other[6] * (a01 - a00)
    slope = (a01 + other[6] * (a11 - a01)) - first
    total = [None] * 3
    for r in range(0, n, 8):
        d = [mine(c, r) - other[c] for c in range(3)]
        d2 = jnp.maximum(d[0] * d[0] + d[1] * d[1] + d[2] * d[2], distance_floor)
        inverse = lax.rsqrt(d2)
        dist = d2 * inverse
        wc = jnp.maximum(1.0 - dist, 0.0)
        wd = jnp.maximum(cutoff_density - dist, 0.0)
        dv = [mine(3 + c, r) - other[3 + c] for c in range(3)]
        approach = (d[0] * dv[0] + d[1] * dv[1] + d[2] * dv[2]) * inverse
        scalar = (first + mine(6, r) * slope) - approach * wc
        scalar = scalar * wc + (mine(7, r) + other[7]) * wd
        scalar = scalar * inverse
        for c in range(3):
            push = d[c] * scalar
            total[c] = push if total[c] is None else total[c] + push
            if acc_rows is not None:
                acc_rows[c, g, pl.ds(r, 8), :] += push
    for c in range(3):
        acc_cols[c, h] -= total[c]


def zero(*refs):
    for ref in refs:
        ref[...] = jnp.zeros_like(ref)


def spread_kernel(union, spread):
    tiles = union.shape[0]

    def fill(g):
        for c in range(spread.shape[1]):

            def store(r, value, c=c):
                spread[g, c, pl.ds(r, 8), :] = value

            row = union[g, pl.ds(c, 1), :]
            spread_row(row * friction if 3 <= c < 6 else row, store)

    by_fours(tiles, fill)


def local_partner(counts, nbr):
    def partner(g, k):
        if k == 0:
            return g, True
        h = nbr[k - 1, g]
        return jnp.maximum(h, 0), (h >= 0) & (counts[jnp.maximum(h, 0)] > 0)

    return partner


def local_density_kernel(counts_hbm, nbr_hbm, union, spread, acc, sums, counts, nbr, sems):
    wait = fetch(sems, (counts_hbm, counts), (nbr_hbm, nbr))
    tiles, width = union.shape[0], union.shape[2]
    zero(sums)
    wait()
    self_term = (cutoff_density - math.sqrt(distance_floor)) ** 2
    lane = lax.broadcasted_iota(jnp.int32, (8, width), 1)
    sub = lax.broadcasted_iota(jnp.int32, (8, width), 0)
    for g in range(tiles):
        acc[g] = jnp.where((lane < counts[g]) & (sub == 0), -self_term, 0.0)

    def pair(g, k, h, n):
        mine = lambda c, r: spread[g, c, pl.ds(r, 8), :]
        density_pair(mine, union, h, n, acc, sums if k else None, g)

    tile_loop(tiles, width, counts, 1 + nbr.shape[0], local_partner(counts, nbr), pair)


def gather_ghosts(ghosts, face, near, flip, below, above):
    at = 0
    for ref in (face, near, flip, below, above):
        ghosts[pl.ds(at, ref.shape[0])] = ref[...]
        at += ref.shape[0]


def ghost_meta(ghosts, meta, meta_smem, sem):
    total = ghosts.shape[0]
    for t in range(total):
        meta[pl.ds(t, 1), :] = ghosts[t, pl.ds(7, 1), :].astype(jnp.int32)
    copy = pltpu.make_async_copy(meta, meta_smem, sem)
    copy.start()
    return copy.wait


def ghost_partner(k, g, face_nbr, cross_pair, where, meta, faces, upper, cap, reach):
    columns = face_nbr.shape[0]
    if k < columns:
        f = face_nbr[k, g]
        h = jnp.maximum(f, 0)
        return h, (f >= 0) & (meta[h, meta.shape[1] - 1] > 0)
    s = cross_pair[k - columns, g]
    layer, core = where[0], where[1]
    slot = jnp.maximum(s, 0)
    o = slot // cap
    c = slot - o * cap
    place = core - o + 2 * reach
    hop = place // 2 - 1
    flipped = jnp.where(lax.rem(place, 2) == core, 0, 1)
    hops = jnp.where(hop == 0, 0, jnp.where(hop < 0, 1, 2))
    base = faces + (hops * 2 + flipped) * upper
    u = meta[base + o, c]
    h = base + jnp.maximum(u, 0)
    return h, (s >= 0) & (layer > 0) & (u >= 0) & (meta[h, meta.shape[1] - 1] > 0)


def ghost_density_kernel(
    faces,
    upper,
    cap,
    reach,
    where,
    counts_hbm,
    face_nbr_hbm,
    cross_pair_hbm,
    spread,
    local_acc,
    local_sums,
    face,
    near,
    flip,
    below,
    above,
    own_out,
    top_out,
    face_out,
    pair_out,
    below_out,
    above_out,
    sums,
    ghosts,
    acc,
    reduced,
    counts,
    face_nbr,
    cross_pair,
    meta,
    meta_smem,
    sems,
    sem,
):
    wait = fetch(
        sems, (counts_hbm, counts), (face_nbr_hbm, face_nbr), (cross_pair_hbm, cross_pair)
    )
    tiles, width = spread.shape[0], spread.shape[2]
    gather_ghosts(ghosts, face, near, flip, below, above)
    wait_meta = ghost_meta(ghosts, meta, meta_smem, sem)
    zero(acc)
    wait()
    wait_meta()

    def partner(g, k):
        return ghost_partner(
            k, g, face_nbr, cross_pair, where, meta_smem, faces, upper, cap, reach
        )

    def pair(g, k, h, n):
        mine = lambda c, r: spread[g, c, pl.ds(r, 8), :]
        density_pair(mine, ghosts, h, n, acc, sums, g)

    slots = face_nbr.shape[0] + cross_pair.shape[0]
    tile_loop(tiles, width, counts, slots, partner, pair)
    for t in range(0, acc.shape[0], 8):
        reduced[pl.ds(t, 8), :] = fold(acc, t)
    face_out[...] = reduced[pl.ds(0, faces)]
    pair_out[...] = reduced[pl.ds(faces, 2 * upper)]
    below_out[...] = reduced[pl.ds(faces + 2 * upper, 2 * upper)]
    above_out[...] = reduced[pl.ds(faces + 4 * upper, 2 * upper)]

    def collect(t):
        acc[t] = local_acc[t] + row_sums(sums, t)

    by_fours(tiles, collect)
    for t in range(0, tiles, 8):
        own_out[pl.ds(t, 8), :] = fold(acc, t)
    top_out[...] = own_out[pl.ds(tiles - upper, upper)]


def force_tile(union, density, t):
    tile = union[t]
    channel = lax.broadcasted_iota(jnp.int32, tile.shape, 0)
    tile = jnp.where((channel >= 3) & (channel < 6), tile * friction, tile)
    return jnp.where(channel == 7, density * (crowd_scale * density_scale), tile)


def amplitudes(a_table):
    return (a_table[0, 0], 0.5 * (a_table[0, 1] + a_table[1, 0]), a_table[1, 1])


def force_mine(spread, crowd, g):
    def mine(c, r):
        return crowd[g, pl.ds(r, 8), :] if c == 7 else spread[g, c, pl.ds(r, 8), :]

    return mine


def local_force_kernel(
    counts_hbm,
    nbr_hbm,
    a_table,
    union,
    spread,
    crowd,
    density,
    acc,
    beads,
    sums,
    counts,
    nbr,
    sems,
):
    wait = fetch(sems, (counts_hbm, counts), (nbr_hbm, nbr))
    tiles, width = union.shape[0], union.shape[2]
    table = amplitudes(a_table)
    zero(acc, sums)
    for t in range(tiles):
        beads[t] = force_tile(union, density[pl.ds(t, 1), :], t)
    wait()

    def pair(g, k, h, n):
        force_pair(force_mine(spread, crowd, g), beads, h, n, table, acc, sums if k else None, g)

    tile_loop(tiles, width, counts, 1 + nbr.shape[0], local_partner(counts, nbr), pair)

    def collect(t):
        for c in range(3):
            acc[c, t] += row_sums(sums, c, t)

    by_fours(tiles, collect)


def ghost_force_kernel(
    faces,
    upper,
    cap,
    reach,
    where,
    counts_hbm,
    face_nbr_hbm,
    cross_pair_hbm,
    a_table,
    union,
    spread,
    density,
    face,
    near,
    flip,
    below,
    above,
    face_rho,
    pair_rho,
    below_rho,
    above_rho,
    own_out,
    crowd,
    face_out,
    pair_out,
    below_out,
    above_out,
    ghosts,
    acc,
    rho,
    sums,
    reduced,
    counts,
    face_nbr,
    cross_pair,
    meta,
    meta_smem,
    sems,
    sem,
):
    wait = fetch(
        sems, (counts_hbm, counts), (face_nbr_hbm, face_nbr), (cross_pair_hbm, cross_pair)
    )
    tiles, width = union.shape[0], union.shape[2]
    gather_ghosts(ghosts, face, near, flip, below, above)
    wait_meta = ghost_meta(ghosts, meta, meta_smem, sem)
    zero(acc, sums)
    table = amplitudes(a_table)
    at = 0
    for ref in (face_rho, pair_rho, below_rho, above_rho):
        rho[pl.ds(at, ref.shape[0]), :] = ref[...]
        at += ref.shape[0]
    for t in range(ghosts.shape[0]):
        ghosts[t] = force_tile(ghosts, rho[pl.ds(t, 1), :], t)

    def fill(g):
        def store(r, value):
            crowd[g, pl.ds(r, 8), :] = value

        spread_row(density[pl.ds(g, 1), :] * (crowd_scale * density_scale), store)

    by_fours(tiles, fill)
    wait()
    wait_meta()

    def partner(g, k):
        return ghost_partner(
            k, g, face_nbr, cross_pair, where, meta_smem, faces, upper, cap, reach
        )

    def pair(g, k, h, n):
        force_pair(force_mine(spread, crowd, g), ghosts, h, n, table, acc, sums, g)

    slots = face_nbr.shape[0] + cross_pair.shape[0]
    tile_loop(tiles, width, counts, slots, partner, pair)
    for c in range(3):
        for t in range(0, acc.shape[1], 8):
            reduced[pl.ds(t, 8), :] = fold(acc, t, c)
        face_out[c] = reduced[pl.ds(0, faces)]
        pair_out[c] = reduced[pl.ds(faces, 2 * upper)]
        below_out[c] = reduced[pl.ds(faces + 2 * upper, 2 * upper)]
        above_out[c] = reduced[pl.ds(faces + 4 * upper, 2 * upper)]

    def collect(t):
        for c in range(3):
            own_out[c, t] = row_sums(sums, c, t)

    by_fours(tiles, collect)


def finish_kernel(counts, pos, vel, local_acc, ghost_acc, face_back, top_back, pos_out, vel_out, force):
    tiles, width = local_acc.shape[1], local_acc.shape[3]
    faces, upper = face_back.shape[1], top_back.shape[1]
    lane = lax.broadcasted_iota(jnp.int32, (1, width), 1)

    def add(t):
        for c in range(3):
            force[c, t] = local_acc[c, t] + ghost_acc[c, t]

    for t in range(tiles):
        add(t)
    for c in range(3):
        for t in range(0, tiles, 8):
            total = fold(force, t, c)
            if t < faces:
                total = total + face_back[c, pl.ds(t, 8), :]
            if t >= tiles - upper:
                total = total + top_back[c, pl.ds(t - (tiles - upper), 8), :]
            for i in range(8):
                g = t + i
                cols = pl.ds(g * width, width)
                live = lane < counts[g]
                speed = vel[pl.ds(c, 1), cols] + time_step * total[i : i + 1]
                speed = jnp.where(live, speed, 0.0)
                vel_out[pl.ds(c, 1), cols] = speed
                place = jnp.where(live, pos[pl.ds(c, 1), cols] + time_step * speed, 0.0)
                pos_out[pl.ds(c, 1), cols] = place


def on_device(
    layers,
    places,
    positions,
    velocities,
    types,
    counts,
    a_table,
    local_nbr,
    face_nbr,
    cross_send,
    cross_pair,
):
    tiles = counts.shape[0]
    width = positions.shape[1] // tiles
    faces, upper = tiles // 4, tiles // 2
    offsets, cap = cross_send.shape[1], cross_send.shape[2]
    reach = offsets // 2
    total = faces + 6 * upper
    both = ("layer", "lat")

    def lateral(value, by):
        return lax.ppermute(value, "lat", [(m, (m + by) % places) for m in range(places)])

    def swap(value):
        return lax.ppermute(value, "lat", [(m, m ^ 1) for m in range(places)])

    def climb(value, by, flip=0):
        return lax.ppermute(
            value,
            both,
            [
                (l * places + m, ((l + by) % layers) * places + (m ^ flip))
                for l in range(layers)
                for m in range(places)
            ],
        )

    kinds = types.reshape(tiles, width)
    local_nbr, face_nbr, cross_pair = local_nbr.T, face_nbr.T, cross_pair.T
    send = cross_send.transpose(1, 0, 2)
    ints = jnp.int32
    counts_smem = pltpu.SMEM((tiles,), ints)
    payload, top, face = pl.pallas_call(
        pack_kernel,
        out_shape=(sds(tiles, 8, width), sds(upper, 8, width), sds(faces, 8, width)),
        in_specs=[HBM] * 5,
        out_specs=[VMEM] * 3,
        scratch_shapes=[
            pltpu.VMEM(positions.shape, f32),
            pltpu.VMEM(velocities.shape, f32),
            pltpu.VMEM(kinds.shape, ints),
            counts_smem,
            pltpu.SMEM(send.shape, ints),
            pltpu.SemaphoreType.DMA((5,)),
        ],
        compiler_params=params(),
    )(positions, velocities, kinds, counts, send)
    spread = pl.pallas_call(
        spread_kernel,
        out_shape=sds(tiles, 7, width, width),
        in_specs=[VMEM],
        out_specs=VMEM,
        cost_estimate=pl.CostEstimate(flops=10**9, bytes_accessed=15 * 10**6, transcendentals=0),
        compiler_params=params(),
    )(payload)
    near = climb(top, 1)
    flip = climb(top, 1, 1)
    face_ghosts = lateral(face, 1)
    chip_ghosts = jnp.concatenate([near, flip], axis=0)
    below = lateral(chip_ghosts, 2)
    above = lateral(chip_ghosts, -2)
    where = jnp.stack([lax.axis_index("layer"), lax.axis_index("lat") % 2]).astype(jnp.int32)

    local_acc, local_sums = pl.pallas_call(
        local_density_kernel,
        out_shape=(sds(tiles, 8, width), sds(tiles, width, width)),
        in_specs=[HBM, HBM, VMEM, VMEM],
        out_specs=[VMEM] * 2,
        scratch_shapes=[
            counts_smem,
            pltpu.SMEM(local_nbr.shape, ints),
            pltpu.SemaphoreType.DMA((2,)),
        ],
        cost_estimate=pl.CostEstimate(flops=10**9, bytes_accessed=15 * 10**6, transcendentals=0),
        compiler_params=params(),
    )(counts, local_nbr, payload, spread)

    sizes = (faces, upper, cap, reach)
    tables = [
        counts_smem,
        pltpu.SMEM(face_nbr.shape, ints),
        pltpu.SMEM(cross_pair.shape, ints),
        pltpu.VMEM((total, width), ints),
        pltpu.SMEM((total, width), ints),
        pltpu.SemaphoreType.DMA((3,)),
        pltpu.SemaphoreType.DMA,
    ]
    own, own_top, face_part, pair_part, below_part, above_part, _ = pl.pallas_call(
        functools.partial(ghost_density_kernel, *sizes),
        out_shape=(
            sds(tiles, width),
            sds(upper, width),
            sds(faces, width),
            sds(2 * upper, width),
            sds(2 * upper, width),
            sds(2 * upper, width),
            sds(tiles, width, width),
        ),
        in_specs=[SMEM] + [HBM] * 3 + [VMEM] * 8,
        out_specs=[VMEM] * 7,
        scratch_shapes=[
            pltpu.VMEM((total, 8, width), f32),
            pltpu.VMEM((total, 8, width), f32),
            pltpu.VMEM((total, width), f32),
        ]
        + tables,
        input_output_aliases={6: 6},
        compiler_params=params(),
    )(
        where,
        counts,
        face_nbr,
        cross_pair,
        spread,
        local_acc,
        local_sums,
        face_ghosts,
        near,
        flip,
        below,
        above,
    )

    owner_part = climb(own_top, 1)
    from_above = lateral(below_part, -2)
    from_below = lateral(above_part, 2)
    face_back = lateral(face_part, -1)
    met = pair_part + from_above + from_below
    met = jnp.concatenate([met[:upper] + owner_part, met[upper:]], axis=0)
    other = swap(met)
    pair_rho = met + jnp.concatenate([other[upper:], other[:upper]], axis=0)
    top_rho = climb(pair_rho[:upper], -1)
    below_rho = lateral(pair_rho, 2)
    above_rho = lateral(pair_rho, -2)
    bottom_rho = own[:faces] + face_back
    face_rho = lateral(bottom_rho, 1)
    density = jnp.concatenate([bottom_rho, own[faces : tiles - upper], top_rho], axis=0)

    ghost_acc, crowd, face_force, pair_force, below_force, above_force = pl.pallas_call(
        functools.partial(ghost_force_kernel, *sizes),
        out_shape=(
            sds(3, tiles, 8, width),
            sds(tiles, width, width),
            sds(3, faces, width),
            sds(3, 2 * upper, width),
            sds(3, 2 * upper, width),
            sds(3, 2 * upper, width),
        ),
        in_specs=[SMEM] + [HBM] * 3 + [SMEM] + [VMEM] * 12,
        out_specs=[VMEM] * 6,
        scratch_shapes=[
            pltpu.VMEM((total, 8, width), f32),
            pltpu.VMEM((3, total, 8, width), f32),
            pltpu.VMEM((total, width), f32),
            pltpu.VMEM((3, tiles, width, width), f32),
            pltpu.VMEM((total, width), f32),
        ]
        + tables,
        compiler_params=params(),
    )(
        where,
        counts,
        face_nbr,
        cross_pair,
        a_table,
        payload,
        spread,
        density,
        face_ghosts,
        near,
        flip,
        below,
        above,
        face_rho,
        pair_rho,
        below_rho,
        above_rho,
    )

    force_face = lateral(face_force, -1)
    force_met = pair_force + lateral(below_force, -2) + lateral(above_force, 2)
    force_other = swap(force_met[:, upper:])
    force_top = climb(force_met[:, :upper] + force_other, -1)

    local_force = pl.pallas_call(
        local_force_kernel,
        out_shape=sds(3, tiles, 8, width),
        in_specs=[HBM, HBM, SMEM] + [VMEM] * 4,
        out_specs=VMEM,
        scratch_shapes=[
            pltpu.VMEM((tiles, 8, width), f32),
            pltpu.VMEM((3, tiles, width, width), f32),
            counts_smem,
            pltpu.SMEM(local_nbr.shape, ints),
            pltpu.SemaphoreType.DMA((2,)),
        ],
        cost_estimate=pl.CostEstimate(flops=2 * 10**9, bytes_accessed=20 * 10**6, transcendentals=0),
        compiler_params=params(),
    )(counts, local_nbr, a_table, payload, spread, crowd, density)

    return pl.pallas_call(
        finish_kernel,
        out_shape=(sds(*positions.shape), sds(*velocities.shape)),
        in_specs=[SMEM] + [VMEM] * 6,
        out_specs=[VMEM] * 2,
        scratch_shapes=[pltpu.VMEM((3, tiles, 8, width), f32)],
        compiler_params=params(),
    )(counts, positions, velocities, local_force, ghost_acc, force_face, force_top)


def solution(mesh):
    placed = (
        P(None, ("layer", "lat")),
        P(None, ("layer", "lat")),
        P(("layer", "lat")),
        P(("layer", "lat")),
        P(),
        P(("layer", "lat"), None),
        P(("layer", "lat"), None),
        P(("layer", "lat"), None, None),
        P(("layer", "lat"), None),
    )
    return jax.shard_map(
        functools.partial(on_device, mesh.shape["layer"], mesh.shape["lat"]),
        mesh=mesh,
        in_specs=placed,
        out_specs=(P(None, ("layer", "lat")), P(None, ("layer", "lat"))),
        check_vma=False,
    )
```

time: 112 us -> 95.9 us (0.86); the launches traced: 110 us -> 95.6 us
  Pallas kernels: 62.2 us -> 50.3 us
  local copies, waits for them, and re-layouts: 6.71 us -> 3.79 us
    pallas_call x1, Pallas kernels: 14.1 us -> 5.29 us  [on_device(): pl.pallas_call(local_density_kernel, out_shape=(sds(tiles, 8, width), sds...]
    pallas_call x0 -> x1, Pallas kernels: none -> 4.38 us  [on_device(): pl.pallas_call(spread_kernel, out_shape=sds(tiles, 7, width, width), in_s...]
    pallas_call x1, Pallas kernels: 20.1 us -> 16.4 us  [on_device(): pl.pallas_call(functools.partial(ghost_force_kernel, *sizes), out_shape=(...]
    unnamed x21 -> x25, local copies, waits for them, and re-layouts: 6.69 us -> 3.77 us
    pallas_call x1, Pallas kernels: 13 us -> 10.6 us  [on_device(): pl.pallas_call(functools.partial(ghost_density_kernel, *sizes), out_shape...]
    pallas_call x1, Pallas kernels: 12.8 us -> 11.3 us  [on_device(): pl.pallas_call(local_force_kernel, out_shape=sds(3, tiles, 8, width), in_...]
  transfers between devices with their start and end apart: 19 -> 19, of which waited for: 11 -> 10; matrix products, arithmetic and copies ran while one was open for 2% -> 0% of each run, Pallas kernels for 24% -> 22%
where the time goes in v3:
time: 95.9 us; the launch traced here: 95.6 us
  Pallas kernels  50.3 us (52%)
  waiting for transfers between devices  22.4 us (23%)
  starting transfers between devices  18.2 us (19%)
  local copies, waits for them, and re-layouts  3.79 us (4%)
    pallas_call x1, Pallas kernels, on_device(): pl.pallas_call(functools.partial(ghost_force_kernel, *sizes), out_shape=(...  16.4 us
    ppermute x12, starting transfers between devices, lateral(): lax.ppermute(value, 'lat', [(m, (m + by) % places) for m in range(places)])  16.3 us
    ppermute x12, waiting for transfers between devices, lateral(): lax.ppermute(value, 'lat', [(m, (m + by) % places) for m in range(places)])  16.2 us
    pallas_call x1, Pallas kernels, on_device(): pl.pallas_call(local_force_kernel, out_shape=sds(3, tiles, 8, width), in_...  11.3 us
    pallas_call x1, Pallas kernels, on_device(): pl.pallas_call(functools.partial(ghost_density_kernel, *sizes), out_shape...  10.6 us
    pallas_call x1, Pallas kernels, on_device(): pl.pallas_call(local_density_kernel, out_shape=(sds(tiles, 8, width), sds...  5.29 us
    ppermute x5, waiting for transfers between devices, climb(): lax.ppermute(value, both, [(l * places + m, (l + by) % layers * places +...  5.02 us
    pallas_call x1, Pallas kernels, on_device(): pl.pallas_call(spread_kernel, out_shape=sds(tiles, 7, width, width), in_s...  4.38 us
  transfers between devices with their start and end apart: 19, of which 10 were waited for; matrix products, arithmetic and copies ran while one was open for 0% of the time, Pallas kernels for 22%

profile of v3, /device:TPU:4, one launch (start us, length us, event | category | flops | bytes accessed | tf_op | source)
XLA Modules:
  0.0 95.6 jit_solution(11324317115705071117)
XLA Ops:
  0.6 0.0 copy-start
  0.6 0.8 copy-done
  1.5 0.8 copy-done.2
  2.3 0.7 copy-done.4
  3.0 0.7 copy-done.6
  3.7 0.7 copy-done.11
  4.4 0.9 shard_map.104
  5.3 1.0 %collective-permute-start.2 = (f32[16,8,128]{2,1,0:T(8,128)S(1)}, f32[16,8,128]{2,1,0:T(8,128)S(1)}, u32[]{:S(2)}, u32[]{:S(2)}) collective-permute-start(f32[16,8,128]{2,1,0:T(8,128)S(1)} %get-tuple-element.23), channel_id=1, source_target_pairs={{0,9},{1,8},{2,11},{3,10},{4,13},{5,12},{6,15},{7,14},{8,17},{9,16... | collective-permute-start | bytes 196616 | tf_op jit(solution)/shard_map/ppermute | solution.py:568
  6.2 0.6 collective-permute-start.1
  6.9 0.1 collective-permute-start
  6.9 0.1 pad_add_fusion.where
  7.0 5.0 %collective-permute-done.1.near = f32[16,8,128]{2,1,0:T(8,128)S(1)} collective-permute-done((f32[16,8,128]{2,1,0:T(8,128)S(1)}, f32[16,8,128]{2,1,0:T(8,128)S(1)}, u32[]{:S(2)}, u32[]{:S(2)}) %collective-permute-start.1) | collective-permute-done | bytes 65568 | tf_op jit(solution)/shard_map/ppermute | solution.py:568
  12.0 0.0 collective-permute-done.2.flip
  12.0 3.7 %collective-permute-start.4 = (f32[32,8,128]{2,1,0:T(8,128)S(1)}, f32[32,8,128]{2,1,0:T(8,128)S(1)}, u32[]{:S(2)}, u32[]{:S(2)}) collective-permute-start(f32[32,8,128]{2,1,0:T(8,128)S(1)} %constant_dynamic-update-slice_fusion), channel_id=1, source_target_pairs={{0,6},{1,7},{2,0},{3,1},{4,2},{5,3},{6,4},{7,5},{8,14},{9,15},{10,... | collective-permute-start | bytes 393224 | tf_op jit(solution)/shard_map/ppermute | solution.py:562
  15.7 4.4 %shard_map.105.spread = f32[32,7,128,128]{3,2,1,0:T(8,128)S(1)} custom-call(f32[32,8,128]{2,1,0:T(8,128)S(1)} %get-tuple-element.19.union), custom_call_target="tpu_custom_call" | custom-call | flops 1000000000 | bytes 15000000 | tf_op jit(solution)/shard_map/pallas_call | solution.py:598
  20.1 0.0 copy-start.7
  20.1 0.0 copy-start.8
  20.1 5.3 %shard_map.106 = (f32[32,8,128]{2,1,0:T(8,128)S(1)}, f32[32,128,128]{2,1,0:T(8,128)S(1)}) custom-call(s32[32]{0:T(128)S(1)} %copy-done.5, s32[2,32]{1,0:T(2,128)S(1)} %bitcast.12, f32[32,8,128]{2,1,0:T(8,128)S(1)} %get-tuple-element.19.union, f32[32,7,128,128]{3,2,1,0:T(8,128)S(1)} %shard_map.105.spread), custom_call_target="tpu_custom_call" | custom-call | flops 1000000000 | bytes 15000000 | tf_op jit(solution)/shard_map/pallas_call | solution.py:614
  25.4 0.0 collective-permute-done.4.above
  25.4 0.0 collective-permute-done.3.below
  25.5 0.0 copy-start.10
  25.5 10.6 %shard_map.107 = (f32[32,128]{1,0:T(8,128)S(1)}, f32[16,128]{1,0:T(8,128)S(1)}, f32[8,128]{1,0:T(8,128)S(1)}, f32[32,128]{1,0:T(8,128)S(1)}, f32[32,128]{1,0:T(8...) custom-call(s32[2]{0:T(128)S(1)} %pad_add_fusion.where, ...), custom_call_target="tpu_custom_call", output_to_operand_aliasing={{6}: (6, {})} | custom-call | tf_op jit(solution)/shard_map/pallas_call | solution.py:638
  36.1 3.7 %collective-permute-start.6 = (f32[32,128]{1,0:T(8,128)S(1)}, f32[32,128]{1,0:T(8,128)S(1)}, u32[]{:S(2)}, u32[]{:S(2)}) collective-permute-start(f32[32,128]{1,0:T(8,128)S(1)} %get-tuple-element.27), channel_id=1, source_target_pairs={{0,6},{1,7},{2,0},{3,1},{4,2},{5,3},{6,4},{7,5},{8,14},{9,15},{10,... | collective-permute-start | bytes 49160 | tf_op jit(solution)/shard_map/ppermute | solution.py:562
  39.9 0.0 collective-permute-start.7
  39.9 0.0 collective-permute-start.8
  39.9 1.4 %collective-permute-done.6 = f32[32,128]{1,0:T(8,128)S(1)} collective-permute-done((f32[32,128]{1,0:T(8,128)S(1)}, f32[32,128]{1,0:T(8,128)S(1)}, u32[]{:S(2)}, u32[]{:S(2)}) %collective-permute-start.6) | collective-permute-done | bytes 16416 | tf_op jit(solution)/shard_map/ppermute | solution.py:562
  41.3 4.1 %collective-permute-done.7 = f32[32,128]{1,0:T(8,128)S(1)} collective-permute-done((f32[32,128]{1,0:T(8,128)S(1)}, f32[32,128]{1,0:T(8,128)S(1)}, u32[]{:S(2)}, u32[]{:S(2)}) %collective-permute-start.7) | collective-permute-done | bytes 16416 | tf_op jit(solution)/shard_map/ppermute | solution.py:562
  45.4 0.0 collective-permute-done.8
  45.4 0.1 collective-permute-start.9
  45.5 2.8 %collective-permute-start.5 = (f32[8,128]{1,0:T(8,128)S(1)}, f32[8,128]{1,0:T(8,128)S(1)}, u32[]{:S(2)}, u32[]{:S(2)}) collective-permute-start(f32[8,128]{1,0:T(8,128)S(1)} %get-tuple-element.25), channel_id=1, source_target_pairs={{0,7},{1,0},{2,1},{3,2},{4,3},{5,4},{6,5},{7,6},{8,15},{9,8},{10,9... | collective-permute-start | bytes 12296 | tf_op jit(solution)/shard_map/ppermute | solution.py:562
  48.4 0.1 collective-permute-start.10
  48.5 1.2 %collective-permute-done.5 = f32[8,128]{1,0:T(8,128)S(1)} collective-permute-done((f32[8,128]{1,0:T(8,128)S(1)}, f32[8,128]{1,0:T(8,128)S(1)}, u32[]{:S(2)}, u32[]{:S(2)}) %collective-permute-start.5) | collective-permute-done | bytes 4128 | tf_op jit(solution)/shard_map/ppermute | solution.py:562
  49.7 3.9 %collective-permute-start.13 = (f32[32,128]{1,0:T(8,128)S(1)}, f32[32,128]{1,0:T(8,128)S(1)}, u32[]{:S(2)}, u32[]{:S(2)}) collective-permute-start(f32[32,128]{1,0:T(8,128)S(1)} %maximum_add_fusion.pair_rho), channel_id=1, source_target_pairs={{0,6},{1,7},{2,0},{3,1},{4,2},{5,3},{6,4},{7,5},{8,14},{9,15},{10,... | collective-permute-start | bytes 49160 | tf_op jit(solution)/shard_map/ppermute | solution.py:562
  53.6 0.9 collective-permute-done.11.face_rho
  54.5 0.5 collective-permute-done.13.above_rho
  55.1 4.1 %collective-permute-done.12.below_rho = f32[32,128]{1,0:T(8,128)S(1)} collective-permute-done((f32[32,128]{1,0:T(8,128)S(1)}, f32[32,128]{1,0:T(8,128)S(1)}, u32[]{:S(2)}, u32[]{:S(2)}) %collective-permute-start.12) | collective-permute-done | bytes 16416 | tf_op jit(solution)/shard_map/ppermute | solution.py:562
  59.1 16.4 %shard_map.108 = (f32[3,32,8,128]{3,2,1,0:T(8,128)S(1)}, f32[32,128,128]{2,1,0:T(8,128)S(1)}, f32[3,8,128]{2,1,0:T(8,128)S(1)}, f32[3,32,128]{2,1,0:T(8,128)S(1)...) custom-call(s32[2]{0:T(128)S(1)} %pad_add_fusion.where, s32[32]{0:T(128)S(1)} %copy-done.5, s32[2,32]{1,0:T(2,128)S(1)} %bitcast.9, ...), custom_call_target="tpu_custom_call" | custom-call | tf_op jit(solution)/shard_map/pallas_call | solution.py:689
  75.6 0.1 collective-permute-start.15
  75.7 2.0 %collective-permute-start.16 = (f32[3,32,128]{2,1,0:T(8,128)S(1)}, f32[3,32,128]{2,1,0:T(8,128)S(1)}, u32[]{:S(2)}, u32[]{:S(2)}) collective-permute-start(f32[3,32,128]{2,1,0:T(8,128)S(1)} %get-tuple-element.35), channel_id=1, source_target_pairs={{0,2},{1,3},{2,4},{3,5},{4,6},{5,7},{6,0},{7,1},{8,10},{9,11},{10,... | collective-permute-start | bytes 147464 | tf_op jit(solution)/shard_map/ppermute | solution.py:562
  77.7 2.1 %collective-permute-done.15 = f32[3,32,128]{2,1,0:T(8,128)S(1)} collective-permute-done((f32[3,32,128]{2,1,0:T(8,128)S(1)}, f32[3,32,128]{2,1,0:T(8,128)S(1)}, u32[]{:S(2)}, u32[]{:S(2)}) %collective-permute-start.15) | collective-permute-done | bytes 49184 | tf_op jit(solution)/shard_map/ppermute | solution.py:562
  79.7 1.9 %collective-permute-done.16 = f32[3,32,128]{2,1,0:T(8,128)S(1)} collective-permute-done((f32[3,32,128]{2,1,0:T(8,128)S(1)}, f32[3,32,128]{2,1,0:T(8,128)S(1)}, u32[]{:S(2)}, u32[]{:S(2)}) %collective-permute-start.16) | collective-permute-done | bytes 49184 | tf_op jit(solution)/shard_map/ppermute | solution.py:562
  81.6 0.1 collective-permute-start.17
  81.7 0.1 collective-permute-start.14
  81.8 1.1 %collective-permute-done.17 = f32[3,16,128]{2,1,0:T(8,128)S(1)} collective-permute-done((f32[3,16,128]{2,1,0:T(8,128)S(1)}, f32[3,16,128]{2,1,0:T(8,128)S(1)}, u32[]{:S(2)}, u32[]{:S(2)}) %collective-permute-start.17) | collective-permute-done | bytes 24608 | tf_op jit(solution)/shard_map/ppermute | solution.py:565
  82.9 0.0 copy-start.1
  82.9 0.0 copy-start.3
  82.9 11.3 %shard_map.109.local_acc = f32[3,32,8,128]{3,2,1,0:T(8,128)S(1)} custom-call(s32[32]{0:T(128)S(1)} %copy-done.5, s32[2,32]{1,0:T(2,128)S(1)} %bitcast.13, f32[2,2]{1,0:T(2,128)S(1)} %copy-done.10, f32[32,8,128]{2,1,0:T(8,128)S(1)} %get-tuple-element.19.union, f32[32,7,128,128]{3,2,1,0:T(8,128)S(1)} %shard_map.105.spread, ...), custom_call_target="tpu_custom_call" | custom-call | flops 2000000000 | bytes 20000000 | tf_op jit(solution)/shard_map/pallas_call | solution.py:735
  94.2 1.4 %shard_map.110 = (f32[3,4096]{1,0:T(4,128)}, f32[3,4096]{1,0:T(4,128)}) custom-call(s32[32]{0:T(128)S(1)} %copy-done.5, f32[3,4096]{1,0:T(4,128)S(1)} %copy-done.1, f32[3,4096]{1,0:T(4,128)S(1)} %copy-done.3, f32[3,32,8,128]{3,2,1,0:T(8,128)S(1)} %shard_map.109.local_acc, f32[3,32,8,128]{3,2,1,0:T(8,128)S(1)} %get-tuple-element.31.ghost_acc, ...), custom_call_target="tpu_custom_call" | custom-call | tf_op jit(solution)/shard_map/pallas_call | solution.py:751
  (35 shorter events, 0.1 us)
Async XLA Ops:
  0.6 0.8 copy-start
  1.5 0.8 copy-start.2
  2.3 0.7 copy-start.4
  3.0 0.7 copy-start.6
  3.7 0.7 copy-start.11
  5.3 6.8 %collective-permute-start.2 = (f32[16,8,128]{2,1,0:T(8,128)S(1)}, f32[16,8,128]{2,1,0:T(8,128)S(1)}, u32[]{:S(2)}, u32[]{:S(2)}) collective-permute-start(f32[16,8,128]{2,1,0:T(8,128)S(1)} %get-tuple-element.23), channel_id=1, source_target_pairs={{0,9},{1,8},{2,11},{3,10},{4,13},{5,12},{6,15},{7,14},{8,17},{9,16... | collective-permute-start | bytes 196616 | tf_op jit(solution)/shard_map/ppermute | solution.py:568
  6.2 5.8 %collective-permute-start.1 = (f32[16,8,128]{2,1,0:T(8,128)S(1)}, f32[16,8,128]{2,1,0:T(8,128)S(1)}, u32[]{:S(2)}, u32[]{:S(2)}) collective-permute-start(f32[16,8,128]{2,1,0:T(8,128)S(1)} %get-tuple-element.23), channel_id=1, source_target_pairs={{0,8},{1,9},{2,10},{3,11},{4,12},{5,13},{6,14},{7,15},{8,16},{9,17... | collective-permute-start | bytes 196616 | tf_op jit(solution)/shard_map/ppermute | solution.py:568
  6.9 18.6 %collective-permute-start = (f32[8,8,128]{2,1,0:T(8,128)S(1)}, f32[8,8,128]{2,1,0:T(8,128)S(1)}, u32[]{:S(2)}, u32[]{:S(2)}) collective-permute-start(f32[8,8,128]{2,1,0:T(8,128)S(1)} %get-tuple-element.22), channel_id=1, source_target_pairs={{0,1},{1,2},{2,3},{3,4},{4,5},{5,6},{6,7},{7,0},{8,9},{9,10},{10,1... | collective-permute-start | bytes 98312 | tf_op jit(solution)/shard_map/ppermute | solution.py:562
  12.0 13.4 %collective-permute-start.4 = (f32[32,8,128]{2,1,0:T(8,128)S(1)}, f32[32,8,128]{2,1,0:T(8,128)S(1)}, u32[]{:S(2)}, u32[]{:S(2)}) collective-permute-start(f32[32,8,128]{2,1,0:T(8,128)S(1)} %constant_dynamic-update-slice_fusion), channel_id=1, source_target_pairs={{0,6},{1,7},{2,0},{3,1},{4,2},{5,3},{6,4},{7,5},{8,14},{9,15},{10,... | collective-permute-start | bytes 393224 | tf_op jit(solution)/shard_map/ppermute | solution.py:562
  15.7 9.8 %collective-permute-start.3 = (f32[32,8,128]{2,1,0:T(8,128)S(1)}, f32[32,8,128]{2,1,0:T(8,128)S(1)}, u32[]{:S(2)}, u32[]{:S(2)}) collective-permute-start(f32[32,8,128]{2,1,0:T(8,128)S(1)} %constant_dynamic-update-slice_fusion), channel_id=1, source_target_pairs={{0,2},{1,3},{2,4},{3,5},{4,6},{5,7},{6,0},{7,1},{8,10},{9,11},{10,... | collective-permute-start | bytes 393224 | tf_op jit(solution)/shard_map/ppermute | solution.py:562
  15.7 4.4 %copy-start.5 = (s32[32]{0:T(128)S(1)}, s32[32]{0:T(128)}, u32[]{:S(2)}) copy-start(s32[32]{0:T(128)} %counts.1) | copy-start | bytes 388
  15.7 4.4 %copy-start.9 = (s32[32,2]{0,1:T(2,128)S(1)}, s32[32,2]{0,1:T(2,128)}, u32[]{:S(2)}) copy-start(s32[32,2]{0,1:T(2,128)} %param.14) | copy-start | bytes 772
  20.1 5.4 %copy-start.7 = (s32[32,2]{0,1:T(2,128)S(1)}, s32[32,2]{0,1:T(2,128)}, u32[]{:S(2)}) copy-start(s32[32,2]{0,1:T(2,128)} %param.15) | copy-start | bytes 772
  20.1 5.4 %copy-start.8 = (s32[32,2]{0,1:T(2,128)S(1)}, s32[32,2]{0,1:T(2,128)}, u32[]{:S(2)}) copy-start(s32[32,2]{0,1:T(2,128)} %param.17) | copy-start | bytes 772
  25.5 33.7 %copy-start.10 = (f32[2,2]{1,0:T(2,128)S(1)}, f32[2,2]{1,0:T(2,128)}, u32[]{:S(2)}) copy-start(f32[2,2]{1,0:T(2,128)} %a_table.3) | copy-start | bytes 52
  36.1 5.2 %collective-permute-start.6 = (f32[32,128]{1,0:T(8,128)S(1)}, f32[32,128]{1,0:T(8,128)S(1)}, u32[]{:S(2)}, u32[]{:S(2)}) collective-permute-start(f32[32,128]{1,0:T(8,128)S(1)} %get-tuple-element.27), channel_id=1, source_target_pairs={{0,6},{1,7},{2,0},{3,1},{4,2},{5,3},{6,4},{7,5},{8,14},{9,15},{10,... | collective-permute-start | bytes 49160 | tf_op jit(solution)/shard_map/ppermute | solution.py:562
  39.9 5.5 %collective-permute-start.7 = (f32[32,128]{1,0:T(8,128)S(1)}, f32[32,128]{1,0:T(8,128)S(1)}, u32[]{:S(2)}, u32[]{:S(2)}) collective-permute-start(f32[32,128]{1,0:T(8,128)S(1)} %get-tuple-element.28), channel_id=1, source_target_pairs={{0,2},{1,3},{2,4},{3,5},{4,6},{5,7},{6,0},{7,1},{8,10},{9,11},{10,... | collective-permute-start | bytes 49160 | tf_op jit(solution)/shard_map/ppermute | solution.py:562
  39.9 5.5 %collective-permute-start.8 = (f32[16,128]{1,0:T(8,128)S(1)}, f32[16,128]{1,0:T(8,128)S(1)}, u32[]{:S(2)}, u32[]{:S(2)}) collective-permute-start(f32[16,128]{1,0:T(8,128)S(1)} %get-tuple-element.29), channel_id=1, source_target_pairs={{0,8},{1,9},{2,10},{3,11},{4,12},{5,13},{6,14},{7,15},{8,16},{9,17... | collective-permute-start | bytes 24584 | tf_op jit(solution)/shard_map/ppermute | solution.py:568
  45.4 2.9 %collective-permute-start.9 = (f32[32,128]{1,0:T(8,128)S(1)}, f32[32,128]{1,0:T(8,128)S(1)}, u32[]{:S(2)}, u32[]{:S(2)}) collective-permute-start(f32[32,128]{1,0:T(8,128)S(1)} %pad_maximum_fusion), channel_id=1, source_target_pairs={{0,1},{1,0},{2,3},{3,2},{4,5},{5,4},{6,7},{7,6},{8,9},{9,8},{10,11... | collective-permute-start | bytes 49160 | tf_op jit(solution)/shard_map/ppermute | solution.py:565
  45.5 4.2 %collective-permute-start.5 = (f32[8,128]{1,0:T(8,128)S(1)}, f32[8,128]{1,0:T(8,128)S(1)}, u32[]{:S(2)}, u32[]{:S(2)}) collective-permute-start(f32[8,128]{1,0:T(8,128)S(1)} %get-tuple-element.25), channel_id=1, source_target_pairs={{0,7},{1,0},{2,1},{3,2},{4,3},{5,4},{6,5},{7,6},{8,15},{9,8},{10,9... | collective-permute-start | bytes 12296 | tf_op jit(solution)/shard_map/ppermute | solution.py:562
  48.4 5.2 %collective-permute-start.10 = (f32[16,128]{1,0:T(8,128)S(1)}, f32[16,128]{1,0:T(8,128)S(1)}, u32[]{:S(2)}, u32[]{:S(2)}) collective-permute-start(f32[16,128]{1,0:T(8,128)S(1)} %slice.40), channel_id=1, source_target_pairs={{0,24},{1,25},{2,26},{3,27},{4,28},{5,29},{6,30},{7,31},{8,0},{9,1... | collective-permute-start | bytes 24584 | tf_op jit(solution)/shard_map/ppermute | solution.py:568
  49.7 4.8 %collective-permute-start.11 = (f32[8,128]{1,0:T(8,128)S(1)}, f32[8,128]{1,0:T(8,128)S(1)}, u32[]{:S(2)}, u32[]{:S(2)}) collective-permute-start(f32[8,128]{1,0:T(8,128)S(1)} %get-tuple-element.36), channel_id=1, source_target_pairs={{0,1},{1,2},{2,3},{3,4},{4,5},{5,6},{6,7},{7,0},{8,9},{9,10},{10,1... | collective-permute-start | bytes 12296 | tf_op jit(solution)/shard_map/ppermute | solution.py:562
  49.7 5.3 %collective-permute-start.13 = (f32[32,128]{1,0:T(8,128)S(1)}, f32[32,128]{1,0:T(8,128)S(1)}, u32[]{:S(2)}, u32[]{:S(2)}) collective-permute-start(f32[32,128]{1,0:T(8,128)S(1)} %maximum_add_fusion.pair_rho), channel_id=1, source_target_pairs={{0,6},{1,7},{2,0},{3,1},{4,2},{5,3},{6,4},{7,5},{8,14},{9,15},{10,... | collective-permute-start | bytes 49160 | tf_op jit(solution)/shard_map/ppermute | solution.py:562
  53.6 5.5 %collective-permute-start.12 = (f32[32,128]{1,0:T(8,128)S(1)}, f32[32,128]{1,0:T(8,128)S(1)}, u32[]{:S(2)}, u32[]{:S(2)}) collective-permute-start(f32[32,128]{1,0:T(8,128)S(1)} %maximum_add_fusion.pair_rho), channel_id=1, source_target_pairs={{0,2},{1,3},{2,4},{3,5},{4,6},{5,7},{6,0},{7,1},{8,10},{9,11},{10,... | collective-permute-start | bytes 49160 | tf_op jit(solution)/shard_map/ppermute | solution.py:562
  75.6 4.1 %collective-permute-start.15 = (f32[3,32,128]{2,1,0:T(8,128)S(1)}, f32[3,32,128]{2,1,0:T(8,128)S(1)}, u32[]{:S(2)}, u32[]{:S(2)}) collective-permute-start(f32[3,32,128]{2,1,0:T(8,128)S(1)} %get-tuple-element.34), channel_id=1, source_target_pairs={{0,6},{1,7},{2,0},{3,1},{4,2},{5,3},{6,4},{7,5},{8,14},{9,15},{10,... | collective-permute-start | bytes 147464 | tf_op jit(solution)/shard_map/ppermute | solution.py:562
  75.7 5.9 %collective-permute-start.16 = (f32[3,32,128]{2,1,0:T(8,128)S(1)}, f32[3,32,128]{2,1,0:T(8,128)S(1)}, u32[]{:S(2)}, u32[]{:S(2)}) collective-permute-start(f32[3,32,128]{2,1,0:T(8,128)S(1)} %get-tuple-element.35), channel_id=1, source_target_pairs={{0,2},{1,3},{2,4},{3,5},{4,6},{5,7},{6,0},{7,1},{8,10},{9,11},{10,... | collective-permute-start | bytes 147464 | tf_op jit(solution)/shard_map/ppermute | solution.py:562
  81.6 1.3 %collective-permute-start.17 = (f32[3,16,128]{2,1,0:T(8,128)S(1)}, f32[3,16,128]{2,1,0:T(8,128)S(1)}, u32[]{:S(2)}, u32[]{:S(2)}) collective-permute-start(f32[3,16,128]{2,1,0:T(8,128)S(1)} %slice.42), channel_id=1, source_target_pairs={{0,1},{1,0},{2,3},{3,2},{4,5},{5,4},{6,7},{7,6},{8,9},{9,8},{10,11... | collective-permute-start | bytes 73736 | tf_op jit(solution)/shard_map/ppermute | solution.py:565
  81.7 12.5 %collective-permute-start.14 = (f32[3,8,128]{2,1,0:T(8,128)S(1)}, f32[3,8,128]{2,1,0:T(8,128)S(1)}, u32[]{:S(2)}, u32[]{:S(2)}) collective-permute-start(f32[3,8,128]{2,1,0:T(8,128)S(1)} %get-tuple-element.32), channel_id=1, source_target_pairs={{0,7},{1,0},{2,1},{3,2},{4,3},{5,4},{6,5},{7,6},{8,15},{9,8},{10,9... | collective-permute-start | bytes 36872 | tf_op jit(solution)/shard_map/ppermute | solution.py:562
  82.9 11.3 %collective-permute-start.18 = (f32[3,16,128]{2,1,0:T(8,128)S(1)}, f32[3,16,128]{2,1,0:T(8,128)S(1)}, u32[]{:S(2)}, u32[]{:S(2)}) collective-permute-start(f32[3,16,128]{2,1,0:T(8,128)S(1)} %slice_add_fusion), channel_id=1, source_target_pairs={{0,24},{1,25},{2,26},{3,27},{4,28},{5,29},{6,30},{7,31},{8,0},{9,1... | collective-permute-start | bytes 73736 | tf_op jit(solution)/shard_map/ppermute | solution.py:568
  82.9 11.3 %copy-start.1 = (f32[3,4096]{1,0:T(4,128)S(1)}, f32[3,4096]{1,0:T(4,128)}, u32[]{:S(2)}) copy-start(f32[3,4096]{1,0:T(4,128)} %pos.1) | copy-start | bytes 147460
  82.9 11.3 %copy-start.3 = (f32[3,4096]{1,0:T(4,128)S(1)}, f32[3,4096]{1,0:T(4,128)}, u32[]{:S(2)}) copy-start(f32[3,4096]{1,0:T(4,128)} %vel.1) | copy-start | bytes 147460

commit v4 on v3

--- a/solution.py
+++ b/solution.py
@@ -27,8 +27,12 @@
     return jax.ShapeDtypeStruct(shape, f32)
 
 
-def params():
-    return pltpu.CompilerParams(vmem_limit_bytes=32 * 1024 * 1024)
+def params(mib=24):
+    return pltpu.CompilerParams(vmem_limit_bytes=mib * 1024 * 1024)
+
+
+def in_hbm(value):
+    return pltpu.with_memory_space_constraint(value, pltpu.HBM)
 
 
 def fetch(sems, *copies):
@@ -255,10 +259,16 @@
     tile_loop(tiles, width, counts, 1 + nbr.shape[0], local_partner(counts, nbr), pair)
 
 
-def gather_ghosts(ghosts, face, near, flip, below, above):
+def gather(target, *refs):
     at = 0
-    for ref in (face, near, flip, below, above):
-        ghosts[pl.ds(at, ref.shape[0])] = ref[...]
+    for ref in refs:
+        target[pl.ds(at, ref.shape[0])] = ref[...]
+        at += ref.shape[0]
+
+
+def spill(target, at, *refs):
+    for ref in refs:
+        ref[...] = target[pl.ds(at, ref.shape[0])]
         at += ref.shape[0]
 
 
@@ -316,6 +326,7 @@
     below_out,
     above_out,
     sums,
+    listed,
     ghosts,
     acc,
     reduced,
@@ -331,29 +342,35 @@
         sems, (counts_hbm, counts), (face_nbr_hbm, face_nbr), (cross_pair_hbm, cross_pair)
     )
     tiles, width = spread.shape[0], spread.shape[2]
-    gather_ghosts(ghosts, face, near, flip, below, above)
+    gather(ghosts, face, near, flip, below, above)
     wait_meta = ghost_meta(ghosts, meta, meta_smem, sem)
-    zero(acc)
     wait()
     wait_meta()
+    zero(acc)
+    slots = face_nbr.shape[0] + cross_pair.shape[0]
+    for g in range(tiles):
+        for k in range(slots):
+            h, ok = ghost_partner(
+                k, g, face_nbr, cross_pair, where, meta_smem, faces, upper, cap, reach
+            )
+            listed[k, g] = jnp.where(ok & (counts[g] > 0), h, -1)
 
     def partner(g, k):
-        return ghost_partner(
-            k, g, face_nbr, cross_pair, where, meta_smem, faces, upper, cap, reach
-        )
+        h = listed[k, g]
+        return jnp.maximum(h, 0), h >= 0
 
     def pair(g, k, h, n):
         mine = lambda c, r: spread[g, c, pl.ds(r, 8), :]
         density_pair(mine, ghosts, h, n, acc, sums, g)
 
-    slots = face_nbr.shape[0] + cross_pair.shape[0]
     tile_loop(tiles, width, counts, slots, partner, pair)
     for t in range(0, acc.shape[0], 8):
         reduced[pl.ds(t, 8), :] = fold(acc, t)
     face_out[...] = reduced[pl.ds(0, faces)]
-    pair_out[...] = reduced[pl.ds(faces, 2 * upper)]
-    below_out[...] = reduced[pl.ds(faces + 2 * upper, 2 * upper)]
-    above_out[...] = reduced[pl.ds(faces + 4 * upper, 2 * upper)]
+    spill(reduced, faces, pair_out)
+    below_out[pl.ds(0, 2 * upper)] = reduced[pl.ds(faces + 2 * upper, 2 * upper)]
+    below_out[pl.ds(2 * upper, faces)] = reduced[pl.ds(0, faces)]
+    spill(reduced, faces + 4 * upper, above_out)
 
     def collect(t):
         acc[t] = local_acc[t] + row_sums(sums, t)
@@ -380,6 +397,120 @@
         return crowd[g, pl.ds(r, 8), :] if c == 7 else spread[g, c, pl.ds(r, 8), :]
 
     return mine
+
+
+def listed_partner(listed, first, shift):
+    def partner(g, k):
+        h = listed[first + k, g]
+        return jnp.maximum(h - shift, 0), h >= 0
+
+    return partner
+
+
+def cross_force_kernel(
+    columns,
+    faces,
+    counts_hbm,
+    listed_hbm,
+    a_table,
+    spread,
+    density,
+    near,
+    flip,
+    below,
+    above,
+    pair_rho,
+    below_rho,
+    above_rho,
+    crowd,
+    own_out,
+    pair_out,
+    below_out,
+    above_out,
+    sums,
+    ghosts,
+    acc,
+    rho,
+    reduced,
+    counts,
+    listed,
+    sems,
+):
+    wait = fetch(sems, (counts_hbm, counts), (listed_hbm, listed))
+    tiles, width = spread.shape[0], spread.shape[2]
+    zero(acc, sums)
+    table = amplitudes(a_table)
+    gather(ghosts, near, flip, below, above)
+    gather(rho, pair_rho, below_rho, above_rho)
+    for t in range(ghosts.shape[0]):
+        ghosts[t] = force_tile(ghosts, rho[pl.ds(t, 1), :], t)
+
+    def fill(g):
+        def store(r, value):
+            crowd[g, pl.ds(r, 8), :] = value
+
+        spread_row(density[pl.ds(g, 1), :] * (crowd_scale * density_scale), store)
+
+    by_fours(tiles, fill)
+    wait()
+
+    def pair(g, k, h, n):
+        force_pair(force_mine(spread, crowd, g), ghosts, h, n, table, acc, sums, g)
+
+    partner = listed_partner(listed, columns, faces)
+    tile_loop(tiles, width, counts, listed.shape[0] - columns, partner, pair)
+    for c in range(3):
+        for t in range(0, acc.shape[1], 8):
+            reduced[pl.ds(t, 8), :] = fold(acc, t, c)
+        spill(reduced, 0, pair_out.at[c], below_out.at[c], above_out.at[c])
+
+    def collect(t):
+        for c in range(3):
+            own_out[c, t] = row_sums(sums, c, t)
+
+    by_fours(tiles, collect)
+
+
+def face_force_kernel(
+    columns,
+    counts_hbm,
+    listed_hbm,
+    a_table,
+    spread,
+    crowd,
+    cross_acc,
+    face,
+    face_rho,
+    own_out,
+    face_out,
+    sums,
+    ghosts,
+    acc,
+    counts,
+    listed,
+    sems,
+):
+    wait = fetch(sems, (counts_hbm, counts), (listed_hbm, listed))
+    tiles, width = spread.shape[0], spread.shape[2]
+    zero(acc, sums)
+    table = amplitudes(a_table)
+    for t in range(ghosts.shape[0]):
+        ghosts[t] = force_tile(face, face_rho[pl.ds(t, 1), :], t)
+    wait()
+
+    def pair(g, k, h, n):
+        force_pair(force_mine(spread, crowd, g), ghosts, h, n, table, acc, sums, g)
+
+    tile_loop(tiles, width, counts, columns, listed_partner(listed, 0, 0), pair)
+    for c in range(3):
+        for t in range(0, acc.shape[1], 8):
+            face_out[c, pl.ds(t, 8), :] = fold(acc, t, c)
+
+    def collect(t):
+        for c in range(3):
+            own_out[c, t] = cross_acc[c, t] + row_sums(sums, c, t)
+
+    by_fours(tiles, collect)
 
 
 def local_force_kernel(
@@ -390,6 +521,7 @@
     spread,
     crowd,
     density,
+    ghost_acc,
     acc,
     beads,
     sums,
@@ -400,7 +532,8 @@
     wait = fetch(sems, (counts_hbm, counts), (nbr_hbm, nbr))
     tiles, width = union.shape[0], union.shape[2]
     table = amplitudes(a_table)
-    zero(acc, sums)
+    acc[...] = ghost_acc[...]
+    zero(sums)
     for t in range(tiles):
         beads[t] = force_tile(union, density[pl.ds(t, 1), :], t)
     wait()
@@ -417,111 +550,13 @@
     by_fours(tiles, collect)
 
 
-def ghost_force_kernel(
-    faces,
-    upper,
-    cap,
-    reach,
-    where,
-    counts_hbm,
-    face_nbr_hbm,
-    cross_pair_hbm,
-    a_table,
-    union,
-    spread,
-    density,
-    face,
-    near,
-    flip,
-    below,
-    above,
-    face_rho,
-    pair_rho,
-    below_rho,
-    above_rho,
-    own_out,
-    crowd,
-    face_out,
-    pair_out,
-    below_out,
-    above_out,
-    ghosts,
-    acc,
-    rho,
-    sums,
-    reduced,
-    counts,
-    face_nbr,
-    cross_pair,
-    meta,
-    meta_smem,
-    sems,
-    sem,
-):
-    wait = fetch(
-        sems, (counts_hbm, counts), (face_nbr_hbm, face_nbr), (cross_pair_hbm, cross_pair)
-    )
-    tiles, width = union.shape[0], union.shape[2]
-    gather_ghosts(ghosts, face, near, flip, below, above)
-    wait_meta = ghost_meta(ghosts, meta, meta_smem, sem)
-    zero(acc, sums)
-    table = amplitudes(a_table)
-    at = 0
-    for ref in (face_rho, pair_rho, below_rho, above_rho):
-        rho[pl.ds(at, ref.shape[0]), :] = ref[...]
-        at += ref.shape[0]
-    for t in range(ghosts.shape[0]):
-        ghosts[t] = force_tile(ghosts, rho[pl.ds(t, 1), :], t)
-
-    def fill(g):
-        def store(r, value):
-            crowd[g, pl.ds(r, 8), :] = value
-
-        spread_row(density[pl.ds(g, 1), :] * (crowd_scale * density_scale), store)
-
-    by_fours(tiles, fill)
-    wait()
-    wait_meta()
-
-    def partner(g, k):
-        return ghost_partner(
-            k, g, face_nbr, cross_pair, where, meta_smem, faces, upper, cap, reach
-        )
-
-    def pair(g, k, h, n):
-        force_pair(force_mine(spread, crowd, g), ghosts, h, n, table, acc, sums, g)
-
-    slots = face_nbr.shape[0] + cross_pair.shape[0]
-    tile_loop(tiles, width, counts, slots, partner, pair)
-    for c in range(3):
-        for t in range(0, acc.shape[1], 8):
-            reduced[pl.ds(t, 8), :] = fold(acc, t, c)
-        face_out[c] = reduced[pl.ds(0, faces)]
-        pair_out[c] = reduced[pl.ds(faces, 2 * upper)]
-        below_out[c] = reduced[pl.ds(faces + 2 * upper, 2 * upper)]
-        above_out[c] = reduced[pl.ds(faces + 4 * upper, 2 * upper)]
-
-    def collect(t):
-        for c in range(3):
-            own_out[c, t] = row_sums(sums, c, t)
-
-    by_fours(tiles, collect)
-
-
-def finish_kernel(counts, pos, vel, local_acc, ghost_acc, face_back, top_back, pos_out, vel_out, force):
-    tiles, width = local_acc.shape[1], local_acc.shape[3]
+def finish_kernel(counts, pos, vel, acc, face_back, top_back, pos_out, vel_out):
+    tiles, width = acc.shape[1], acc.shape[3]
     faces, upper = face_back.shape[1], top_back.shape[1]
     lane = lax.broadcasted_iota(jnp.int32, (1, width), 1)
-
-    def add(t):
-        for c in range(3):
-            force[c, t] = local_acc[c, t] + ghost_acc[c, t]
-
-    for t in range(tiles):
-        add(t)
     for c in range(3):
         for t in range(0, tiles, 8):
-            total = fold(force, t, c)
+            total = fold(acc, t, c)
             if t < faces:
                 total = total + face_back[c, pl.ds(t, 8), :]
             if t >= tiles - upper:
@@ -576,8 +611,11 @@
         )
 
     kinds = types.reshape(tiles, width)
-    local_nbr, face_nbr, cross_pair = local_nbr.T, face_nbr.T, cross_pair.T
-    send = cross_send.transpose(1, 0, 2)
+    local_nbr, face_nbr, cross_pair = (
+        in_hbm(table.T) for table in (local_nbr, face_nbr, cross_pair)
+    )
+    send = in_hbm(cross_send.transpose(1, 0, 2))
+    counts_hbm = in_hbm(counts)
     ints = jnp.int32
     counts_smem = pltpu.SMEM((tiles,), ints)
     payload, top, face = pl.pallas_call(
@@ -594,7 +632,10 @@
             pltpu.SemaphoreType.DMA((5,)),
         ],
         compiler_params=params(),
-    )(positions, velocities, kinds, counts, send)
+    )(in_hbm(positions), in_hbm(velocities), in_hbm(kinds), counts_hbm, send)
+    near = climb(top, 1)
+    flip = climb(top, 1, 1)
+    face_ghosts = lateral(face, 1)
     spread = pl.pallas_call(
         spread_kernel,
         out_shape=sds(tiles, 7, width, width),
@@ -603,9 +644,7 @@
         cost_estimate=pl.CostEstimate(flops=10**9, bytes_accessed=15 * 10**6, transcendentals=0),
         compiler_params=params(),
     )(payload)
-    near = climb(top, 1)
-    flip = climb(top, 1, 1)
-    face_ghosts = lateral(face, 1)
+    near, flip, spread = lax.optimization_barrier((near, flip, spread))
     chip_ghosts = jnp.concatenate([near, flip], axis=0)
     below = lateral(chip_ghosts, 2)
     above = lateral(chip_ghosts, -2)
@@ -623,7 +662,7 @@
         ],
         cost_estimate=pl.CostEstimate(flops=10**9, bytes_accessed=15 * 10**6, transcendentals=0),
         compiler_params=params(),
-    )(counts, local_nbr, payload, spread)
+    )(counts_hbm, local_nbr, payload, spread)
 
     sizes = (faces, upper, cap, reach)
     tables = [
@@ -635,19 +674,20 @@
         pltpu.SemaphoreType.DMA((3,)),
         pltpu.SemaphoreType.DMA,
     ]
-    own, own_top, face_part, pair_part, below_part, above_part, _ = pl.pallas_call(
+    own, own_top, face_part, pair_part, below_part, above_part, _, listed = pl.pallas_call(
         functools.partial(ghost_density_kernel, *sizes),
         out_shape=(
             sds(tiles, width),
             sds(upper, width),
             sds(faces, width),
             sds(2 * upper, width),
-            sds(2 * upper, width),
+            sds(2 * upper + faces, width),
             sds(2 * upper, width),
             sds(tiles, width, width),
+            jax.ShapeDtypeStruct((face_nbr.shape[0] + cross_pair.shape[0], tiles), ints),
         ),
         in_specs=[SMEM] + [HBM] * 3 + [VMEM] * 8,
-        out_specs=[VMEM] * 7,
+        out_specs=[VMEM] * 7 + [SMEM],
         scratch_shapes=[
             pltpu.VMEM((total, 8, width), f32),
             pltpu.VMEM((total, 8, width), f32),
@@ -658,7 +698,7 @@
         compiler_params=params(),
     )(
         where,
-        counts,
+        counts_hbm,
         face_nbr,
         cross_pair,
         spread,
@@ -671,71 +711,94 @@
         above,
     )
 
+    pairs = 2 * upper
+    odd = where[1] == 1
     owner_part = climb(own_top, 1)
     from_above = lateral(below_part, -2)
     from_below = lateral(above_part, 2)
-    face_back = lateral(face_part, -1)
-    met = pair_part + from_above + from_below
+    passed = jnp.where(odd, face_part, from_above[pairs:])
+    met = pair_part + from_above[:pairs] + from_below
     met = jnp.concatenate([met[:upper] + owner_part, met[upper:]], axis=0)
-    other = swap(met)
-    pair_rho = met + jnp.concatenate([other[upper:], other[:upper]], axis=0)
+    other = swap(jnp.concatenate([met, passed, own[:faces]], axis=0))
+    pair_rho = met + jnp.concatenate([other[upper:pairs], other[:upper]], axis=0)
+    bottom_rho = own[:faces] + other[pairs : pairs + faces]
+    other_rho = passed + other[pairs + faces :]
     top_rho = climb(pair_rho[:upper], -1)
-    below_rho = lateral(pair_rho, 2)
+    below_rho = lateral(jnp.concatenate([pair_rho, other_rho], axis=0), 2)
     above_rho = lateral(pair_rho, -2)
-    bottom_rho = own[:faces] + face_back
-    face_rho = lateral(bottom_rho, 1)
+    face_rho = jnp.where(odd, other_rho, below_rho[pairs:])
+    below_rho = below_rho[:pairs]
     density = jnp.concatenate([bottom_rho, own[faces : tiles - upper], top_rho], axis=0)
 
-    ghost_acc, crowd, face_force, pair_force, below_force, above_force = pl.pallas_call(
-        functools.partial(ghost_force_kernel, *sizes),
+    listed = in_hbm(listed)
+    columns = face_nbr.shape[0]
+    small = [
+        counts_smem,
+        pltpu.SMEM(listed.shape, ints),
+        pltpu.SemaphoreType.DMA((2,)),
+    ]
+    crowd, cross_acc, pair_force, below_force, above_force = pl.pallas_call(
+        functools.partial(cross_force_kernel, columns, faces),
         out_shape=(
+            sds(tiles, width, width),
             sds(3, tiles, 8, width),
-            sds(tiles, width, width),
-            sds(3, faces, width),
-            sds(3, 2 * upper, width),
-            sds(3, 2 * upper, width),
-            sds(3, 2 * upper, width),
+            sds(3, pairs, width),
+            sds(3, pairs, width),
+            sds(3, pairs, width),
         ),
-        in_specs=[SMEM] + [HBM] * 3 + [SMEM] + [VMEM] * 12,
-        out_specs=[VMEM] * 6,
+        in_specs=[HBM] * 2 + [SMEM] + [VMEM] * 9,
+        out_specs=[VMEM] * 5,
         scratch_shapes=[
-            pltpu.VMEM((total, 8, width), f32),
-            pltpu.VMEM((3, total, 8, width), f32),
-            pltpu.VMEM((total, width), f32),
             pltpu.VMEM((3, tiles, width, width), f32),
-            pltpu.VMEM((total, width), f32),
+            pltpu.VMEM((3 * pairs, 8, width), f32),
+            pltpu.VMEM((3, 3 * pairs, 8, width), f32),
+            pltpu.VMEM((3 * pairs, width), f32),
+            pltpu.VMEM((3 * pairs, width), f32),
         ]
-        + tables,
+        + small,
         compiler_params=params(),
     )(
-        where,
-        counts,
-        face_nbr,
-        cross_pair,
+        counts_hbm,
+        listed,
         a_table,
-        payload,
         spread,
         density,
-        face_ghosts,
         near,
         flip,
         below,
         above,
-        face_rho,
         pair_rho,
         below_rho,
         above_rho,
     )
-
+    from_above = lateral(below_force, -2)
+    from_below = lateral(above_force, 2)
+    ghost_acc, face_force = pl.pallas_call(
+        functools.partial(face_force_kernel, columns),
+        out_shape=(sds(3, tiles, 8, width), sds(3, faces, width)),
+        in_specs=[HBM] * 2 + [SMEM] + [VMEM] * 5,
+        out_specs=[VMEM] * 2,
+        scratch_shapes=[
+            pltpu.VMEM((3, tiles, width, width), f32),
+            pltpu.VMEM((faces, 8, width), f32),
+            pltpu.VMEM((3, faces, 8, width), f32),
+        ]
+        + small,
+        cost_estimate=pl.CostEstimate(flops=10**9, bytes_accessed=20 * 10**6, transcendentals=0),
+        compiler_params=params(),
+    )(counts_hbm, listed, a_table, spread, crowd, cross_acc, face_ghosts, face_rho)
+    from_above, from_below, face_force = lax.optimization_barrier(
+        (from_above, from_below, face_force)
+    )
     force_face = lateral(face_force, -1)
-    force_met = pair_force + lateral(below_force, -2) + lateral(above_force, 2)
+    force_met = pair_force + from_above + from_below
     force_other = swap(force_met[:, upper:])
     force_top = climb(force_met[:, :upper] + force_other, -1)
 
-    local_force = pl.pallas_call(
+    force = pl.pallas_call(
         local_force_kernel,
         out_shape=sds(3, tiles, 8, width),
-        in_specs=[HBM, HBM, SMEM] + [VMEM] * 4,
+        in_specs=[HBM, HBM, SMEM] + [VMEM] * 5,
         out_specs=VMEM,
         scratch_shapes=[
             pltpu.VMEM((tiles, 8, width), f32),
@@ -746,16 +809,15 @@
         ],
         cost_estimate=pl.CostEstimate(flops=2 * 10**9, bytes_accessed=20 * 10**6, transcendentals=0),
         compiler_params=params(),
-    )(counts, local_nbr, a_table, payload, spread, crowd, density)
+    )(counts_hbm, local_nbr, a_table, payload, spread, crowd, density, ghost_acc)
 
     return pl.pallas_call(
         finish_kernel,
         out_shape=(sds(*positions.shape), sds(*velocities.shape)),
-        in_specs=[SMEM] + [VMEM] * 6,
+        in_specs=[SMEM] + [VMEM] * 5,
         out_specs=[VMEM] * 2,
-        scratch_shapes=[pltpu.VMEM((3, tiles, 8, width), f32)],
         compiler_params=params(),
-    )(counts, positions, velocities, local_force, ghost_acc, force_face, force_top)
+    )(counts, positions, velocities, force, force_face, force_top)
 
 
 def solution(mesh):

time: 95.9 us -> 89.8 us (0.936)
  waiting for transfers between devices: 22.4 us -> 14.3 us
  Pallas kernels: 50.3 us -> 53.3 us
  starting transfers between devices: 18.2 us -> 15.2 us
  local copies, waits for them, and re-layouts: 3.79 us -> 5.8 us
    ppermute x12 -> x10, waiting for transfers between devices: 16.2 us -> 9.93 us  [lateral(): lax.ppermute(value, 'lat', [(m, (m + by) % places) for m in range(places)])]
    ppermute x12 -> x10, starting transfers between devices: 16.3 us -> 12.5 us  [lateral(): lax.ppermute(value, 'lat', [(m, (m + by) % places) for m in range(places)])]
    unnamed x25 -> x23, local copies, waits for them, and re-layouts: 3.77 us -> 5.79 us
    pallas_call x1 -> x2, Pallas kernels: 16.4 us -> 18.3 us  [the longest x1 9.27 us: on_device(): pl.pallas_call(functools.partial(face_force_kernel, columns), out_shape=(...]
    ppermute x5, waiting for transfers between devices: 5.02 us -> 3.22 us  [climb(): lax.ppermute(value, both, [(l * places + m, (l + by) % layers * places +...]
  transfers between devices with their start and end apart: 19 -> 17, of which waited for: 10 -> 6; matrix products, arithmetic and copies ran while one was open for 0% -> 0% of each run, Pallas kernels for 22% -> 34%
where the time goes in v4:
time: 89.8 us
  Pallas kernels  53.3 us (59%)
  starting transfers between devices  15.2 us (17%)
  waiting for transfers between devices  14.3 us (16%)
  local copies, waits for them, and re-layouts  5.8 us (6%)
  between operations  0.96 us (1%)
    ppermute x10, starting transfers between devices, lateral(): lax.ppermute(value, 'lat', [(m, (m + by) % places) for m in range(places)])  12.5 us
    pallas_call x1, Pallas kernels, on_device(): pl.pallas_call(local_force_kernel, out_shape=sds(3, tiles, 8, width), in_...  11.4 us
    pallas_call x1, Pallas kernels, on_device(): pl.pallas_call(functools.partial(ghost_density_kernel, *sizes), out_shape...  11.3 us
    ppermute x10, waiting for transfers between devices, lateral(): lax.ppermute(value, 'lat', [(m, (m + by) % places) for m in range(places)])  9.93 us
    pallas_call x1, Pallas kernels, on_device(): pl.pallas_call(functools.partial(face_force_kernel, columns), out_shape=(...  9.27 us
    pallas_call x1, Pallas kernels, on_device(): pl.pallas_call(functools.partial(cross_force_kernel, columns, faces), out...  9.08 us
    unnamed x23, local copies, waits for them, and re-layouts  5.79 us
    pallas_call x1, Pallas kernels, on_device(): pl.pallas_call(local_density_kernel, out_shape=(sds(tiles, 8, width), sds...  5.46 us
  transfers between devices with their start and end apart: 17, of which 6 were waited for; matrix products, arithmetic and copies ran while one was open for 0% of the time, Pallas kernels for 34%

profile of v4, /device:TPU:4, one launch (start us, length us, event | category | flops | bytes accessed | tf_op | source)
XLA Modules:
  0.0 89.8 jit_solution(13916559440063702588)
XLA Ops:
  0.6 1.0 %shard_map.104 = (f32[32,8,128]{2,1,0:T(8,128)S(1)}, f32[16,8,128]{2,1,0:T(8,128)S(1)}, f32[8,8,128]{2,1,0:T(8,128)S(1)}) custom-call(f32[3,4096]{1,0:T(4,128)} %pos.1, f32[3,4096]{1,0:T(4,128)} %vel.1, s32[32,128]{1,0:T(8,128)} %bitcast.9, s32[32]{0:T(128)} %counts.1, s32[5,1,12]{2,1,0:T(1,128)} %bitcast.12), custom_call_target="tpu_custom_call" | custom-call | tf_op jit(solution)/shard_map/pallas_call | solution.py:621
  1.7 1.0 %collective-permute-start.1 = (f32[16,8,128]{2,1,0:T(8,128)S(1)}, f32[16,8,128]{2,1,0:T(8,128)S(1)}, u32[]{:S(2)}, u32[]{:S(2)}) collective-permute-start(f32[16,8,128]{2,1,0:T(8,128)S(1)} %get-tuple-element.28), channel_id=1, source_target_pairs={{0,9},{1,8},{2,11},{3,10},{4,13},{5,12},{6,15},{7,14},{8,17},{9,16... | collective-permute-start | bytes 196616 | tf_op jit(solution)/shard_map/ppermute | solution.py:603
  2.7 0.6 collective-permute-start
  3.3 0.1 collective-permute-start.2
  3.3 4.4 %shard_map.105.spread = f32[32,7,128,128]{3,2,1,0:T(8,128)S(1)} custom-call(f32[32,8,128]{2,1,0:T(8,128)S(1)} %get-tuple-element.27.union), custom_call_target="tpu_custom_call" | custom-call | flops 1000000000 | bytes 15000000 | tf_op jit(solution)/shard_map/pallas_call | solution.py:639
  7.7 0.0 collective-permute-done.1.flip
  7.8 0.7 collective-permute-done.near
  8.4 3.7 %collective-permute-start.4 = (f32[32,8,128]{2,1,0:T(8,128)S(1)}, f32[32,8,128]{2,1,0:T(8,128)S(1)}, u32[]{:S(2)}, u32[]{:S(2)}) collective-permute-start(f32[32,8,128]{2,1,0:T(8,128)S(1)} %constant_dynamic-update-slice_fusion), channel_id=1, source_target_pairs={{0,6},{1,7},{2,0},{3,1},{4,2},{5,3},{6,4},{7,5},{8,14},{9,15},{10,... | collective-permute-start | bytes 393224 | tf_op jit(solution)/shard_map/ppermute | solution.py:597
  12.1 0.0 collective-permute-start.3
  12.1 0.1 pad_add_fusion.where
  12.2 5.5 %shard_map.106 = (f32[32,8,128]{2,1,0:T(8,128)S(1)}, f32[32,128,128]{2,1,0:T(8,128)S(1)}) custom-call(s32[32]{0:T(128)} %counts.1, s32[2,32]{1,0:T(2,128)} %bitcast.10, f32[32,8,128]{2,1,0:T(8,128)S(1)} %get-tuple-element.27.union, f32[32,7,128,128]{3,2,1,0:T(8,128)S(1)} %shard_map.105.spread), custom_call_target="tpu_custom_call" | custom-call | flops 1000000000 | bytes 15000000 | tf_op jit(solution)/shard_map/pallas_call | solution.py:653
  17.6 0.0 collective-permute-done.2.face
  17.7 0.0 collective-permute-done.4.above
  17.7 2.0 %collective-permute-done.3.below = f32[32,8,128]{2,1,0:T(8,128)S(1)} collective-permute-done((f32[32,8,128]{2,1,0:T(8,128)S(1)}, f32[32,8,128]{2,1,0:T(8,128)S(1)}, u32[]{:S(2)}, u32[]{:S(2)}) %collective-permute-start.3) | collective-permute-done | bytes 131104 | tf_op jit(solution)/shard_map/ppermute | solution.py:597
  19.7 11.3 %shard_map.107 = (f32[32,128]{1,0:T(8,128)S(1)}, f32[16,128]{1,0:T(8,128)S(1)}, f32[8,128]{1,0:T(8,128)S(1)}, f32[32,128]{1,0:T(8,128)S(1)}, f32[40,128]{1,0:T(8...) custom-call(s32[2]{0:T(128)S(1)} %pad_add_fusion.where, ...), custom_call_target="tpu_custom_call", output_to_operand_aliasing={{6}: (6, {})} | custom-call | tf_op jit(solution)/shard_map/pallas_call | solution.py:677
  31.0 0.0 copy-start.6
  31.0 0.6 copy-done.6
  31.6 1.5 %collective-permute-start.5 = (f32[40,128]{1,0:T(8,128)S(1)}, f32[40,128]{1,0:T(8,128)S(1)}, u32[]{:S(2)}, u32[]{:S(2)}) collective-permute-start(f32[40,128]{1,0:T(8,128)S(1)} %get-tuple-element.38), channel_id=1, source_target_pairs={{0,6},{1,7},{2,0},{3,1},{4,2},{5,3},{6,4},{7,5},{8,14},{9,15},{10,... | collective-permute-start | bytes 61448 | tf_op jit(solution)/shard_map/ppermute | solution.py:597
  33.1 0.5 collective-permute-start.6
  33.6 0.0 collective-permute-start.7
  33.6 5.0 %collective-permute-done.6 = f32[32,128]{1,0:T(8,128)S(1)} collective-permute-done((f32[32,128]{1,0:T(8,128)S(1)}, f32[32,128]{1,0:T(8,128)S(1)}, u32[]{:S(2)}, u32[]{:S(2)}) %collective-permute-start.6) | collective-permute-done | bytes 16416 | tf_op jit(solution)/shard_map/ppermute | solution.py:597
  38.7 0.0 collective-permute-done.5
  38.7 0.0 collective-permute-done.7
  38.7 0.1 collective-permute-start.8
  38.8 1.2 %collective-permute-done.8 = f32[48,128]{1,0:T(8,128)S(1)} collective-permute-done((f32[48,128]{1,0:T(8,128)S(1)}, f32[48,128]{1,0:T(8,128)S(1)}, u32[]{:S(2)}, u32[]{:S(2)}) %collective-permute-start.8) | collective-permute-done | bytes 24608 | tf_op jit(solution)/shard_map/ppermute | solution.py:600
  40.0 2.8 %collective-permute-start.11 = (f32[32,128]{1,0:T(8,128)S(1)}, f32[32,128]{1,0:T(8,128)S(1)}, u32[]{:S(2)}, u32[]{:S(2)}) collective-permute-start(f32[32,128]{1,0:T(8,128)S(1)} %maximum_add_fusion.pair_rho), channel_id=1, source_target_pairs={{0,6},{1,7},{2,0},{3,1},{4,2},{5,3},{6,4},{7,5},{8,14},{9,15},{10,... | collective-permute-start | bytes 49160 | tf_op jit(solution)/shard_map/ppermute | solution.py:597
  42.8 0.9 %collective-permute-start.9 = (f32[16,128]{1,0:T(8,128)S(1)}, f32[16,128]{1,0:T(8,128)S(1)}, u32[]{:S(2)}, u32[]{:S(2)}) collective-permute-start(f32[16,128]{1,0:T(8,128)S(1)} %slice.68), channel_id=1, source_target_pairs={{0,24},{1,25},{2,26},{3,27},{4,28},{5,29},{6,30},{7,31},{8,0},{9,1... | collective-permute-start | bytes 24584 | tf_op jit(solution)/shard_map/ppermute | solution.py:603
  43.7 0.2 collective-permute-start.10
  43.9 2.5 %collective-permute-done.9 = f32[16,128]{1,0:T(8,128)S(1)} collective-permute-done((f32[16,128]{1,0:T(8,128)S(1)}, f32[16,128]{1,0:T(8,128)S(1)}, u32[]{:S(2)}, u32[]{:S(2)}) %collective-permute-start.9) | collective-permute-done | bytes 8224 | tf_op jit(solution)/shard_map/ppermute | solution.py:603
  46.4 2.8 %collective-permute-done.10 = f32[40,128]{1,0:T(8,128)S(1)} collective-permute-done((f32[40,128]{1,0:T(8,128)S(1)}, f32[40,128]{1,0:T(8,128)S(1)}, u32[]{:S(2)}, u32[]{:S(2)}) %collective-permute-start.10) | collective-permute-done | bytes 20512 | tf_op jit(solution)/shard_map/ppermute | solution.py:597
  49.3 0.0 collective-permute-done.11.above_rho
  49.3 5.2 %copy-done.1 = f32[32,7,128,128]{3,2,1,0:T(8,128)S(1)} copy-done((f32[32,7,128,128]{3,2,1,0:T(8,128)S(1)}, f32[32,7,128,128]{3,2,1,0:T(8,128)}, u32[]{:S(2)}) %copy-start.1) | copy-done | bytes 14680088
  54.5 9.1 %shard_map.108 = (f32[32,128,128]{2,1,0:T(8,128)S(1)}, f32[3,32,8,128]{3,2,1,0:T(8,128)S(1)}, f32[3,32,128]{2,1,0:T(8,128)S(1)}, f32[3,32,128]{2,1,0:T(8,128)S(1)}, f32[3,32,128]{2,1,0:T(8,128)S(1)}) custom-call(s32[32]{0:T(128)} %counts.1, s32[4,32]{1,0:T(4,128)} %copy-done.6, f32[2,2]{1,0:T(2,128)S(1)} %copy-done.5, f32[32,7,128,128]{3,2,1,0:T(8,128)S(1)} %copy-done.1, ...), custom_call_target="tpu_custom_call" | custom-call | tf_op jit(solution)/shard_map/pallas_call | solution.py:740
  63.6 0.1 collective-permute-start.12
  63.6 2.0 %collective-permute-start.13 = (f32[3,32,128]{2,1,0:T(8,128)S(1)}, f32[3,32,128]{2,1,0:T(8,128)S(1)}, u32[]{:S(2)}, u32[]{:S(2)}) collective-permute-start(f32[3,32,128]{2,1,0:T(8,128)S(1)} %get-tuple-element.46), channel_id=1, source_target_pairs={{0,2},{1,3},{2,4},{3,5},{4,6},{5,7},{6,0},{7,1},{8,10},{9,11},{10,... | collective-permute-start | bytes 147464 | tf_op jit(solution)/shard_map/ppermute | solution.py:597
  65.6 9.3 %shard_map.109 = (f32[3,32,8,128]{3,2,1,0:T(8,128)S(1)}, f32[3,8,128]{2,1,0:T(8,128)S(1)}) custom-call(s32[32]{0:T(128)} %counts.1, s32[4,32]{1,0:T(4,128)} %copy-done.6, f32[2,2]{1,0:T(2,128)S(1)} %copy-done.5, f32[32,7,128,128]{3,2,1,0:T(8,128)S(1)} %copy-done.1, f32[32,128,128]{2,1,0:T(8,128)S(1)} %get-tuple-element.42.crowd, ...), custom_call_target="tpu_custom_call" | custom-call | flops 1000000000 | bytes 20000000 | tf_op jit(solution)/shard_map/pallas_call | solution.py:776
  74.9 0.0 collective-permute-done.12
  74.9 0.0 collective-permute-done.13
  75.0 0.1 collective-permute-start.15
  75.0 1.7 %collective-permute-start.14 = (f32[3,8,128]{2,1,0:T(8,128)S(1)}, f32[3,8,128]{2,1,0:T(8,128)S(1)}, u32[]{:S(2)}, u32[]{:S(2)}) collective-permute-start(f32[3,8,128]{2,1,0:T(8,128)S(1)} %get-tuple-element.48), channel_id=1, source_target_pairs={{0,7},{1,0},{2,1},{3,2},{4,3},{5,4},{6,5},{7,6},{8,15},{9,8},{10,9... | collective-permute-start | bytes 36872 | tf_op jit(solution)/shard_map/ppermute | solution.py:597
  76.7 0.0 collective-permute-done.15
  76.8 0.1 collective-permute-start.16
  76.9 0.0 copy-start.2
  76.9 0.0 copy-start.3
  76.9 0.0 copy-start.4
  76.9 11.4 %shard_map.110.acc = f32[3,32,8,128]{3,2,1,0:T(8,128)S(1)} custom-call(s32[32]{0:T(128)} %counts.1, s32[2,32]{1,0:T(2,128)} %bitcast.11, f32[2,2]{1,0:T(2,128)S(1)} %copy-done.5, f32[32,8,128]{2,1,0:T(8,128)S(1)} %get-tuple-element.27.union, f32[32,7,128,128]{3,2,1,0:T(8,128)S(1)} %bitcast.8, f32[32,128,128]{2,1,0:T(8,128)S(1)} %get-tuple-element.42.crowd, ...), custom_call_target="tpu_custom_call" | custom-call | flops 2000000000 | bytes 20000000 | tf_op jit(solution)/shard_map/pallas_call | solution.py:798
  88.3 0.0 collective-permute-done.16.top_back
  88.4 1.4 %shard_map.111 = (f32[3,4096]{1,0:T(4,128)}, f32[3,4096]{1,0:T(4,128)}) custom-call(s32[32]{0:T(128)S(1)} %copy-done.4, f32[3,4096]{1,0:T(4,128)S(1)} %copy-done.2, f32[3,4096]{1,0:T(4,128)S(1)} %copy-done.3, f32[3,32,8,128]{3,2,1,0:T(8,128)S(1)} %shard_map.110.acc, f32[3,8,128]{2,1,0:T(8,128)S(1)} %collective-permute-done.14.face_back, ...), custom_call_target="tpu_custom_call" | custom-call | tf_op jit(solution)/shard_map/pallas_call | solution.py:814
  (36 shorter events, 0.1 us)
Async XLA Ops:
  1.7 6.1 %collective-permute-start.1 = (f32[16,8,128]{2,1,0:T(8,128)S(1)}, f32[16,8,128]{2,1,0:T(8,128)S(1)}, u32[]{:S(2)}, u32[]{:S(2)}) collective-permute-start(f32[16,8,128]{2,1,0:T(8,128)S(1)} %get-tuple-element.28), channel_id=1, source_target_pairs={{0,9},{1,8},{2,11},{3,10},{4,13},{5,12},{6,15},{7,14},{8,17},{9,16... | collective-permute-start | bytes 196616 | tf_op jit(solution)/shard_map/ppermute | solution.py:603
  2.7 5.8 %collective-permute-start = (f32[16,8,128]{2,1,0:T(8,128)S(1)}, f32[16,8,128]{2,1,0:T(8,128)S(1)}, u32[]{:S(2)}, u32[]{:S(2)}) collective-permute-start(f32[16,8,128]{2,1,0:T(8,128)S(1)} %get-tuple-element.28), channel_id=1, source_target_pairs={{0,8},{1,9},{2,10},{3,11},{4,12},{5,13},{6,14},{7,15},{8,16},{9,17... | collective-permute-start | bytes 196616 | tf_op jit(solution)/shard_map/ppermute | solution.py:603
  3.3 14.4 %collective-permute-start.2 = (f32[8,8,128]{2,1,0:T(8,128)S(1)}, f32[8,8,128]{2,1,0:T(8,128)S(1)}, u32[]{:S(2)}, u32[]{:S(2)}) collective-permute-start(f32[8,8,128]{2,1,0:T(8,128)S(1)} %get-tuple-element.32), channel_id=1, source_target_pairs={{0,1},{1,2},{2,3},{3,4},{4,5},{5,6},{6,7},{7,0},{8,9},{9,10},{10,1... | collective-permute-start | bytes 98312 | tf_op jit(solution)/shard_map/ppermute | solution.py:597
  7.7 12.0 %copy-start = (f32[32,7,128,128]{3,2,1,0:T(8,128)}, f32[32,7,128,128]{3,2,1,0:T(8,128)S(1)}, u32[]{:S(2)}) copy-start(f32[32,7,128,128]{3,2,1,0:T(8,128)S(1)} %shard_map.105.spread) | copy-start | bytes 44040196
  8.4 9.2 %collective-permute-start.4 = (f32[32,8,128]{2,1,0:T(8,128)S(1)}, f32[32,8,128]{2,1,0:T(8,128)S(1)}, u32[]{:S(2)}, u32[]{:S(2)}) collective-permute-start(f32[32,8,128]{2,1,0:T(8,128)S(1)} %constant_dynamic-update-slice_fusion), channel_id=1, source_target_pairs={{0,6},{1,7},{2,0},{3,1},{4,2},{5,3},{6,4},{7,5},{8,14},{9,15},{10,... | collective-permute-start | bytes 393224 | tf_op jit(solution)/shard_map/ppermute | solution.py:597
  12.1 7.6 %collective-permute-start.3 = (f32[32,8,128]{2,1,0:T(8,128)S(1)}, f32[32,8,128]{2,1,0:T(8,128)S(1)}, u32[]{:S(2)}, u32[]{:S(2)}) collective-permute-start(f32[32,8,128]{2,1,0:T(8,128)S(1)} %constant_dynamic-update-slice_fusion), channel_id=1, source_target_pairs={{0,2},{1,3},{2,4},{3,5},{4,6},{5,7},{6,0},{7,1},{8,10},{9,11},{10,... | collective-permute-start | bytes 393224 | tf_op jit(solution)/shard_map/ppermute | solution.py:597
  19.7 29.6 %copy-start.5 = (f32[2,2]{1,0:T(2,128)S(1)}, f32[2,2]{1,0:T(2,128)}, u32[]{:S(2)}) copy-start(f32[2,2]{1,0:T(2,128)} %a_table.5) | copy-start | bytes 52
  31.0 0.6 copy-start.6
  31.6 7.1 %collective-permute-start.5 = (f32[40,128]{1,0:T(8,128)S(1)}, f32[40,128]{1,0:T(8,128)S(1)}, u32[]{:S(2)}, u32[]{:S(2)}) collective-permute-start(f32[40,128]{1,0:T(8,128)S(1)} %get-tuple-element.38), channel_id=1, source_target_pairs={{0,6},{1,7},{2,0},{3,1},{4,2},{5,3},{6,4},{7,5},{8,14},{9,15},{10,... | collective-permute-start | bytes 61448 | tf_op jit(solution)/shard_map/ppermute | solution.py:597
  33.1 5.5 %collective-permute-start.6 = (f32[32,128]{1,0:T(8,128)S(1)}, f32[32,128]{1,0:T(8,128)S(1)}, u32[]{:S(2)}, u32[]{:S(2)}) collective-permute-start(f32[32,128]{1,0:T(8,128)S(1)} %get-tuple-element.39), channel_id=1, source_target_pairs={{0,2},{1,3},{2,4},{3,5},{4,6},{5,7},{6,0},{7,1},{8,10},{9,11},{10,... | collective-permute-start | bytes 49160 | tf_op jit(solution)/shard_map/ppermute | solution.py:597
  33.6 5.1 %collective-permute-start.7 = (f32[16,128]{1,0:T(8,128)S(1)}, f32[16,128]{1,0:T(8,128)S(1)}, u32[]{:S(2)}, u32[]{:S(2)}) collective-permute-start(f32[16,128]{1,0:T(8,128)S(1)} %get-tuple-element.40), channel_id=1, source_target_pairs={{0,8},{1,9},{2,10},{3,11},{4,12},{5,13},{6,14},{7,15},{8,16},{9,17... | collective-permute-start | bytes 24584 | tf_op jit(solution)/shard_map/ppermute | solution.py:603
  38.7 1.3 %collective-permute-start.8 = (f32[48,128]{1,0:T(8,128)S(1)}, f32[48,128]{1,0:T(8,128)S(1)}, u32[]{:S(2)}, u32[]{:S(2)}) collective-permute-start(f32[48,128]{1,0:T(8,128)S(1)} %pad_maximum_fusion), channel_id=1, source_target_pairs={{0,1},{1,0},{2,3},{3,2},{4,5},{5,4},{6,7},{7,6},{8,9},{9,8},{10,11... | collective-permute-start | bytes 73736 | tf_op jit(solution)/shard_map/ppermute | solution.py:600
  40.0 9.3 %collective-permute-start.11 = (f32[32,128]{1,0:T(8,128)S(1)}, f32[32,128]{1,0:T(8,128)S(1)}, u32[]{:S(2)}, u32[]{:S(2)}) collective-permute-start(f32[32,128]{1,0:T(8,128)S(1)} %maximum_add_fusion.pair_rho), channel_id=1, source_target_pairs={{0,6},{1,7},{2,0},{3,1},{4,2},{5,3},{6,4},{7,5},{8,14},{9,15},{10,... | collective-permute-start | bytes 49160 | tf_op jit(solution)/shard_map/ppermute | solution.py:597
  42.8 3.7 %collective-permute-start.9 = (f32[16,128]{1,0:T(8,128)S(1)}, f32[16,128]{1,0:T(8,128)S(1)}, u32[]{:S(2)}, u32[]{:S(2)}) collective-permute-start(f32[16,128]{1,0:T(8,128)S(1)} %slice.68), channel_id=1, source_target_pairs={{0,24},{1,25},{2,26},{3,27},{4,28},{5,29},{6,30},{7,31},{8,0},{9,1... | collective-permute-start | bytes 24584 | tf_op jit(solution)/shard_map/ppermute | solution.py:603
  43.7 5.6 %collective-permute-start.10 = (f32[40,128]{1,0:T(8,128)S(1)}, f32[40,128]{1,0:T(8,128)S(1)}, u32[]{:S(2)}, u32[]{:S(2)}) collective-permute-start(f32[40,128]{1,0:T(8,128)S(1)} %pad_maximum_fusion.1), channel_id=1, source_target_pairs={{0,2},{1,3},{2,4},{3,5},{4,6},{5,7},{6,0},{7,1},{8,10},{9,11},{10,... | collective-permute-start | bytes 61448 | tf_op jit(solution)/shard_map/ppermute | solution.py:597
  49.3 5.2 %copy-start.1 = (f32[32,7,128,128]{3,2,1,0:T(8,128)S(1)}, f32[32,7,128,128]{3,2,1,0:T(8,128)}, u32[]{:S(2)}) copy-start(f32[32,7,128,128]{3,2,1,0:T(8,128)} %copy-done) | copy-start | bytes 44040196
  54.5 22.4 %slice-start = ((s8[14680064]{0:T(1024)(128)(4,1)}), s8[2097152]{0:T(1024)(128)(4,1)S(1)}, s32[]{:S(2)}) async-start(s8[14680064]{0:T(1024)(128)(4,1)} %bitcast.7), calls=%async_computation | async-start | bytes 4194304
  54.5 22.4 %slice-start.1 = ((s8[14680064]{0:T(1024)(128)(4,1)}), s8[4194304]{0:T(1024)(128)(4,1)S(1)}, s32[]{:S(2)}) async-start(s8[14680064]{0:T(1024)(128)(4,1)} %bitcast.7), calls=%async_computation.1 | async-start | bytes 8388608
  63.6 11.4 %collective-permute-start.12 = (f32[3,32,128]{2,1,0:T(8,128)S(1)}, f32[3,32,128]{2,1,0:T(8,128)S(1)}, u32[]{:S(2)}, u32[]{:S(2)}) collective-permute-start(f32[3,32,128]{2,1,0:T(8,128)S(1)} %get-tuple-element.45), channel_id=1, source_target_pairs={{0,6},{1,7},{2,0},{3,1},{4,2},{5,3},{6,4},{7,5},{8,14},{9,15},{10,... | collective-permute-start | bytes 147464 | tf_op jit(solution)/shard_map/ppermute | solution.py:597
  63.6 11.3 %collective-permute-start.13 = (f32[3,32,128]{2,1,0:T(8,128)S(1)}, f32[3,32,128]{2,1,0:T(8,128)S(1)}, u32[]{:S(2)}, u32[]{:S(2)}) collective-permute-start(f32[3,32,128]{2,1,0:T(8,128)S(1)} %get-tuple-element.46), channel_id=1, source_target_pairs={{0,2},{1,3},{2,4},{3,5},{4,6},{5,7},{6,0},{7,1},{8,10},{9,11},{10,... | collective-permute-start | bytes 147464 | tf_op jit(solution)/shard_map/ppermute | solution.py:597
  65.6 11.2 %slice-start.2 = ((s8[14680064]{0:T(1024)(128)(4,1)}), s8[4194304]{0:T(1024)(128)(4,1)S(1)}, s32[]{:S(2)}) async-start(s8[14680064]{0:T(1024)(128)(4,1)} %bitcast.7), calls=%async_computation.2 | async-start | bytes 8388608
  65.6 11.2 %slice-start.3 = ((s8[14680064]{0:T(1024)(128)(4,1)}), s8[4194304]{0:T(1024)(128)(4,1)S(1)}, s32[]{:S(2)}) async-start(s8[14680064]{0:T(1024)(128)(4,1)} %bitcast.7), calls=%async_computation.3 | async-start | bytes 8388608
  75.0 1.8 %collective-permute-start.15 = (f32[3,16,128]{2,1,0:T(8,128)S(1)}, f32[3,16,128]{2,1,0:T(8,128)S(1)}, u32[]{:S(2)}, u32[]{:S(2)}) collective-permute-start(f32[3,16,128]{2,1,0:T(8,128)S(1)} %slice.73), channel_id=1, source_target_pairs={{0,1},{1,0},{2,3},{3,2},{4,5},{5,4},{6,7},{7,6},{8,9},{9,8},{10,11... | collective-permute-start | bytes 73736 | tf_op jit(solution)/shard_map/ppermute | solution.py:600
  75.0 13.3 %collective-permute-start.14 = (f32[3,8,128]{2,1,0:T(8,128)S(1)}, f32[3,8,128]{2,1,0:T(8,128)S(1)}, u32[]{:S(2)}, u32[]{:S(2)}) collective-permute-start(f32[3,8,128]{2,1,0:T(8,128)S(1)} %get-tuple-element.48), channel_id=1, source_target_pairs={{0,7},{1,0},{2,1},{3,2},{4,3},{5,4},{6,5},{7,6},{8,15},{9,8},{10,9... | collective-permute-start | bytes 36872 | tf_op jit(solution)/shard_map/ppermute | solution.py:597
  76.8 11.6 %collective-permute-start.16 = (f32[3,16,128]{2,1,0:T(8,128)S(1)}, f32[3,16,128]{2,1,0:T(8,128)S(1)}, u32[]{:S(2)}, u32[]{:S(2)}) collective-permute-start(f32[3,16,128]{2,1,0:T(8,128)S(1)} %slice_add_fusion), channel_id=1, source_target_pairs={{0,24},{1,25},{2,26},{3,27},{4,28},{5,29},{6,30},{7,31},{8,0},{9,1... | collective-permute-start | bytes 73736 | tf_op jit(solution)/shard_map/ppermute | solution.py:603
  76.9 11.5 %copy-start.2 = (f32[3,4096]{1,0:T(4,128)S(1)}, f32[3,4096]{1,0:T(4,128)}, u32[]{:S(2)}) copy-start(f32[3,4096]{1,0:T(4,128)} %pos.1) | copy-start | bytes 147460
  76.9 11.5 %copy-start.3 = (f32[3,4096]{1,0:T(4,128)S(1)}, f32[3,4096]{1,0:T(4,128)}, u32[]{:S(2)}) copy-start(f32[3,4096]{1,0:T(4,128)} %vel.1) | copy-start | bytes 147460
  76.9 11.5 %copy-start.4 = (s32[32]{0:T(128)S(1)}, s32[32]{0:T(128)}, u32[]{:S(2)}) copy-start(s32[32]{0:T(128)} %counts.1) | copy-start | bytes 388

commit v5 on v4

--- a/solution.py
+++ b/solution.py
@@ -15,6 +15,7 @@
 time_step = 0.01
 distance_floor = 0.01
 far_away = 10000.0
+SIZES = (4, 5, 6, 7, 8)
 density_scale = density_norm / (cutoff_density * cutoff_density)
 crowd_scale = repulse / cutoff_density
 VMEM = pl.BlockSpec(memory_space=pltpu.VMEM)
@@ -27,7 +28,7 @@
     return jax.ShapeDtypeStruct(shape, f32)
 
 
-def params(mib=24):
+def params(mib=16):
     return pltpu.CompilerParams(vmem_limit_bytes=mib * 1024 * 1024)
 
 
@@ -128,7 +129,7 @@
 
 
 def branch(used, count, width, body):
-    sizes = (0,) + tuple(width * e // 8 for e in (4, 6, 8))
+    sizes = (0,) + tuple(width * e // 8 for e in SIZES)
     index = jnp.where(used, 1, 0)
     for n in sizes[1:-1]:
         index += jnp.where(used & (count > n), 1, 0)
@@ -423,11 +424,10 @@
     below_rho,
     above_rho,
     crowd,
-    own_out,
+    sums,
     pair_out,
     below_out,
     above_out,
-    sums,
     ghosts,
     acc,
     rho,
@@ -464,12 +464,6 @@
             reduced[pl.ds(t, 8), :] = fold(acc, t, c)
         spill(reduced, 0, pair_out.at[c], below_out.at[c], above_out.at[c])
 
-    def collect(t):
-        for c in range(3):
-            own_out[c, t] = row_sums(sums, c, t)
-
-    by_fours(tiles, collect)
-
 
 def face_force_kernel(
     columns,
@@ -478,12 +472,11 @@
     a_table,
     spread,
     crowd,
-    cross_acc,
+    cross_sums,
     face,
     face_rho,
-    own_out,
+    sums,
     face_out,
-    sums,
     ghosts,
     acc,
     counts,
@@ -492,7 +485,8 @@
 ):
     wait = fetch(sems, (counts_hbm, counts), (listed_hbm, listed))
     tiles, width = spread.shape[0], spread.shape[2]
-    zero(acc, sums)
+    zero(acc)
+    sums[...] = cross_sums[...]
     table = amplitudes(a_table)
     for t in range(ghosts.shape[0]):
         ghosts[t] = force_tile(face, face_rho[pl.ds(t, 1), :], t)
@@ -505,12 +499,6 @@
     for c in range(3):
         for t in range(0, acc.shape[1], 8):
             face_out[c, pl.ds(t, 8), :] = fold(acc, t, c)
-
-    def collect(t):
-        for c in range(3):
-            own_out[c, t] = cross_acc[c, t] + row_sums(sums, c, t)
-
-    by_fours(tiles, collect)
 
 
 def local_force_kernel(
@@ -521,7 +509,7 @@
     spread,
     crowd,
     density,
-    ghost_acc,
+    ghost_sums,
     acc,
     beads,
     sums,
@@ -532,8 +520,8 @@
     wait = fetch(sems, (counts_hbm, counts), (nbr_hbm, nbr))
     tiles, width = union.shape[0], union.shape[2]
     table = amplitudes(a_table)
-    acc[...] = ghost_acc[...]
-    zero(sums)
+    zero(acc)
+    sums[...] = ghost_sums[...]
     for t in range(tiles):
         beads[t] = force_tile(union, density[pl.ds(t, 1), :], t)
     wait()
@@ -636,14 +624,22 @@
     near = climb(top, 1)
     flip = climb(top, 1, 1)
     face_ghosts = lateral(face, 1)
-    spread = pl.pallas_call(
-        spread_kernel,
-        out_shape=sds(tiles, 7, width, width),
-        in_specs=[VMEM],
-        out_specs=VMEM,
-        cost_estimate=pl.CostEstimate(flops=10**9, bytes_accessed=15 * 10**6, transcendentals=0),
-        compiler_params=params(),
-    )(payload)
+    def spread_rows(payload, channels):
+        return pl.pallas_call(
+            spread_kernel,
+            out_shape=sds(tiles, channels, width, width),
+            in_specs=[VMEM],
+            out_specs=VMEM,
+            cost_estimate=pl.CostEstimate(
+                flops=10**9, bytes_accessed=15 * 10**6, transcendentals=0
+            ),
+            compiler_params=params(),
+        )(payload)
+
+    near = climb(top, 1)
+    flip = climb(top, 1, 1)
+    face_ghosts = lateral(face, 1)
+    spread = spread_rows(payload, 3)
     near, flip, spread = lax.optimization_barrier((near, flip, spread))
     chip_ghosts = jnp.concatenate([near, flip], axis=0)
     below = lateral(chip_ghosts, 2)
@@ -716,6 +712,9 @@
     owner_part = climb(own_top, 1)
     from_above = lateral(below_part, -2)
     from_below = lateral(above_part, 2)
+    payload, _ = lax.optimization_barrier((payload, pair_part))
+    spread = spread_rows(payload, 7)
+    from_above, from_below, spread = lax.optimization_barrier((from_above, from_below, spread))
     passed = jnp.where(odd, face_part, from_above[pairs:])
     met = pair_part + from_above[:pairs] + from_below
     met = jnp.concatenate([met[:upper] + owner_part, met[upper:]], axis=0)
@@ -730,18 +729,17 @@
     below_rho = below_rho[:pairs]
     density = jnp.concatenate([bottom_rho, own[faces : tiles - upper], top_rho], axis=0)
 
-    listed = in_hbm(listed)
     columns = face_nbr.shape[0]
     small = [
         counts_smem,
         pltpu.SMEM(listed.shape, ints),
         pltpu.SemaphoreType.DMA((2,)),
     ]
-    crowd, cross_acc, pair_force, below_force, above_force = pl.pallas_call(
+    crowd, cross_sums, pair_force, below_force, above_force = pl.pallas_call(
         functools.partial(cross_force_kernel, columns, faces),
         out_shape=(
             sds(tiles, width, width),
-            sds(3, tiles, 8, width),
+            sds(3, tiles, width, width),
             sds(3, pairs, width),
             sds(3, pairs, width),
             sds(3, pairs, width),
@@ -749,7 +747,6 @@
         in_specs=[HBM] * 2 + [SMEM] + [VMEM] * 9,
         out_specs=[VMEM] * 5,
         scratch_shapes=[
-            pltpu.VMEM((3, tiles, width, width), f32),
             pltpu.VMEM((3 * pairs, 8, width), f32),
             pltpu.VMEM((3, 3 * pairs, 8, width), f32),
             pltpu.VMEM((3 * pairs, width), f32),
@@ -773,20 +770,19 @@
     )
     from_above = lateral(below_force, -2)
     from_below = lateral(above_force, 2)
-    ghost_acc, face_force = pl.pallas_call(
+    ghost_sums, face_force = pl.pallas_call(
         functools.partial(face_force_kernel, columns),
-        out_shape=(sds(3, tiles, 8, width), sds(3, faces, width)),
+        out_shape=(sds(3, tiles, width, width), sds(3, faces, width)),
         in_specs=[HBM] * 2 + [SMEM] + [VMEM] * 5,
         out_specs=[VMEM] * 2,
         scratch_shapes=[
-            pltpu.VMEM((3, tiles, width, width), f32),
             pltpu.VMEM((faces, 8, width), f32),
             pltpu.VMEM((3, faces, 8, width), f32),
         ]
         + small,
         cost_estimate=pl.CostEstimate(flops=10**9, bytes_accessed=20 * 10**6, transcendentals=0),
         compiler_params=params(),
-    )(counts_hbm, listed, a_table, spread, crowd, cross_acc, face_ghosts, face_rho)
+    )(counts_hbm, listed, a_table, spread, crowd, cross_sums, face_ghosts, face_rho)
     from_above, from_below, face_force = lax.optimization_barrier(
         (from_above, from_below, face_force)
     )
@@ -809,7 +805,7 @@
         ],
         cost_estimate=pl.CostEstimate(flops=2 * 10**9, bytes_accessed=20 * 10**6, transcendentals=0),
         compiler_params=params(),
-    )(counts_hbm, local_nbr, a_table, payload, spread, crowd, density, ghost_acc)
+    )(counts_hbm, local_nbr, a_table, payload, spread, crowd, density, ghost_sums)
 
     return pl.pallas_call(
         finish_kernel,

time: 89.8 us -> 84.6 us (0.942)
  waiting for transfers between devices: 14.3 us -> 7 us
  starting transfers between devices: 15.2 us -> 18.8 us
  Pallas kernels: 53.3 us -> 52 us
    ppermute x10, waiting for transfers between devices: 9.93 us -> 4.24 us  [lateral(): lax.ppermute(value, 'lat', [(m, (m + by) % places) for m in range(places)])]
    pallas_call x1, Pallas kernels: 9.27 us -> 6.64 us  [on_device(): pl.pallas_call(functools.partial(face_force_kernel, columns), out_shape=(...]
    pallas_call x1 -> x2, Pallas kernels: 4.38 us -> 6.61 us  [spread_rows(): pl.pallas_call(spread_kernel, out_shape=sds(tiles, channels, width, width...]
    ppermute x5, starting transfers between devices: 2.57 us -> 4.58 us  [climb(): lax.ppermute(value, both, [(l * places + m, (l + by) % layers * places +...]
    pallas_call x1, Pallas kernels: 9.08 us -> 7.18 us  [on_device(): pl.pallas_call(functools.partial(cross_force_kernel, columns, faces), out...]
    ppermute x5, waiting for transfers between devices: 3.22 us -> 1.57 us  [climb(): lax.ppermute(value, both, [(l * places + m, (l + by) % layers * places +...]
    ppermute x10, starting transfers between devices: 12.5 us -> 14 us  [lateral(): lax.ppermute(value, 'lat', [(m, (m + by) % places) for m in range(places)])]
    unnamed x23 -> x15, local copies, waits for them, and re-layouts: 5.79 us -> 5.44 us
  transfers between devices with their start and end apart: 17 -> 17, of which waited for: 6 -> 4; matrix products, arithmetic and copies ran while one was open for 0% -> 0% of each run, Pallas kernels for 34% -> 36%
where the time goes in v5:
time: 84.6 us; the launch traced here: 84.3 us
  Pallas kernels  52 us (61%)
  starting transfers between devices  18.8 us (22%)
  waiting for transfers between devices  7 us (8%)
  local copies, waits for them, and re-layouts  5.46 us (6%)
  between operations  0.95 us (1%)
    ppermute x10, starting transfers between devices, lateral(): lax.ppermute(value, 'lat', [(m, (m + by) % places) for m in range(places)])  14 us
    pallas_call x1, Pallas kernels, on_device(): pl.pallas_call(functools.partial(ghost_density_kernel, *sizes), out_shape...  11.8 us
    pallas_call x1, Pallas kernels, on_device(): pl.pallas_call(local_force_kernel, out_shape=sds(3, tiles, 8, width), in_...  11.4 us
    pallas_call x1, Pallas kernels, on_device(): pl.pallas_call(functools.partial(cross_force_kernel, columns, faces), out...  7.18 us
    pallas_call x1, Pallas kernels, on_device(): pl.pallas_call(functools.partial(face_force_kernel, columns), out_shape=(...  6.64 us
    pallas_call x2, Pallas kernels, spread_rows(): pl.pallas_call(spread_kernel, out_shape=sds(tiles, channels, width, width...  6.61 us
    pallas_call x1, Pallas kernels, on_device(): pl.pallas_call(local_density_kernel, out_shape=(sds(tiles, 8, width), sds...  5.94 us
    unnamed x15, local copies, waits for them, and re-layouts  5.44 us
  transfers between devices with their start and end apart: 17, of which 4 were waited for; matrix products, arithmetic and copies ran while one was open for 0% of the time, Pallas kernels for 36%

profile of v5, /device:TPU:4, one launch (start us, length us, event | category | flops | bytes accessed | tf_op | source)
XLA Modules:
  0.0 84.3 jit_solution(2268845496451706438)
XLA Ops:
  0.6 1.0 %shard_map.104 = (f32[32,8,128]{2,1,0:T(8,128)S(1)}, f32[16,8,128]{2,1,0:T(8,128)S(1)}, f32[8,8,128]{2,1,0:T(8,128)S(1)}) custom-call(f32[3,4096]{1,0:T(4,128)} %pos.1, f32[3,4096]{1,0:T(4,128)} %vel.1, s32[32,128]{1,0:T(8,128)} %bitcast.7, s32[32]{0:T(128)} %counts.1, s32[5,1,12]{2,1,0:T(1,128)} %bitcast.10), custom_call_target="tpu_custom_call" | custom-call | tf_op jit(solution)/shard_map/pallas_call | solution.py:609
  1.7 1.0 %collective-permute-start.1 = (f32[16,8,128]{2,1,0:T(8,128)S(1)}, f32[16,8,128]{2,1,0:T(8,128)S(1)}, u32[]{:S(2)}, u32[]{:S(2)}) collective-permute-start(f32[16,8,128]{2,1,0:T(8,128)S(1)} %get-tuple-element.32), channel_id=1, source_target_pairs={{0,9},{1,8},{2,11},{3,10},{4,13},{5,12},{6,15},{7,14},{8,17},{9,16... | collective-permute-start | bytes 196616 | tf_op jit(solution)/shard_map/ppermute | solution.py:591
  2.7 0.6 collective-permute-start
  3.3 0.1 collective-permute-start.2
  3.3 2.2 %shard_map.105.spread = f32[32,3,128,128]{3,2,1,0:T(8,128)S(1)} custom-call(f32[32,8,128]{2,1,0:T(8,128)S(1)} %get-tuple-element.40.union), custom_call_target="tpu_custom_call" | custom-call | flops 1000000000 | bytes 15000000 | tf_op jit(solution)/shard_map/pallas_call | solution.py:628
  5.6 2.6 %copy-done = f32[32,3,128,128]{3,2,1,0:T(8,128)} copy-done((f32[32,3,128,128]{3,2,1,0:T(8,128)}, f32[32,3,128,128]{3,2,1,0:T(8,128)S(1)}, u32[]{:S(2)}) %copy-start) | copy-done | bytes 6291480
  8.2 0.0 collective-permute-done.1.flip
  8.2 0.2 collective-permute-done.near
  8.4 3.7 %collective-permute-start.4 = (f32[32,8,128]{2,1,0:T(8,128)S(1)}, f32[32,8,128]{2,1,0:T(8,128)S(1)}, u32[]{:S(2)}, u32[]{:S(2)}) collective-permute-start(f32[32,8,128]{2,1,0:T(8,128)S(1)} %constant_dynamic-update-slice_fusion), channel_id=1, source_target_pairs={{0,6},{1,7},{2,0},{3,1},{4,2},{5,3},{6,4},{7,5},{8,14},{9,15},{10,... | collective-permute-start | bytes 393224 | tf_op jit(solution)/shard_map/ppermute | solution.py:585
  12.1 0.0 collective-permute-start.3
  12.1 0.1 pad_add_fusion.where
  12.2 2.8 %copy-done.1 = f32[32,3,128,128]{3,2,1,0:T(8,128)S(1)} copy-done((f32[32,3,128,128]{3,2,1,0:T(8,128)S(1)}, f32[32,3,128,128]{3,2,1,0:T(8,128)}, u32[]{:S(2)}) %copy-start.1) | copy-done | bytes 6291480
  15.0 5.9 %shard_map.106 = (f32[32,8,128]{2,1,0:T(8,128)S(1)}, f32[32,128,128]{2,1,0:T(8,128)S(1)}) custom-call(s32[32]{0:T(128)} %counts.1, s32[2,32]{1,0:T(2,128)} %bitcast.8, f32[32,8,128]{2,1,0:T(8,128)S(1)} %get-tuple-element.40.union, f32[32,3,128,128]{3,2,1,0:T(8,128)S(1)} %copy-done.1), custom_call_target="tpu_custom_call" | custom-call | flops 1000000000 | bytes 15000000 | tf_op jit(solution)/shard_map/pallas_call | solution.py:649
  20.9 0.0 collective-permute-done.2.face
  20.9 0.0 collective-permute-done.4.above
  20.9 0.0 collective-permute-done.3.below
  21.0 11.8 %shard_map.107 = (f32[32,128]{1,0:T(8,128)S(1)}, f32[16,128]{1,0:T(8,128)S(1)}, f32[8,128]{1,0:T(8,128)S(1)}, f32[32,128]{1,0:T(8,128)S(1)}, f32[40,128]{1,0:T(8...) custom-call(s32[2]{0:T(128)S(1)} %pad_add_fusion.where, ...), custom_call_target="tpu_custom_call", output_to_operand_aliasing={{6}: (6, {})} | custom-call | tf_op jit(solution)/shard_map/pallas_call | solution.py:673
  32.7 0.1 collective-permute-start.7
  32.8 0.8 collective-permute-start.6
  33.6 3.4 %collective-permute-start.5 = (f32[40,128]{1,0:T(8,128)S(1)}, f32[40,128]{1,0:T(8,128)S(1)}, u32[]{:S(2)}, u32[]{:S(2)}) collective-permute-start(f32[40,128]{1,0:T(8,128)S(1)} %get-tuple-element.41), channel_id=1, source_target_pairs={{0,6},{1,7},{2,0},{3,1},{4,2},{5,3},{6,4},{7,5},{8,14},{9,15},{10,... | collective-permute-start | bytes 61448 | tf_op jit(solution)/shard_map/ppermute | solution.py:585
  37.0 4.4 %shard_map.108.spread = f32[32,7,128,128]{3,2,1,0:T(8,128)S(1)} custom-call(f32[32,8,128]{2,1,0:T(8,128)S(1)} %get-tuple-element.40.union), custom_call_target="tpu_custom_call" | custom-call | flops 1000000000 | bytes 15000000 | tf_op jit(solution)/shard_map/pallas_call | solution.py:628
  41.4 0.0 collective-permute-done.6
  41.4 0.0 collective-permute-done.5
  41.4 0.0 collective-permute-done.7
  41.5 0.1 collective-permute-start.8
  41.6 1.2 %collective-permute-done.8 = f32[48,128]{1,0:T(8,128)S(1)} collective-permute-done((f32[48,128]{1,0:T(8,128)S(1)}, f32[48,128]{1,0:T(8,128)S(1)}, u32[]{:S(2)}, u32[]{:S(2)}) %collective-permute-start.8) | collective-permute-done | bytes 24608 | tf_op jit(solution)/shard_map/ppermute | solution.py:588
  42.7 2.0 %collective-permute-start.11 = (f32[32,128]{1,0:T(8,128)S(1)}, f32[32,128]{1,0:T(8,128)S(1)}, u32[]{:S(2)}, u32[]{:S(2)}) collective-permute-start(f32[32,128]{1,0:T(8,128)S(1)} %maximum_add_fusion.pair_rho), channel_id=1, source_target_pairs={{0,6},{1,7},{2,0},{3,1},{4,2},{5,3},{6,4},{7,5},{8,14},{9,15},{10,... | collective-permute-start | bytes 49160 | tf_op jit(solution)/shard_map/ppermute | solution.py:585
  44.7 2.9 %collective-permute-start.9 = (f32[16,128]{1,0:T(8,128)S(1)}, f32[16,128]{1,0:T(8,128)S(1)}, u32[]{:S(2)}, u32[]{:S(2)}) collective-permute-start(f32[16,128]{1,0:T(8,128)S(1)} %slice.66), channel_id=1, source_target_pairs={{0,24},{1,25},{2,26},{3,27},{4,28},{5,29},{6,30},{7,31},{8,0},{9,1... | collective-permute-start | bytes 24584 | tf_op jit(solution)/shard_map/ppermute | solution.py:591
  47.6 0.0 collective-permute-start.10
  47.6 1.4 %collective-permute-done.9 = f32[16,128]{1,0:T(8,128)S(1)} collective-permute-done((f32[16,128]{1,0:T(8,128)S(1)}, f32[16,128]{1,0:T(8,128)S(1)}, u32[]{:S(2)}, u32[]{:S(2)}) %collective-permute-start.9) | collective-permute-done | bytes 8224 | tf_op jit(solution)/shard_map/ppermute | solution.py:591
  49.0 4.2 %collective-permute-done.10 = f32[40,128]{1,0:T(8,128)S(1)} collective-permute-done((f32[40,128]{1,0:T(8,128)S(1)}, f32[40,128]{1,0:T(8,128)S(1)}, u32[]{:S(2)}, u32[]{:S(2)}) %collective-permute-start.10) | collective-permute-done | bytes 20512 | tf_op jit(solution)/shard_map/ppermute | solution.py:585
  53.2 0.0 collective-permute-done.11.above_rho
  53.2 7.2 %shard_map.109 = (f32[32,128,128]{2,1,0:T(8,128)S(1)}, f32[3,32,128,128]{3,2,1,0:T(8,128)S(1)}, f32[3,32,128]{2,1,0:T(8,128)S(1)}, f32[3,32,128]{2,1,0:T(8,128)S(1)}, f32[3,32,128]{2,1,0:T(8,128)S(1)}) custom-call(s32[32]{0:T(128)} %counts.1, s32[4,32]{1,0:T(4,128)S(1)} %get-tuple-element.44.listed_hbm, f32[2,2]{1,0:T(2,128)S(1)} %copy-done.6, ...), custom_call_target="tpu_custom_call" | custom-call | tf_op jit(solution)/shard_map/pallas_call | solution.py:738
  60.4 0.1 collective-permute-start.12
  60.5 2.0 %collective-permute-start.13 = (f32[3,32,128]{2,1,0:T(8,128)S(1)}, f32[3,32,128]{2,1,0:T(8,128)S(1)}, u32[]{:S(2)}, u32[]{:S(2)}) collective-permute-start(f32[3,32,128]{2,1,0:T(8,128)S(1)} %get-tuple-element.54), channel_id=1, source_target_pairs={{0,2},{1,3},{2,4},{3,5},{4,6},{5,7},{6,0},{7,1},{8,10},{9,11},{10,... | collective-permute-start | bytes 147464 | tf_op jit(solution)/shard_map/ppermute | solution.py:585
  62.5 6.6 %shard_map.110 = (f32[3,32,128,128]{3,2,1,0:T(8,128)S(1)}, f32[3,8,128]{2,1,0:T(8,128)S(1)}) custom-call(s32[32]{0:T(128)} %counts.1, s32[4,32]{1,0:T(4,128)S(1)} %get-tuple-element.44.listed_hbm, f32[2,2]{1,0:T(2,128)S(1)} %copy-done.6, f32[32,7,128,128]{3,2,1,0:T(8,128)S(1)} %shard_map.108.spread, f32[32,128,128]{2,1,0:T(8,128)S(1)} %get-tuple-element.50.crowd, ...), custom_call_target="tpu_custom_call" | custom-call | flops 1000000000 | bytes 20000000 | tf_op jit(solution)/shard_map/pallas_call | solution.py:773
  69.1 0.0 collective-permute-done.13
  69.2 0.1 collective-permute-start.15
  69.3 2.1 %collective-permute-start.14 = (f32[3,8,128]{2,1,0:T(8,128)S(1)}, f32[3,8,128]{2,1,0:T(8,128)S(1)}, u32[]{:S(2)}, u32[]{:S(2)}) collective-permute-start(f32[3,8,128]{2,1,0:T(8,128)S(1)} %get-tuple-element.56), channel_id=1, source_target_pairs={{0,7},{1,0},{2,1},{3,2},{4,3},{5,4},{6,5},{7,6},{8,15},{9,8},{10,9... | collective-permute-start | bytes 36872 | tf_op jit(solution)/shard_map/ppermute | solution.py:585
  71.3 0.0 collective-permute-done.15
  71.3 0.1 collective-permute-start.16
  71.4 0.0 copy-start.3
  71.4 0.0 copy-start.4
  71.4 0.0 copy-start.5
  71.4 11.4 %shard_map.111.acc = f32[3,32,8,128]{3,2,1,0:T(8,128)S(1)} custom-call(s32[32]{0:T(128)} %counts.1, s32[2,32]{1,0:T(2,128)} %bitcast.9, f32[2,2]{1,0:T(2,128)S(1)} %copy-done.6, f32[32,8,128]{2,1,0:T(8,128)S(1)} %get-tuple-element.40.union, f32[32,7,128,128]{3,2,1,0:T(8,128)S(1)} %shard_map.108.spread, f32[32,128,128]{2,1,0:T(8,128)S(1)} %get-tuple-element.50.crowd, ...), custom_call_target="tpu_custom_call" | custom-call | flops 2000000000 | bytes 20000000 | tf_op jit(solution)/shard_map/pallas_call | solution.py:794
  82.9 0.0 collective-permute-done.14.face_back
  82.9 0.0 collective-permute-done.16.top_back
  82.9 1.4 %shard_map.112 = (f32[3,4096]{1,0:T(4,128)}, f32[3,4096]{1,0:T(4,128)}) custom-call(s32[32]{0:T(128)S(1)} %copy-done.5, f32[3,4096]{1,0:T(4,128)S(1)} %copy-done.3, f32[3,4096]{1,0:T(4,128)S(1)} %copy-done.4, f32[3,32,8,128]{3,2,1,0:T(8,128)S(1)} %shard_map.111.acc, f32[3,8,128]{2,1,0:T(8,128)S(1)} %collective-permute-done.14.face_back, ...), custom_call_target="tpu_custom_call" | custom-call | tf_op jit(solution)/shard_map/pallas_call | solution.py:810
  (28 shorter events, 0.1 us)
Async XLA Ops:
  1.7 6.5 %collective-permute-start.1 = (f32[16,8,128]{2,1,0:T(8,128)S(1)}, f32[16,8,128]{2,1,0:T(8,128)S(1)}, u32[]{:S(2)}, u32[]{:S(2)}) collective-permute-start(f32[16,8,128]{2,1,0:T(8,128)S(1)} %get-tuple-element.32), channel_id=1, source_target_pairs={{0,9},{1,8},{2,11},{3,10},{4,13},{5,12},{6,15},{7,14},{8,17},{9,16... | collective-permute-start | bytes 196616 | tf_op jit(solution)/shard_map/ppermute | solution.py:591
  2.7 5.8 %collective-permute-start = (f32[16,8,128]{2,1,0:T(8,128)S(1)}, f32[16,8,128]{2,1,0:T(8,128)S(1)}, u32[]{:S(2)}, u32[]{:S(2)}) collective-permute-start(f32[16,8,128]{2,1,0:T(8,128)S(1)} %get-tuple-element.32), channel_id=1, source_target_pairs={{0,8},{1,9},{2,10},{3,11},{4,12},{5,13},{6,14},{7,15},{8,16},{9,17... | collective-permute-start | bytes 196616 | tf_op jit(solution)/shard_map/ppermute | solution.py:591
  3.3 17.6 %collective-permute-start.2 = (f32[8,8,128]{2,1,0:T(8,128)S(1)}, f32[8,8,128]{2,1,0:T(8,128)S(1)}, u32[]{:S(2)}, u32[]{:S(2)}) collective-permute-start(f32[8,8,128]{2,1,0:T(8,128)S(1)} %get-tuple-element.36), channel_id=1, source_target_pairs={{0,1},{1,2},{2,3},{3,4},{4,5},{5,6},{6,7},{7,0},{8,9},{9,10},{10,1... | collective-permute-start | bytes 98312 | tf_op jit(solution)/shard_map/ppermute | solution.py:585
  5.6 2.6 %copy-start = (f32[32,3,128,128]{3,2,1,0:T(8,128)}, f32[32,3,128,128]{3,2,1,0:T(8,128)S(1)}, u32[]{:S(2)}) copy-start(f32[32,3,128,128]{3,2,1,0:T(8,128)S(1)} %shard_map.105.spread) | copy-start | bytes 18874372
  8.4 12.5 %collective-permute-start.4 = (f32[32,8,128]{2,1,0:T(8,128)S(1)}, f32[32,8,128]{2,1,0:T(8,128)S(1)}, u32[]{:S(2)}, u32[]{:S(2)}) collective-permute-start(f32[32,8,128]{2,1,0:T(8,128)S(1)} %constant_dynamic-update-slice_fusion), channel_id=1, source_target_pairs={{0,6},{1,7},{2,0},{3,1},{4,2},{5,3},{6,4},{7,5},{8,14},{9,15},{10,... | collective-permute-start | bytes 393224 | tf_op jit(solution)/shard_map/ppermute | solution.py:585
  12.1 8.8 %collective-permute-start.3 = (f32[32,8,128]{2,1,0:T(8,128)S(1)}, f32[32,8,128]{2,1,0:T(8,128)S(1)}, u32[]{:S(2)}, u32[]{:S(2)}) collective-permute-start(f32[32,8,128]{2,1,0:T(8,128)S(1)} %constant_dynamic-update-slice_fusion), channel_id=1, source_target_pairs={{0,2},{1,3},{2,4},{3,5},{4,6},{5,7},{6,0},{7,1},{8,10},{9,11},{10,... | collective-permute-start | bytes 393224 | tf_op jit(solution)/shard_map/ppermute | solution.py:585
  12.2 2.8 %copy-start.1 = (f32[32,3,128,128]{3,2,1,0:T(8,128)S(1)}, f32[32,3,128,128]{3,2,1,0:T(8,128)}, u32[]{:S(2)}) copy-start(f32[32,3,128,128]{3,2,1,0:T(8,128)} %copy-done) | copy-start | bytes 18874372
  15.0 6.0 %copy-start.2 = (f32[32,3,128,128]{3,2,1,0:T(8,128)S(1)}, f32[32,3,128,128]{3,2,1,0:T(8,128)}, u32[]{:S(2)}) copy-start(f32[32,3,128,128]{3,2,1,0:T(8,128)} %copy-done) | copy-start | bytes 18874372
  32.7 8.7 %collective-permute-start.7 = (f32[16,128]{1,0:T(8,128)S(1)}, f32[16,128]{1,0:T(8,128)S(1)}, u32[]{:S(2)}, u32[]{:S(2)}) collective-permute-start(f32[16,128]{1,0:T(8,128)S(1)} %get-tuple-element.48), channel_id=1, source_target_pairs={{0,8},{1,9},{2,10},{3,11},{4,12},{5,13},{6,14},{7,15},{8,16},{9,17... | collective-permute-start | bytes 24584 | tf_op jit(solution)/shard_map/ppermute | solution.py:591
  32.8 8.6 %collective-permute-start.6 = (f32[32,128]{1,0:T(8,128)S(1)}, f32[32,128]{1,0:T(8,128)S(1)}, u32[]{:S(2)}, u32[]{:S(2)}) collective-permute-start(f32[32,128]{1,0:T(8,128)S(1)} %get-tuple-element.42), channel_id=1, source_target_pairs={{0,2},{1,3},{2,4},{3,5},{4,6},{5,7},{6,0},{7,1},{8,10},{9,11},{10,... | collective-permute-start | bytes 49160 | tf_op jit(solution)/shard_map/ppermute | solution.py:585
  33.6 19.6 %copy-start.6 = (f32[2,2]{1,0:T(2,128)S(1)}, f32[2,2]{1,0:T(2,128)}, u32[]{:S(2)}) copy-start(f32[2,2]{1,0:T(2,128)} %a_table.5) | copy-start | bytes 52
  33.6 7.8 %collective-permute-start.5 = (f32[40,128]{1,0:T(8,128)S(1)}, f32[40,128]{1,0:T(8,128)S(1)}, u32[]{:S(2)}, u32[]{:S(2)}) collective-permute-start(f32[40,128]{1,0:T(8,128)S(1)} %get-tuple-element.41), channel_id=1, source_target_pairs={{0,6},{1,7},{2,0},{3,1},{4,2},{5,3},{6,4},{7,5},{8,14},{9,15},{10,... | collective-permute-start | bytes 61448 | tf_op jit(solution)/shard_map/ppermute | solution.py:585
  41.5 1.3 %collective-permute-start.8 = (f32[48,128]{1,0:T(8,128)S(1)}, f32[48,128]{1,0:T(8,128)S(1)}, u32[]{:S(2)}, u32[]{:S(2)}) collective-permute-start(f32[48,128]{1,0:T(8,128)S(1)} %pad_maximum_fusion), channel_id=1, source_target_pairs={{0,1},{1,0},{2,3},{3,2},{4,5},{5,4},{6,7},{7,6},{8,9},{9,8},{10,11... | collective-permute-start | bytes 73736 | tf_op jit(solution)/shard_map/ppermute | solution.py:588
  42.7 10.5 %collective-permute-start.11 = (f32[32,128]{1,0:T(8,128)S(1)}, f32[32,128]{1,0:T(8,128)S(1)}, u32[]{:S(2)}, u32[]{:S(2)}) collective-permute-start(f32[32,128]{1,0:T(8,128)S(1)} %maximum_add_fusion.pair_rho), channel_id=1, source_target_pairs={{0,6},{1,7},{2,0},{3,1},{4,2},{5,3},{6,4},{7,5},{8,14},{9,15},{10,... | collective-permute-start | bytes 49160 | tf_op jit(solution)/shard_map/ppermute | solution.py:585
  44.7 4.2 %collective-permute-start.9 = (f32[16,128]{1,0:T(8,128)S(1)}, f32[16,128]{1,0:T(8,128)S(1)}, u32[]{:S(2)}, u32[]{:S(2)}) collective-permute-start(f32[16,128]{1,0:T(8,128)S(1)} %slice.66), channel_id=1, source_target_pairs={{0,24},{1,25},{2,26},{3,27},{4,28},{5,29},{6,30},{7,31},{8,0},{9,1... | collective-permute-start | bytes 24584 | tf_op jit(solution)/shard_map/ppermute | solution.py:591
  47.6 5.6 %collective-permute-start.10 = (f32[40,128]{1,0:T(8,128)S(1)}, f32[40,128]{1,0:T(8,128)S(1)}, u32[]{:S(2)}, u32[]{:S(2)}) collective-permute-start(f32[40,128]{1,0:T(8,128)S(1)} %pad_maximum_fusion.1), channel_id=1, source_target_pairs={{0,2},{1,3},{2,4},{3,5},{4,6},{5,7},{6,0},{7,1},{8,10},{9,11},{10,... | collective-permute-start | bytes 61448 | tf_op jit(solution)/shard_map/ppermute | solution.py:585
  60.4 8.7 %collective-permute-start.12 = (f32[3,32,128]{2,1,0:T(8,128)S(1)}, f32[3,32,128]{2,1,0:T(8,128)S(1)}, u32[]{:S(2)}, u32[]{:S(2)}) collective-permute-start(f32[3,32,128]{2,1,0:T(8,128)S(1)} %get-tuple-element.53), channel_id=1, source_target_pairs={{0,6},{1,7},{2,0},{3,1},{4,2},{5,3},{6,4},{7,5},{8,14},{9,15},{10,... | collective-permute-start | bytes 147464 | tf_op jit(solution)/shard_map/ppermute | solution.py:585
  60.5 8.7 %collective-permute-start.13 = (f32[3,32,128]{2,1,0:T(8,128)S(1)}, f32[3,32,128]{2,1,0:T(8,128)S(1)}, u32[]{:S(2)}, u32[]{:S(2)}) collective-permute-start(f32[3,32,128]{2,1,0:T(8,128)S(1)} %get-tuple-element.54), channel_id=1, source_target_pairs={{0,2},{1,3},{2,4},{3,5},{4,6},{5,7},{6,0},{7,1},{8,10},{9,11},{10,... | collective-permute-start | bytes 147464 | tf_op jit(solution)/shard_map/ppermute | solution.py:585
  69.2 2.2 %collective-permute-start.15 = (f32[3,16,128]{2,1,0:T(8,128)S(1)}, f32[3,16,128]{2,1,0:T(8,128)S(1)}, u32[]{:S(2)}, u32[]{:S(2)}) collective-permute-start(f32[3,16,128]{2,1,0:T(8,128)S(1)} %slice.71), channel_id=1, source_target_pairs={{0,1},{1,0},{2,3},{3,2},{4,5},{5,4},{6,7},{7,6},{8,9},{9,8},{10,11... | collective-permute-start | bytes 73736 | tf_op jit(solution)/shard_map/ppermute | solution.py:588
  69.3 13.6 %collective-permute-start.14 = (f32[3,8,128]{2,1,0:T(8,128)S(1)}, f32[3,8,128]{2,1,0:T(8,128)S(1)}, u32[]{:S(2)}, u32[]{:S(2)}) collective-permute-start(f32[3,8,128]{2,1,0:T(8,128)S(1)} %get-tuple-element.56), channel_id=1, source_target_pairs={{0,7},{1,0},{2,1},{3,2},{4,3},{5,4},{6,5},{7,6},{8,15},{9,8},{10,9... | collective-permute-start | bytes 36872 | tf_op jit(solution)/shard_map/ppermute | solution.py:585
  71.3 11.6 %collective-permute-start.16 = (f32[3,16,128]{2,1,0:T(8,128)S(1)}, f32[3,16,128]{2,1,0:T(8,128)S(1)}, u32[]{:S(2)}, u32[]{:S(2)}) collective-permute-start(f32[3,16,128]{2,1,0:T(8,128)S(1)} %slice_add_fusion), channel_id=1, source_target_pairs={{0,24},{1,25},{2,26},{3,27},{4,28},{5,29},{6,30},{7,31},{8,0},{9,1... | collective-permute-start | bytes 73736 | tf_op jit(solution)/shard_map/ppermute | solution.py:591
  71.4 11.5 %copy-start.3 = (f32[3,4096]{1,0:T(4,128)S(1)}, f32[3,4096]{1,0:T(4,128)}, u32[]{:S(2)}) copy-start(f32[3,4096]{1,0:T(4,128)} %pos.1) | copy-start | bytes 147460
  71.4 11.5 %copy-start.4 = (f32[3,4096]{1,0:T(4,128)S(1)}, f32[3,4096]{1,0:T(4,128)}, u32[]{:S(2)}) copy-start(f32[3,4096]{1,0:T(4,128)} %vel.1) | copy-start | bytes 147460
  71.4 11.5 %copy-start.5 = (s32[32]{0:T(128)S(1)}, s32[32]{0:T(128)}, u32[]{:S(2)}) copy-start(s32[32]{0:T(128)} %counts.1) | copy-start | bytes 388

commit v6 on v5

--- a/solution.py
+++ b/solution.py
@@ -15,7 +15,8 @@
 time_step = 0.01
 distance_floor = 0.01
 far_away = 10000.0
-SIZES = (4, 5, 6, 7, 8)
+DENSITY_SIZES = (8,)
+FORCE_SIZES = (5, 8)
 density_scale = density_norm / (cutoff_density * cutoff_density)
 crowd_scale = repulse / cutoff_density
 VMEM = pl.BlockSpec(memory_space=pltpu.VMEM)
@@ -128,8 +129,8 @@
     return parts[0]
 
 
-def branch(used, count, width, body):
-    sizes = (0,) + tuple(width * e // 8 for e in SIZES)
+def branch(used, count, width, eighths, body):
+    sizes = (0,) + tuple(width * e // 8 for e in eighths)
     index = jnp.where(used, 1, 0)
     for n in sizes[1:-1]:
         index += jnp.where(used & (count > n), 1, 0)
@@ -151,7 +152,7 @@
     pick(0, len(sizes) - 1)
 
 
-def tile_loop(tiles, width, counts, slots, partner, pair):
+def tile_loop(tiles, width, counts, slots, eighths, partner, pair):
     def step(g, carry):
         count = counts[g]
         listed = [partner(g, k) for k in range(slots)]
@@ -161,7 +162,7 @@
                 if n:
                     pair(g, k, h, n)
 
-            branch(used & (count > 0), count, width, body)
+            branch(used & (count > 0), count, width, eighths, body)
         return carry
 
     lax.fori_loop(0, tiles, step, 0)
@@ -217,8 +218,9 @@
         ref[...] = jnp.zeros_like(ref)
 
 
-def spread_kernel(union, spread):
+def spread_kernel(union, spread, token):
     tiles = union.shape[0]
+    zero(token)
 
     def fill(g):
         for c in range(spread.shape[1]):
@@ -257,7 +259,9 @@
         mine = lambda c, r: spread[g, c, pl.ds(r, 8), :]
         density_pair(mine, union, h, n, acc, sums if k else None, g)
 
-    tile_loop(tiles, width, counts, 1 + nbr.shape[0], local_partner(counts, nbr), pair)
+    tile_loop(
+        tiles, width, counts, 1 + nbr.shape[0], DENSITY_SIZES, local_partner(counts, nbr), pair
+    )
 
 
 def gather(target, *refs):
@@ -364,7 +368,7 @@
         mine = lambda c, r: spread[g, c, pl.ds(r, 8), :]
         density_pair(mine, ghosts, h, n, acc, sums, g)
 
-    tile_loop(tiles, width, counts, slots, partner, pair)
+    tile_loop(tiles, width, counts, slots, DENSITY_SIZES, partner, pair)
     for t in range(0, acc.shape[0], 8):
         reduced[pl.ds(t, 8), :] = fold(acc, t)
     face_out[...] = reduced[pl.ds(0, faces)]
@@ -458,7 +462,7 @@
         force_pair(force_mine(spread, crowd, g), ghosts, h, n, table, acc, sums, g)
 
     partner = listed_partner(listed, columns, faces)
-    tile_loop(tiles, width, counts, listed.shape[0] - columns, partner, pair)
+    tile_loop(tiles, width, counts, listed.shape[0] - columns, FORCE_SIZES, partner, pair)
     for c in range(3):
         for t in range(0, acc.shape[1], 8):
             reduced[pl.ds(t, 8), :] = fold(acc, t, c)
@@ -495,7 +499,7 @@
     def pair(g, k, h, n):
         force_pair(force_mine(spread, crowd, g), ghosts, h, n, table, acc, sums, g)
 
-    tile_loop(tiles, width, counts, columns, listed_partner(listed, 0, 0), pair)
+    tile_loop(tiles, width, counts, columns, FORCE_SIZES, listed_partner(listed, 0, 0), pair)
     for c in range(3):
         for t in range(0, acc.shape[1], 8):
             face_out[c, pl.ds(t, 8), :] = fold(acc, t, c)
@@ -529,7 +533,9 @@
     def pair(g, k, h, n):
         force_pair(force_mine(spread, crowd, g), beads, h, n, table, acc, sums if k else None, g)
 
-    tile_loop(tiles, width, counts, 1 + nbr.shape[0], local_partner(counts, nbr), pair)
+    tile_loop(
+        tiles, width, counts, 1 + nbr.shape[0], FORCE_SIZES, local_partner(counts, nbr), pair
+    )
 
     def collect(t):
         for c in range(3):
@@ -627,9 +633,9 @@
     def spread_rows(payload, channels):
         return pl.pallas_call(
             spread_kernel,
-            out_shape=sds(tiles, channels, width, width),
+            out_shape=(sds(tiles, channels, width, width), sds(8, width)),
             in_specs=[VMEM],
-            out_specs=VMEM,
+            out_specs=[VMEM] * 2,
             cost_estimate=pl.CostEstimate(
                 flops=10**9, bytes_accessed=15 * 10**6, transcendentals=0
             ),
@@ -639,7 +645,7 @@
     near = climb(top, 1)
     flip = climb(top, 1, 1)
     face_ghosts = lateral(face, 1)
-    spread = spread_rows(payload, 3)
+    spread, token = spread_rows(payload, 3)
     near, flip, spread = lax.optimization_barrier((near, flip, spread))
     chip_ghosts = jnp.concatenate([near, flip], axis=0)
     below = lateral(chip_ghosts, 2)
@@ -713,12 +719,12 @@
     from_above = lateral(below_part, -2)
     from_below = lateral(above_part, 2)
     payload, _ = lax.optimization_barrier((payload, pair_part))
-    spread = spread_rows(payload, 7)
-    from_above, from_below, spread = lax.optimization_barrier((from_above, from_below, spread))
+    spread, token = spread_rows(payload, 7)
     passed = jnp.where(odd, face_part, from_above[pairs:])
     met = pair_part + from_above[:pairs] + from_below
     met = jnp.concatenate([met[:upper] + owner_part, met[upper:]], axis=0)
     other = swap(jnp.concatenate([met, passed, own[:faces]], axis=0))
+    other, spread = lax.optimization_barrier((other, spread))
     pair_rho = met + jnp.concatenate([other[upper:pairs], other[:upper]], axis=0)
     bottom_rho = own[:faces] + other[pairs : pairs + faces]
     other_rho = passed + other[pairs + faces :]

time: 84.6 us -> 79.3 us (0.937)
  waiting for transfers between devices: 7 us -> 15.7 us
  local copies, waits for them, and re-layouts: 5.46 us -> 0.05 us
  starting transfers between devices: 18.8 us -> 14.1 us
  Pallas kernels: 52 us -> 48 us
    unnamed x15 -> x9, local copies, waits for them, and re-layouts: 5.44 us -> 0.03 us
    ppermute x10, waiting for transfers between devices: 4.24 us -> 9.56 us  [lateral(): lax.ppermute(value, 'lat', [(m, (m + by) % places) for m in range(places)])]
    ppermute x5, waiting for transfers between devices: 1.57 us -> 6.17 us  [climb(): lax.ppermute(value, both, [(l * places + m, (l + by) % layers * places +...]
    ppermute x5, starting transfers between devices: 4.58 us -> 1.67 us  [climb(): lax.ppermute(value, both, [(l * places + m, (l + by) % layers * places +...]
    pallas_call x1, Pallas kernels: 11.8 us -> 9.77 us  [on_device(): pl.pallas_call(functools.partial(ghost_density_kernel, *sizes), out_shape...]
    ppermute x10, starting transfers between devices: 14 us -> 12.3 us  [lateral(): lax.ppermute(value, 'lat', [(m, (m + by) % places) for m in range(places)])]
    pallas_call x1, Pallas kernels: 5.94 us -> 4.29 us  [on_device(): pl.pallas_call(local_density_kernel, out_shape=(sds(tiles, 8, width), sds...]
    ppermute x2, waiting for transfers between devices: 1.18 us -> 0.01 us  [swap(): return lax.ppermute(value, 'lat', [(m, m ^ 1) for m in range(places)])]
  transfers between devices with their start and end apart: 17 -> 17, of which waited for: 4 -> 6; matrix products, arithmetic and copies ran while one was open for 0% -> 0% of each run, Pallas kernels for 36% -> 37%
where the time goes in v6:
time: 79.3 us; the launch traced here: 78.9 us
  Pallas kernels  48 us (61%)
  waiting for transfers between devices  15.7 us (20%)
  starting transfers between devices  14.1 us (18%)
  between operations  0.9 us (1%)
    ppermute x10, starting transfers between devices, lateral(): lax.ppermute(value, 'lat', [(m, (m + by) % places) for m in range(places)])  12.3 us
    pallas_call x1, Pallas kernels, on_device(): pl.pallas_call(local_force_kernel, out_shape=sds(3, tiles, 8, width), in_...  11.2 us
    pallas_call x1, Pallas kernels, on_device(): pl.pallas_call(functools.partial(ghost_density_kernel, *sizes), out_shape...  9.77 us
    ppermute x10, waiting for transfers between devices, lateral(): lax.ppermute(value, 'lat', [(m, (m + by) % places) for m in range(places)])  9.56 us
    pallas_call x2, Pallas kernels, spread_rows(): pl.pallas_call(spread_kernel, out_shape=(sds(tiles, channels, width, widt...  6.99 us
    pallas_call x1, Pallas kernels, on_device(): pl.pallas_call(functools.partial(face_force_kernel, columns), out_shape=(...  6.68 us
    pallas_call x1, Pallas kernels, on_device(): pl.pallas_call(functools.partial(cross_force_kernel, columns, faces), out...  6.67 us
    ppermute x5, waiting for transfers between devices, climb(): lax.ppermute(value, both, [(l * places + m, (l + by) % layers * places +...  6.17 us
  transfers between devices with their start and end apart: 17, of which 6 were waited for; matrix products, arithmetic and copies ran while one was open for 0% of the time, Pallas kernels for 37%

profile of v6, /device:TPU:4, one launch (start us, length us, event | category | flops | bytes accessed | tf_op | source)
XLA Modules:
  0.0 78.9 jit_solution(3539432950164136019)
XLA Ops:
  0.6 1.0 %shard_map.104 = (f32[32,8,128]{2,1,0:T(8,128)S(1)}, f32[16,8,128]{2,1,0:T(8,128)S(1)}, f32[8,8,128]{2,1,0:T(8,128)S(1)}) custom-call(f32[3,4096]{1,0:T(4,128)} %pos.1, f32[3,4096]{1,0:T(4,128)} %vel.1, s32[32,128]{1,0:T(8,128)} %bitcast.7, s32[32]{0:T(128)} %counts.1, s32[5,1,12]{2,1,0:T(1,128)} %bitcast.10), custom_call_target="tpu_custom_call" | custom-call | tf_op jit(solution)/shard_map/pallas_call | solution.py:615
  1.7 1.0 %collective-permute-start.1 = (f32[16,8,128]{2,1,0:T(8,128)S(1)}, f32[16,8,128]{2,1,0:T(8,128)S(1)}, u32[]{:S(2)}, u32[]{:S(2)}) collective-permute-start(f32[16,8,128]{2,1,0:T(8,128)S(1)} %get-tuple-element.33), channel_id=1, source_target_pairs={{0,9},{1,8},{2,11},{3,10},{4,13},{5,12},{6,15},{7,14},{8,17},{9,16... | collective-permute-start | bytes 196616 | tf_op jit(solution)/shard_map/ppermute | solution.py:597
  2.7 0.6 collective-permute-start
  3.3 0.1 collective-permute-start.2
  3.3 2.6 %shard_map.105 = (f32[32,3,128,128]{3,2,1,0:T(8,128)S(1)}, f32[8,128]{1,0:T(8,128)}) custom-call(f32[32,8,128]{2,1,0:T(8,128)S(1)} %get-tuple-element.42.union), custom_call_target="tpu_custom_call" | custom-call | flops 1000000000 | bytes 15000000 | tf_op jit(solution)/shard_map/pallas_call | solution.py:634
  5.9 1.1 %collective-permute-done.1.flip = f32[16,8,128]{2,1,0:T(8,128)S(1)} collective-permute-done((f32[16,8,128]{2,1,0:T(8,128)S(1)}, f32[16,8,128]{2,1,0:T(8,128)S(1)}, u32[]{:S(2)}, u32[]{:S(2)}) %collective-permute-start.1) | collective-permute-done | bytes 65568 | tf_op jit(solution)/shard_map/ppermute | solution.py:597
  7.0 1.4 %collective-permute-done.near = f32[16,8,128]{2,1,0:T(8,128)S(1)} collective-permute-done((f32[16,8,128]{2,1,0:T(8,128)S(1)}, f32[16,8,128]{2,1,0:T(8,128)S(1)}, u32[]{:S(2)}, u32[]{:S(2)}) %collective-permute-start) | collective-permute-done | bytes 65568 | tf_op jit(solution)/shard_map/ppermute | solution.py:597
  8.4 3.7 %collective-permute-start.4 = (f32[32,8,128]{2,1,0:T(8,128)S(1)}, f32[32,8,128]{2,1,0:T(8,128)S(1)}, u32[]{:S(2)}, u32[]{:S(2)}) collective-permute-start(f32[32,8,128]{2,1,0:T(8,128)S(1)} %constant_dynamic-update-slice_fusion), channel_id=1, source_target_pairs={{0,6},{1,7},{2,0},{3,1},{4,2},{5,3},{6,4},{7,5},{8,14},{9,15},{10,... | collective-permute-start | bytes 393224 | tf_op jit(solution)/shard_map/ppermute | solution.py:591
  12.1 0.0 collective-permute-start.3
  12.1 0.1 pad_add_fusion.where
  12.2 4.3 %shard_map.106 = (f32[32,8,128]{2,1,0:T(8,128)S(1)}, f32[32,128,128]{2,1,0:T(8,128)S(1)}) custom-call(s32[32]{0:T(128)} %counts.1, s32[2,32]{1,0:T(2,128)} %bitcast.8, f32[32,8,128]{2,1,0:T(8,128)S(1)} %get-tuple-element.42.union, f32[32,3,128,128]{3,2,1,0:T(8,128)S(1)} %get-tuple-element.35.spread), custom_call_target="tpu_custom_call" | custom-call | flops 1000000000 | bytes 15000000 | tf_op jit(solution)/shard_map/pallas_call | solution.py:655
  16.5 0.0 collective-permute-done.2.face
  16.5 0.0 collective-permute-done.4.above
  16.5 2.5 %collective-permute-done.3.below = f32[32,8,128]{2,1,0:T(8,128)S(1)} collective-permute-done((f32[32,8,128]{2,1,0:T(8,128)S(1)}, f32[32,8,128]{2,1,0:T(8,128)S(1)}, u32[]{:S(2)}, u32[]{:S(2)}) %collective-permute-start.3) | collective-permute-done | bytes 131104 | tf_op jit(solution)/shard_map/ppermute | solution.py:591
  19.0 9.8 %shard_map.107 = (f32[32,128]{1,0:T(8,128)S(1)}, f32[16,128]{1,0:T(8,128)S(1)}, f32[8,128]{1,0:T(8,128)S(1)}, f32[32,128]{1,0:T(8,128)S(1)}, f32[40,128]{1,0:T(8...) custom-call(s32[2]{0:T(128)S(1)} %pad_add_fusion.where, ...), custom_call_target="tpu_custom_call", output_to_operand_aliasing={{6}: (6, {})} | custom-call | tf_op jit(solution)/shard_map/pallas_call | solution.py:679
  28.7 1.7 %collective-permute-start.5 = (f32[40,128]{1,0:T(8,128)S(1)}, f32[40,128]{1,0:T(8,128)S(1)}, u32[]{:S(2)}, u32[]{:S(2)}) collective-permute-start(f32[40,128]{1,0:T(8,128)S(1)} %get-tuple-element.43), channel_id=1, source_target_pairs={{0,6},{1,7},{2,0},{3,1},{4,2},{5,3},{6,4},{7,5},{8,14},{9,15},{10,... | collective-permute-start | bytes 61448 | tf_op jit(solution)/shard_map/ppermute | solution.py:591
  30.4 0.4 collective-permute-start.6
  30.8 0.0 collective-permute-start.7
  30.8 5.1 %collective-permute-done.6 = f32[32,128]{1,0:T(8,128)S(1)} collective-permute-done((f32[32,128]{1,0:T(8,128)S(1)}, f32[32,128]{1,0:T(8,128)S(1)}, u32[]{:S(2)}, u32[]{:S(2)}) %collective-permute-start.6) | collective-permute-done | bytes 16416 | tf_op jit(solution)/shard_map/ppermute | solution.py:591
  36.0 0.0 collective-permute-done.5
  36.0 0.0 collective-permute-done.7
  36.0 0.1 collective-permute-start.8
  36.1 4.4 %shard_map.108 = (f32[32,7,128,128]{3,2,1,0:T(8,128)S(1)}, f32[8,128]{1,0:T(8,128)}) custom-call(f32[32,8,128]{2,1,0:T(8,128)S(1)} %get-tuple-element.42.union), custom_call_target="tpu_custom_call" | custom-call | flops 1000000000 | bytes 15000000 | tf_op jit(solution)/shard_map/pallas_call | solution.py:634
  40.6 0.0 collective-permute-done.8
  40.6 2.8 %collective-permute-start.11 = (f32[32,128]{1,0:T(8,128)S(1)}, f32[32,128]{1,0:T(8,128)S(1)}, u32[]{:S(2)}, u32[]{:S(2)}) collective-permute-start(f32[32,128]{1,0:T(8,128)S(1)} %maximum_add_fusion.pair_rho), channel_id=1, source_target_pairs={{0,6},{1,7},{2,0},{3,1},{4,2},{5,3},{6,4},{7,5},{8,14},{9,15},{10,... | collective-permute-start | bytes 49160 | tf_op jit(solution)/shard_map/ppermute | solution.py:591
  43.4 0.0 collective-permute-start.9
  43.4 0.0 collective-permute-start.10
  43.4 3.6 %collective-permute-done.9 = f32[16,128]{1,0:T(8,128)S(1)} collective-permute-done((f32[16,128]{1,0:T(8,128)S(1)}, f32[16,128]{1,0:T(8,128)S(1)}, u32[]{:S(2)}, u32[]{:S(2)}) %collective-permute-start.9) | collective-permute-done | bytes 8224 | tf_op jit(solution)/shard_map/ppermute | solution.py:597
  47.0 1.9 %collective-permute-done.10 = f32[40,128]{1,0:T(8,128)S(1)} collective-permute-done((f32[40,128]{1,0:T(8,128)S(1)}, f32[40,128]{1,0:T(8,128)S(1)}, u32[]{:S(2)}, u32[]{:S(2)}) %collective-permute-start.10) | collective-permute-done | bytes 20512 | tf_op jit(solution)/shard_map/ppermute | solution.py:591
  48.9 0.0 collective-permute-done.11.above_rho
  49.0 0.0 copy-done.3
  49.0 6.7 %shard_map.109 = (f32[32,128,128]{2,1,0:T(8,128)S(1)}, f32[3,32,128,128]{3,2,1,0:T(8,128)S(1)}, f32[3,32,128]{2,1,0:T(8,128)S(1)}, f32[3,32,128]{2,1,0:T(8,128)S(1)}, f32[3,32,128]{2,1,0:T(8,128)S(1)}) custom-call(s32[32]{0:T(128)} %counts.1, s32[4,32]{1,0:T(4,128)S(1)} %get-tuple-element.50.listed_hbm, f32[2,2]{1,0:T(2,128)S(1)} %copy-done.3, ...), custom_call_target="tpu_custom_call" | custom-call | tf_op jit(solution)/shard_map/pallas_call | solution.py:744
  55.6 0.1 collective-permute-start.12
  55.7 2.0 %collective-permute-start.13 = (f32[3,32,128]{2,1,0:T(8,128)S(1)}, f32[3,32,128]{2,1,0:T(8,128)S(1)}, u32[]{:S(2)}, u32[]{:S(2)}) collective-permute-start(f32[3,32,128]{2,1,0:T(8,128)S(1)} %get-tuple-element.56), channel_id=1, source_target_pairs={{0,2},{1,3},{2,4},{3,5},{4,6},{5,7},{6,0},{7,1},{8,10},{9,11},{10,... | collective-permute-start | bytes 147464 | tf_op jit(solution)/shard_map/ppermute | solution.py:591
  57.7 6.7 %shard_map.110 = (f32[3,32,128,128]{3,2,1,0:T(8,128)S(1)}, f32[3,8,128]{2,1,0:T(8,128)S(1)}) custom-call(s32[32]{0:T(128)} %counts.1, s32[4,32]{1,0:T(4,128)S(1)} %get-tuple-element.50.listed_hbm, f32[2,2]{1,0:T(2,128)S(1)} %copy-done.3, f32[32,7,128,128]{3,2,1,0:T(8,128)S(1)} %get-tuple-element.49.spread, f32[32,128,128]{2,1,0:T(8,128)S(1)} %get-tuple-element.52.crowd, ...), custom_call_target="tpu_custom_call" | custom-call | flops 1000000000 | bytes 20000000 | tf_op jit(solution)/shard_map/pallas_call | solution.py:779
  64.4 0.0 collective-permute-done.12
  64.4 0.0 collective-permute-done.13
  64.5 0.1 collective-permute-start.15
  64.5 1.6 %collective-permute-start.14 = (f32[3,8,128]{2,1,0:T(8,128)S(1)}, f32[3,8,128]{2,1,0:T(8,128)S(1)}, u32[]{:S(2)}, u32[]{:S(2)}) collective-permute-start(f32[3,8,128]{2,1,0:T(8,128)S(1)} %get-tuple-element.58), channel_id=1, source_target_pairs={{0,7},{1,0},{2,1},{3,2},{4,3},{5,4},{6,5},{7,6},{8,15},{9,8},{10,9... | collective-permute-start | bytes 36872 | tf_op jit(solution)/shard_map/ppermute | solution.py:591
  66.2 0.0 collective-permute-done.15
  66.2 0.1 collective-permute-start.16
  66.2 0.0 copy-start
  66.3 0.0 copy-start.1
  66.3 0.0 copy-start.2
  66.3 11.2 %shard_map.111.acc = f32[3,32,8,128]{3,2,1,0:T(8,128)S(1)} custom-call(s32[32]{0:T(128)} %counts.1, s32[2,32]{1,0:T(2,128)} %bitcast.9, f32[2,2]{1,0:T(2,128)S(1)} %copy-done.3, f32[32,8,128]{2,1,0:T(8,128)S(1)} %get-tuple-element.42.union, f32[32,7,128,128]{3,2,1,0:T(8,128)S(1)} %get-tuple-element.49.spread, f32[32,128,128]{2,1,0:T(8,128)S(1)} %get-tuple-element.52.crowd, ...), custom_call_target="tpu_custom_call" | custom-call | flops 2000000000 | bytes 20000000 | tf_op jit(solution)/shard_map/pallas_call | solution.py:800
  77.5 0.0 collective-permute-done.14.face_back
  77.5 0.0 collective-permute-done.16.top_back
  77.6 1.4 %shard_map.112 = (f32[3,4096]{1,0:T(4,128)}, f32[3,4096]{1,0:T(4,128)}) custom-call(s32[32]{0:T(128)S(1)} %copy-done.2, f32[3,4096]{1,0:T(4,128)S(1)} %copy-done, f32[3,4096]{1,0:T(4,128)S(1)} %copy-done.1, f32[3,32,8,128]{3,2,1,0:T(8,128)S(1)} %shard_map.111.acc, f32[3,8,128]{2,1,0:T(8,128)S(1)} %collective-permute-done.14.face_back, ...), custom_call_target="tpu_custom_call" | custom-call | tf_op jit(solution)/shard_map/pallas_call | solution.py:816
  (22 shorter events, 0.1 us)
Async XLA Ops:
  1.7 5.3 %collective-permute-start.1 = (f32[16,8,128]{2,1,0:T(8,128)S(1)}, f32[16,8,128]{2,1,0:T(8,128)S(1)}, u32[]{:S(2)}, u32[]{:S(2)}) collective-permute-start(f32[16,8,128]{2,1,0:T(8,128)S(1)} %get-tuple-element.33), channel_id=1, source_target_pairs={{0,9},{1,8},{2,11},{3,10},{4,13},{5,12},{6,15},{7,14},{8,17},{9,16... | collective-permute-start | bytes 196616 | tf_op jit(solution)/shard_map/ppermute | solution.py:597
  2.7 5.8 %collective-permute-start = (f32[16,8,128]{2,1,0:T(8,128)S(1)}, f32[16,8,128]{2,1,0:T(8,128)S(1)}, u32[]{:S(2)}, u32[]{:S(2)}) collective-permute-start(f32[16,8,128]{2,1,0:T(8,128)S(1)} %get-tuple-element.33), channel_id=1, source_target_pairs={{0,8},{1,9},{2,10},{3,11},{4,12},{5,13},{6,14},{7,15},{8,16},{9,17... | collective-permute-start | bytes 196616 | tf_op jit(solution)/shard_map/ppermute | solution.py:597
  3.3 13.2 %collective-permute-start.2 = (f32[8,8,128]{2,1,0:T(8,128)S(1)}, f32[8,8,128]{2,1,0:T(8,128)S(1)}, u32[]{:S(2)}, u32[]{:S(2)}) collective-permute-start(f32[8,8,128]{2,1,0:T(8,128)S(1)} %get-tuple-element.38), channel_id=1, source_target_pairs={{0,1},{1,2},{2,3},{3,4},{4,5},{5,6},{6,7},{7,0},{8,9},{9,10},{10,1... | collective-permute-start | bytes 98312 | tf_op jit(solution)/shard_map/ppermute | solution.py:591
  8.4 8.0 %collective-permute-start.4 = (f32[32,8,128]{2,1,0:T(8,128)S(1)}, f32[32,8,128]{2,1,0:T(8,128)S(1)}, u32[]{:S(2)}, u32[]{:S(2)}) collective-permute-start(f32[32,8,128]{2,1,0:T(8,128)S(1)} %constant_dynamic-update-slice_fusion), channel_id=1, source_target_pairs={{0,6},{1,7},{2,0},{3,1},{4,2},{5,3},{6,4},{7,5},{8,14},{9,15},{10,... | collective-permute-start | bytes 393224 | tf_op jit(solution)/shard_map/ppermute | solution.py:591
  12.1 6.9 %collective-permute-start.3 = (f32[32,8,128]{2,1,0:T(8,128)S(1)}, f32[32,8,128]{2,1,0:T(8,128)S(1)}, u32[]{:S(2)}, u32[]{:S(2)}) collective-permute-start(f32[32,8,128]{2,1,0:T(8,128)S(1)} %constant_dynamic-update-slice_fusion), channel_id=1, source_target_pairs={{0,2},{1,3},{2,4},{3,5},{4,6},{5,7},{6,0},{7,1},{8,10},{9,11},{10,... | collective-permute-start | bytes 393224 | tf_op jit(solution)/shard_map/ppermute | solution.py:591
  19.0 30.0 %copy-start.3 = (f32[2,2]{1,0:T(2,128)S(1)}, f32[2,2]{1,0:T(2,128)}, u32[]{:S(2)}) copy-start(f32[2,2]{1,0:T(2,128)} %a_table.5) | copy-start | bytes 52
  28.7 7.2 %collective-permute-start.5 = (f32[40,128]{1,0:T(8,128)S(1)}, f32[40,128]{1,0:T(8,128)S(1)}, u32[]{:S(2)}, u32[]{:S(2)}) collective-permute-start(f32[40,128]{1,0:T(8,128)S(1)} %get-tuple-element.43), channel_id=1, source_target_pairs={{0,6},{1,7},{2,0},{3,1},{4,2},{5,3},{6,4},{7,5},{8,14},{9,15},{10,... | collective-permute-start | bytes 61448 | tf_op jit(solution)/shard_map/ppermute | solution.py:591
  30.4 5.5 %collective-permute-start.6 = (f32[32,128]{1,0:T(8,128)S(1)}, f32[32,128]{1,0:T(8,128)S(1)}, u32[]{:S(2)}, u32[]{:S(2)}) collective-permute-start(f32[32,128]{1,0:T(8,128)S(1)} %get-tuple-element.44), channel_id=1, source_target_pairs={{0,2},{1,3},{2,4},{3,5},{4,6},{5,7},{6,0},{7,1},{8,10},{9,11},{10,... | collective-permute-start | bytes 49160 | tf_op jit(solution)/shard_map/ppermute | solution.py:591
  30.8 5.2 %collective-permute-start.7 = (f32[16,128]{1,0:T(8,128)S(1)}, f32[16,128]{1,0:T(8,128)S(1)}, u32[]{:S(2)}, u32[]{:S(2)}) collective-permute-start(f32[16,128]{1,0:T(8,128)S(1)} %get-tuple-element.45), channel_id=1, source_target_pairs={{0,8},{1,9},{2,10},{3,11},{4,12},{5,13},{6,14},{7,15},{8,16},{9,17... | collective-permute-start | bytes 24584 | tf_op jit(solution)/shard_map/ppermute | solution.py:597
  36.0 4.5 %collective-permute-start.8 = (f32[48,128]{1,0:T(8,128)S(1)}, f32[48,128]{1,0:T(8,128)S(1)}, u32[]{:S(2)}, u32[]{:S(2)}) collective-permute-start(f32[48,128]{1,0:T(8,128)S(1)} %pad_maximum_fusion), channel_id=1, source_target_pairs={{0,1},{1,0},{2,3},{3,2},{4,5},{5,4},{6,7},{7,6},{8,9},{9,8},{10,11... | collective-permute-start | bytes 73736 | tf_op jit(solution)/shard_map/ppermute | solution.py:594
  40.6 8.4 %collective-permute-start.11 = (f32[32,128]{1,0:T(8,128)S(1)}, f32[32,128]{1,0:T(8,128)S(1)}, u32[]{:S(2)}, u32[]{:S(2)}) collective-permute-start(f32[32,128]{1,0:T(8,128)S(1)} %maximum_add_fusion.pair_rho), channel_id=1, source_target_pairs={{0,6},{1,7},{2,0},{3,1},{4,2},{5,3},{6,4},{7,5},{8,14},{9,15},{10,... | collective-permute-start | bytes 49160 | tf_op jit(solution)/shard_map/ppermute | solution.py:591
  43.4 3.7 %collective-permute-start.9 = (f32[16,128]{1,0:T(8,128)S(1)}, f32[16,128]{1,0:T(8,128)S(1)}, u32[]{:S(2)}, u32[]{:S(2)}) collective-permute-start(f32[16,128]{1,0:T(8,128)S(1)} %slice.65), channel_id=1, source_target_pairs={{0,24},{1,25},{2,26},{3,27},{4,28},{5,29},{6,30},{7,31},{8,0},{9,1... | collective-permute-start | bytes 24584 | tf_op jit(solution)/shard_map/ppermute | solution.py:597
  43.4 5.6 %collective-permute-start.10 = (f32[40,128]{1,0:T(8,128)S(1)}, f32[40,128]{1,0:T(8,128)S(1)}, u32[]{:S(2)}, u32[]{:S(2)}) collective-permute-start(f32[40,128]{1,0:T(8,128)S(1)} %pad_maximum_fusion.1), channel_id=1, source_target_pairs={{0,2},{1,3},{2,4},{3,5},{4,6},{5,7},{6,0},{7,1},{8,10},{9,11},{10,... | collective-permute-start | bytes 61448 | tf_op jit(solution)/shard_map/ppermute | solution.py:591
  55.6 8.8 %collective-permute-start.12 = (f32[3,32,128]{2,1,0:T(8,128)S(1)}, f32[3,32,128]{2,1,0:T(8,128)S(1)}, u32[]{:S(2)}, u32[]{:S(2)}) collective-permute-start(f32[3,32,128]{2,1,0:T(8,128)S(1)} %get-tuple-element.55), channel_id=1, source_target_pairs={{0,6},{1,7},{2,0},{3,1},{4,2},{5,3},{6,4},{7,5},{8,14},{9,15},{10,... | collective-permute-start | bytes 147464 | tf_op jit(solution)/shard_map/ppermute | solution.py:591
  55.7 8.7 %collective-permute-start.13 = (f32[3,32,128]{2,1,0:T(8,128)S(1)}, f32[3,32,128]{2,1,0:T(8,128)S(1)}, u32[]{:S(2)}, u32[]{:S(2)}) collective-permute-start(f32[3,32,128]{2,1,0:T(8,128)S(1)} %get-tuple-element.56), channel_id=1, source_target_pairs={{0,2},{1,3},{2,4},{3,5},{4,6},{5,7},{6,0},{7,1},{8,10},{9,11},{10,... | collective-permute-start | bytes 147464 | tf_op jit(solution)/shard_map/ppermute | solution.py:591
  64.5 1.7 %collective-permute-start.15 = (f32[3,16,128]{2,1,0:T(8,128)S(1)}, f32[3,16,128]{2,1,0:T(8,128)S(1)}, u32[]{:S(2)}, u32[]{:S(2)}) collective-permute-start(f32[3,16,128]{2,1,0:T(8,128)S(1)} %slice.69), channel_id=1, source_target_pairs={{0,1},{1,0},{2,3},{3,2},{4,5},{5,4},{6,7},{7,6},{8,9},{9,8},{10,11... | collective-permute-start | bytes 73736 | tf_op jit(solution)/shard_map/ppermute | solution.py:594
  64.5 13.0 %collective-permute-start.14 = (f32[3,8,128]{2,1,0:T(8,128)S(1)}, f32[3,8,128]{2,1,0:T(8,128)S(1)}, u32[]{:S(2)}, u32[]{:S(2)}) collective-permute-start(f32[3,8,128]{2,1,0:T(8,128)S(1)} %get-tuple-element.58), channel_id=1, source_target_pairs={{0,7},{1,0},{2,1},{3,2},{4,3},{5,4},{6,5},{7,6},{8,15},{9,8},{10,9... | collective-permute-start | bytes 36872 | tf_op jit(solution)/shard_map/ppermute | solution.py:591
  66.2 11.4 %collective-permute-start.16 = (f32[3,16,128]{2,1,0:T(8,128)S(1)}, f32[3,16,128]{2,1,0:T(8,128)S(1)}, u32[]{:S(2)}, u32[]{:S(2)}) collective-permute-start(f32[3,16,128]{2,1,0:T(8,128)S(1)} %slice_add_fusion), channel_id=1, source_target_pairs={{0,24},{1,25},{2,26},{3,27},{4,28},{5,29},{6,30},{7,31},{8,0},{9,1... | collective-permute-start | bytes 73736 | tf_op jit(solution)/shard_map/ppermute | solution.py:597
  66.2 11.3 %copy-start = (f32[3,4096]{1,0:T(4,128)S(1)}, f32[3,4096]{1,0:T(4,128)}, u32[]{:S(2)}) copy-start(f32[3,4096]{1,0:T(4,128)} %pos.1) | copy-start | bytes 147460
  66.3 11.3 %copy-start.1 = (f32[3,4096]{1,0:T(4,128)S(1)}, f32[3,4096]{1,0:T(4,128)}, u32[]{:S(2)}) copy-start(f32[3,4096]{1,0:T(4,128)} %vel.1) | copy-start | bytes 147460
  66.3 11.3 %copy-start.2 = (s32[32]{0:T(128)S(1)}, s32[32]{0:T(128)}, u32[]{:S(2)}) copy-start(s32[32]{0:T(128)} %counts.1) | copy-start | bytes 388

commit v7 on v6

--- a/solution.py
+++ b/solution.py
@@ -100,13 +100,13 @@
     return out
 
 
-def by_fours(tiles, body):
+def by_eights(tiles, body):
     def step(i, carry):
-        for t in range(4):
-            body(4 * i + t)
+        for t in range(8):
+            body(8 * i + t)
         return carry
 
-    lax.fori_loop(0, tiles // 4, step, 0)
+    lax.fori_loop(0, tiles // 8, step, 0)
 
 
 def fold(ref, first, *at):
@@ -231,7 +231,7 @@
             row = union[g, pl.ds(c, 1), :]
             spread_row(row * friction if 3 <= c < 6 else row, store)
 
-    by_fours(tiles, fill)
+    by_eights(tiles, fill)
 
 
 def local_partner(counts, nbr):
@@ -380,7 +380,7 @@
     def collect(t):
         acc[t] = local_acc[t] + row_sums(sums, t)
 
-    by_fours(tiles, collect)
+    by_eights(tiles, collect)
     for t in range(0, tiles, 8):
         own_out[pl.ds(t, 8), :] = fold(acc, t)
     top_out[...] = own_out[pl.ds(tiles - upper, upper)]
@@ -455,7 +455,7 @@
 
         spread_row(density[pl.ds(g, 1), :] * (crowd_scale * density_scale), store)
 
-    by_fours(tiles, fill)
+    by_eights(tiles, fill)
     wait()
 
     def pair(g, k, h, n):
@@ -541,7 +541,7 @@
         for c in range(3):
             acc[c, t] += row_sums(sums, c, t)
 
-    by_fours(tiles, collect)
+    by_eights(tiles, collect)
 
 
 def finish_kernel(counts, pos, vel, acc, face_back, top_back, pos_out, vel_out):

time: 79.3 us -> 78.6 us (level); the launches traced: 78.9 us -> 77.2 us
  Pallas kernels: 48 us -> 46.3 us
    ppermute x10, waiting for transfers between devices: 9.56 us -> 8.57 us  [lateral(): lax.ppermute(value, 'lat', [(m, (m + by) % places) for m in range(places)])]
    pallas_call x2, Pallas kernels: 6.99 us -> 6.12 us  [spread_rows(): pl.pallas_call(spread_kernel, out_shape=(sds(tiles, channels, width, widt...]
  transfers between devices with their start and end apart: 17 -> 17, of which waited for: 6 -> 7; matrix products, arithmetic and copies ran while one was open for 0% -> 0% of each run, Pallas kernels for 37% -> 36%
where the time goes in v7:
time: 78.6 us; the launch traced here: 77.2 us
  Pallas kernels  46.3 us (59%)
  waiting for transfers between devices  15.4 us (20%)
  starting transfers between devices  14.4 us (18%)
  between operations  0.9 us (1%)
    ppermute x10, starting transfers between devices, lateral(): lax.ppermute(value, 'lat', [(m, (m + by) % places) for m in range(places)])  12.7 us
    pallas_call x1, Pallas kernels, on_device(): pl.pallas_call(local_force_kernel, out_shape=sds(3, tiles, 8, width), in_...  10.6 us
    pallas_call x1, Pallas kernels, on_device(): pl.pallas_call(functools.partial(ghost_density_kernel, *sizes), out_shape...  9.7 us
    ppermute x10, waiting for transfers between devices, lateral(): lax.ppermute(value, 'lat', [(m, (m + by) % places) for m in range(places)])  8.57 us
    ppermute x5, waiting for transfers between devices, climb(): lax.ppermute(value, both, [(l * places + m, (l + by) % layers * places +...  6.87 us
    pallas_call x1, Pallas kernels, on_device(): pl.pallas_call(functools.partial(cross_force_kernel, columns, faces), out...  6.67 us
    pallas_call x1, Pallas kernels, on_device(): pl.pallas_call(functools.partial(face_force_kernel, columns), out_shape=(...  6.4 us
    pallas_call x2, Pallas kernels, spread_rows(): pl.pallas_call(spread_kernel, out_shape=(sds(tiles, channels, width, widt...  6.12 us
  transfers between devices with their start and end apart: 17, of which 7 were waited for; matrix products, arithmetic and copies ran while one was open for 0% of the time, Pallas kernels for 36%

profile of v7, /device:TPU:4, one launch (start us, length us, event | category | flops | bytes accessed | tf_op | source)
XLA Modules:
  0.0 77.2 jit_solution(5925949068263318829)
XLA Ops:
  0.6 1.0 %shard_map.104 = (f32[32,8,128]{2,1,0:T(8,128)S(1)}, f32[16,8,128]{2,1,0:T(8,128)S(1)}, f32[8,8,128]{2,1,0:T(8,128)S(1)}) custom-call(f32[3,4096]{1,0:T(4,128)} %pos.1, f32[3,4096]{1,0:T(4,128)} %vel.1, s32[32,128]{1,0:T(8,128)} %bitcast.7, s32[32]{0:T(128)} %counts.1, s32[5,1,12]{2,1,0:T(1,128)} %bitcast.10), custom_call_target="tpu_custom_call" | custom-call | tf_op jit(solution)/shard_map/pallas_call | solution.py:615
  1.7 1.0 %collective-permute-start.1 = (f32[16,8,128]{2,1,0:T(8,128)S(1)}, f32[16,8,128]{2,1,0:T(8,128)S(1)}, u32[]{:S(2)}, u32[]{:S(2)}) collective-permute-start(f32[16,8,128]{2,1,0:T(8,128)S(1)} %get-tuple-element.33), channel_id=1, source_target_pairs={{0,9},{1,8},{2,11},{3,10},{4,13},{5,12},{6,15},{7,14},{8,17},{9,16... | collective-permute-start | bytes 196616 | tf_op jit(solution)/shard_map/ppermute | solution.py:597
  2.7 0.6 collective-permute-start
  3.3 0.1 collective-permute-start.2
  3.3 2.0 %shard_map.105 = (f32[32,3,128,128]{3,2,1,0:T(8,128)S(1)}, f32[8,128]{1,0:T(8,128)}) custom-call(f32[32,8,128]{2,1,0:T(8,128)S(1)} %get-tuple-element.42.union), custom_call_target="tpu_custom_call" | custom-call | flops 1000000000 | bytes 15000000 | tf_op jit(solution)/shard_map/pallas_call | solution.py:634
  5.4 1.6 %collective-permute-done.1.flip = f32[16,8,128]{2,1,0:T(8,128)S(1)} collective-permute-done((f32[16,8,128]{2,1,0:T(8,128)S(1)}, f32[16,8,128]{2,1,0:T(8,128)S(1)}, u32[]{:S(2)}, u32[]{:S(2)}) %collective-permute-start.1) | collective-permute-done | bytes 65568 | tf_op jit(solution)/shard_map/ppermute | solution.py:597
  7.0 1.4 %collective-permute-done.near = f32[16,8,128]{2,1,0:T(8,128)S(1)} collective-permute-done((f32[16,8,128]{2,1,0:T(8,128)S(1)}, f32[16,8,128]{2,1,0:T(8,128)S(1)}, u32[]{:S(2)}, u32[]{:S(2)}) %collective-permute-start) | collective-permute-done | bytes 65568 | tf_op jit(solution)/shard_map/ppermute | solution.py:597
  8.4 3.7 %collective-permute-start.4 = (f32[32,8,128]{2,1,0:T(8,128)S(1)}, f32[32,8,128]{2,1,0:T(8,128)S(1)}, u32[]{:S(2)}, u32[]{:S(2)}) collective-permute-start(f32[32,8,128]{2,1,0:T(8,128)S(1)} %constant_dynamic-update-slice_fusion), channel_id=1, source_target_pairs={{0,6},{1,7},{2,0},{3,1},{4,2},{5,3},{6,4},{7,5},{8,14},{9,15},{10,... | collective-permute-start | bytes 393224 | tf_op jit(solution)/shard_map/ppermute | solution.py:591
  12.1 0.0 collective-permute-start.3
  12.1 0.1 pad_add_fusion.where
  12.2 4.4 %shard_map.106 = (f32[32,8,128]{2,1,0:T(8,128)S(1)}, f32[32,128,128]{2,1,0:T(8,128)S(1)}) custom-call(s32[32]{0:T(128)} %counts.1, s32[2,32]{1,0:T(2,128)} %bitcast.8, f32[32,8,128]{2,1,0:T(8,128)S(1)} %get-tuple-element.42.union, f32[32,3,128,128]{3,2,1,0:T(8,128)S(1)} %get-tuple-element.35.spread), custom_call_target="tpu_custom_call" | custom-call | flops 1000000000 | bytes 15000000 | tf_op jit(solution)/shard_map/pallas_call | solution.py:655
  16.6 0.0 collective-permute-done.2.face
  16.6 0.0 collective-permute-done.4.above
  16.6 2.3 %collective-permute-done.3.below = f32[32,8,128]{2,1,0:T(8,128)S(1)} collective-permute-done((f32[32,8,128]{2,1,0:T(8,128)S(1)}, f32[32,8,128]{2,1,0:T(8,128)S(1)}, u32[]{:S(2)}, u32[]{:S(2)}) %collective-permute-start.3) | collective-permute-done | bytes 131104 | tf_op jit(solution)/shard_map/ppermute | solution.py:591
  19.0 9.7 %shard_map.107 = (f32[32,128]{1,0:T(8,128)S(1)}, f32[16,128]{1,0:T(8,128)S(1)}, f32[8,128]{1,0:T(8,128)S(1)}, f32[32,128]{1,0:T(8,128)S(1)}, f32[40,128]{1,0:T(8...) custom-call(s32[2]{0:T(128)S(1)} %pad_add_fusion.where, ...), custom_call_target="tpu_custom_call", output_to_operand_aliasing={{6}: (6, {})} | custom-call | tf_op jit(solution)/shard_map/pallas_call | solution.py:679
  28.7 0.8 %collective-permute-start.5 = (f32[40,128]{1,0:T(8,128)S(1)}, f32[40,128]{1,0:T(8,128)S(1)}, u32[]{:S(2)}, u32[]{:S(2)}) collective-permute-start(f32[40,128]{1,0:T(8,128)S(1)} %get-tuple-element.43), channel_id=1, source_target_pairs={{0,6},{1,7},{2,0},{3,1},{4,2},{5,3},{6,4},{7,5},{8,14},{9,15},{10,... | collective-permute-start | bytes 61448 | tf_op jit(solution)/shard_map/ppermute | solution.py:591
  29.5 1.3 %collective-permute-start.6 = (f32[32,128]{1,0:T(8,128)S(1)}, f32[32,128]{1,0:T(8,128)S(1)}, u32[]{:S(2)}, u32[]{:S(2)}) collective-permute-start(f32[32,128]{1,0:T(8,128)S(1)} %get-tuple-element.44), channel_id=1, source_target_pairs={{0,2},{1,3},{2,4},{3,5},{4,6},{5,7},{6,0},{7,1},{8,10},{9,11},{10,... | collective-permute-start | bytes 49160 | tf_op jit(solution)/shard_map/ppermute | solution.py:591
  30.8 0.0 collective-permute-start.7
  30.8 4.3 %collective-permute-done.6 = f32[32,128]{1,0:T(8,128)S(1)} collective-permute-done((f32[32,128]{1,0:T(8,128)S(1)}, f32[32,128]{1,0:T(8,128)S(1)}, u32[]{:S(2)}, u32[]{:S(2)}) %collective-permute-start.6) | collective-permute-done | bytes 16416 | tf_op jit(solution)/shard_map/ppermute | solution.py:591
  35.0 0.0 collective-permute-done.5
  35.1 0.3 collective-permute-done.7
  35.3 0.0 collective-permute-start.8
  35.3 4.1 %shard_map.108 = (f32[32,7,128,128]{3,2,1,0:T(8,128)S(1)}, f32[8,128]{1,0:T(8,128)}) custom-call(f32[32,8,128]{2,1,0:T(8,128)S(1)} %get-tuple-element.42.union), custom_call_target="tpu_custom_call" | custom-call | flops 1000000000 | bytes 15000000 | tf_op jit(solution)/shard_map/pallas_call | solution.py:634
  39.4 0.0 collective-permute-done.8
  39.5 2.6 %collective-permute-start.11 = (f32[32,128]{1,0:T(8,128)S(1)}, f32[32,128]{1,0:T(8,128)S(1)}, u32[]{:S(2)}, u32[]{:S(2)}) collective-permute-start(f32[32,128]{1,0:T(8,128)S(1)} %maximum_add_fusion.pair_rho), channel_id=1, source_target_pairs={{0,6},{1,7},{2,0},{3,1},{4,2},{5,3},{6,4},{7,5},{8,14},{9,15},{10,... | collective-permute-start | bytes 49160 | tf_op jit(solution)/shard_map/ppermute | solution.py:591
  42.1 0.0 collective-permute-start.9
  42.1 0.1 collective-permute-start.10
  42.2 3.6 %collective-permute-done.9 = f32[16,128]{1,0:T(8,128)S(1)} collective-permute-done((f32[16,128]{1,0:T(8,128)S(1)}, f32[16,128]{1,0:T(8,128)S(1)}, u32[]{:S(2)}, u32[]{:S(2)}) %collective-permute-start.9) | collective-permute-done | bytes 8224 | tf_op jit(solution)/shard_map/ppermute | solution.py:597
  45.8 1.9 %collective-permute-done.10 = f32[40,128]{1,0:T(8,128)S(1)} collective-permute-done((f32[40,128]{1,0:T(8,128)S(1)}, f32[40,128]{1,0:T(8,128)S(1)}, u32[]{:S(2)}, u32[]{:S(2)}) %collective-permute-start.10) | collective-permute-done | bytes 20512 | tf_op jit(solution)/shard_map/ppermute | solution.py:591
  47.7 0.0 collective-permute-done.11.above_rho
  47.7 0.0 copy-done.3
  47.7 6.7 %shard_map.109 = (f32[32,128,128]{2,1,0:T(8,128)S(1)}, f32[3,32,128,128]{3,2,1,0:T(8,128)S(1)}, f32[3,32,128]{2,1,0:T(8,128)S(1)}, f32[3,32,128]{2,1,0:T(8,128)S(1)}, f32[3,32,128]{2,1,0:T(8,128)S(1)}) custom-call(s32[32]{0:T(128)} %counts.1, s32[4,32]{1,0:T(4,128)S(1)} %get-tuple-element.50.listed_hbm, f32[2,2]{1,0:T(2,128)S(1)} %copy-done.3, ...), custom_call_target="tpu_custom_call" | custom-call | tf_op jit(solution)/shard_map/pallas_call | solution.py:744
  54.4 0.1 collective-permute-start.12
  54.4 2.0 %collective-permute-start.13 = (f32[3,32,128]{2,1,0:T(8,128)S(1)}, f32[3,32,128]{2,1,0:T(8,128)S(1)}, u32[]{:S(2)}, u32[]{:S(2)}) collective-permute-start(f32[3,32,128]{2,1,0:T(8,128)S(1)} %get-tuple-element.56), channel_id=1, source_target_pairs={{0,2},{1,3},{2,4},{3,5},{4,6},{5,7},{6,0},{7,1},{8,10},{9,11},{10,... | collective-permute-start | bytes 147464 | tf_op jit(solution)/shard_map/ppermute | solution.py:591
  56.5 6.4 %shard_map.110 = (f32[3,32,128,128]{3,2,1,0:T(8,128)S(1)}, f32[3,8,128]{2,1,0:T(8,128)S(1)}) custom-call(s32[32]{0:T(128)} %counts.1, s32[4,32]{1,0:T(4,128)S(1)} %get-tuple-element.50.listed_hbm, f32[2,2]{1,0:T(2,128)S(1)} %copy-done.3, f32[32,7,128,128]{3,2,1,0:T(8,128)S(1)} %get-tuple-element.49.spread, f32[32,128,128]{2,1,0:T(8,128)S(1)} %get-tuple-element.52.crowd, ...), custom_call_target="tpu_custom_call" | custom-call | flops 1000000000 | bytes 20000000 | tf_op jit(solution)/shard_map/pallas_call | solution.py:779
  62.9 0.0 collective-permute-done.12
  62.9 0.0 collective-permute-done.13
  62.9 0.1 collective-permute-start.15
  63.0 2.1 %collective-permute-start.14 = (f32[3,8,128]{2,1,0:T(8,128)S(1)}, f32[3,8,128]{2,1,0:T(8,128)S(1)}, u32[]{:S(2)}, u32[]{:S(2)}) collective-permute-start(f32[3,8,128]{2,1,0:T(8,128)S(1)} %get-tuple-element.58), channel_id=1, source_target_pairs={{0,7},{1,0},{2,1},{3,2},{4,3},{5,4},{6,5},{7,6},{8,15},{9,8},{10,9... | collective-permute-start | bytes 36872 | tf_op jit(solution)/shard_map/ppermute | solution.py:591
  65.1 0.0 collective-permute-done.15
  65.1 0.1 collective-permute-start.16
  65.2 0.0 copy-start
  65.2 0.0 copy-start.1
  65.2 0.0 copy-start.2
  65.2 10.6 %shard_map.111.acc = f32[3,32,8,128]{3,2,1,0:T(8,128)S(1)} custom-call(s32[32]{0:T(128)} %counts.1, s32[2,32]{1,0:T(2,128)} %bitcast.9, f32[2,2]{1,0:T(2,128)S(1)} %copy-done.3, f32[32,8,128]{2,1,0:T(8,128)S(1)} %get-tuple-element.42.union, f32[32,7,128,128]{3,2,1,0:T(8,128)S(1)} %get-tuple-element.49.spread, f32[32,128,128]{2,1,0:T(8,128)S(1)} %get-tuple-element.52.crowd, ...), custom_call_target="tpu_custom_call" | custom-call | flops 2000000000 | bytes 20000000 | tf_op jit(solution)/shard_map/pallas_call | solution.py:800
  75.8 0.0 collective-permute-done.14.face_back
  75.8 0.0 collective-permute-done.16.top_back
  75.9 1.4 %shard_map.112 = (f32[3,4096]{1,0:T(4,128)}, f32[3,4096]{1,0:T(4,128)}) custom-call(s32[32]{0:T(128)S(1)} %copy-done.2, f32[3,4096]{1,0:T(4,128)S(1)} %copy-done, f32[3,4096]{1,0:T(4,128)S(1)} %copy-done.1, f32[3,32,8,128]{3,2,1,0:T(8,128)S(1)} %shard_map.111.acc, f32[3,8,128]{2,1,0:T(8,128)S(1)} %collective-permute-done.14.face_back, ...), custom_call_target="tpu_custom_call" | custom-call | tf_op jit(solution)/shard_map/pallas_call | solution.py:816
  (22 shorter events, 0.1 us)
Async XLA Ops:
  1.7 5.3 %collective-permute-start.1 = (f32[16,8,128]{2,1,0:T(8,128)S(1)}, f32[16,8,128]{2,1,0:T(8,128)S(1)}, u32[]{:S(2)}, u32[]{:S(2)}) collective-permute-start(f32[16,8,128]{2,1,0:T(8,128)S(1)} %get-tuple-element.33), channel_id=1, source_target_pairs={{0,9},{1,8},{2,11},{3,10},{4,13},{5,12},{6,15},{7,14},{8,17},{9,16... | collective-permute-start | bytes 196616 | tf_op jit(solution)/shard_map/ppermute | solution.py:597
  2.7 5.8 %collective-permute-start = (f32[16,8,128]{2,1,0:T(8,128)S(1)}, f32[16,8,128]{2,1,0:T(8,128)S(1)}, u32[]{:S(2)}, u32[]{:S(2)}) collective-permute-start(f32[16,8,128]{2,1,0:T(8,128)S(1)} %get-tuple-element.33), channel_id=1, source_target_pairs={{0,8},{1,9},{2,10},{3,11},{4,12},{5,13},{6,14},{7,15},{8,16},{9,17... | collective-permute-start | bytes 196616 | tf_op jit(solution)/shard_map/ppermute | solution.py:597
  3.3 13.3 %collective-permute-start.2 = (f32[8,8,128]{2,1,0:T(8,128)S(1)}, f32[8,8,128]{2,1,0:T(8,128)S(1)}, u32[]{:S(2)}, u32[]{:S(2)}) collective-permute-start(f32[8,8,128]{2,1,0:T(8,128)S(1)} %get-tuple-element.38), channel_id=1, source_target_pairs={{0,1},{1,2},{2,3},{3,4},{4,5},{5,6},{6,7},{7,0},{8,9},{9,10},{10,1... | collective-permute-start | bytes 98312 | tf_op jit(solution)/shard_map/ppermute | solution.py:591
  8.4 8.2 %collective-permute-start.4 = (f32[32,8,128]{2,1,0:T(8,128)S(1)}, f32[32,8,128]{2,1,0:T(8,128)S(1)}, u32[]{:S(2)}, u32[]{:S(2)}) collective-permute-start(f32[32,8,128]{2,1,0:T(8,128)S(1)} %constant_dynamic-update-slice_fusion), channel_id=1, source_target_pairs={{0,6},{1,7},{2,0},{3,1},{4,2},{5,3},{6,4},{7,5},{8,14},{9,15},{10,... | collective-permute-start | bytes 393224 | tf_op jit(solution)/shard_map/ppermute | solution.py:591
  12.1 6.9 %collective-permute-start.3 = (f32[32,8,128]{2,1,0:T(8,128)S(1)}, f32[32,8,128]{2,1,0:T(8,128)S(1)}, u32[]{:S(2)}, u32[]{:S(2)}) collective-permute-start(f32[32,8,128]{2,1,0:T(8,128)S(1)} %constant_dynamic-update-slice_fusion), channel_id=1, source_target_pairs={{0,2},{1,3},{2,4},{3,5},{4,6},{5,7},{6,0},{7,1},{8,10},{9,11},{10,... | collective-permute-start | bytes 393224 | tf_op jit(solution)/shard_map/ppermute | solution.py:591
  19.0 28.7 %copy-start.3 = (f32[2,2]{1,0:T(2,128)S(1)}, f32[2,2]{1,0:T(2,128)}, u32[]{:S(2)}) copy-start(f32[2,2]{1,0:T(2,128)} %a_table.5) | copy-start | bytes 52
  28.7 6.4 %collective-permute-start.5 = (f32[40,128]{1,0:T(8,128)S(1)}, f32[40,128]{1,0:T(8,128)S(1)}, u32[]{:S(2)}, u32[]{:S(2)}) collective-permute-start(f32[40,128]{1,0:T(8,128)S(1)} %get-tuple-element.43), channel_id=1, source_target_pairs={{0,6},{1,7},{2,0},{3,1},{4,2},{5,3},{6,4},{7,5},{8,14},{9,15},{10,... | collective-permute-start | bytes 61448 | tf_op jit(solution)/shard_map/ppermute | solution.py:591
  29.5 5.5 %collective-permute-start.6 = (f32[32,128]{1,0:T(8,128)S(1)}, f32[32,128]{1,0:T(8,128)S(1)}, u32[]{:S(2)}, u32[]{:S(2)}) collective-permute-start(f32[32,128]{1,0:T(8,128)S(1)} %get-tuple-element.44), channel_id=1, source_target_pairs={{0,2},{1,3},{2,4},{3,5},{4,6},{5,7},{6,0},{7,1},{8,10},{9,11},{10,... | collective-permute-start | bytes 49160 | tf_op jit(solution)/shard_map/ppermute | solution.py:591
  30.8 4.5 %collective-permute-start.7 = (f32[16,128]{1,0:T(8,128)S(1)}, f32[16,128]{1,0:T(8,128)S(1)}, u32[]{:S(2)}, u32[]{:S(2)}) collective-permute-start(f32[16,128]{1,0:T(8,128)S(1)} %get-tuple-element.45), channel_id=1, source_target_pairs={{0,8},{1,9},{2,10},{3,11},{4,12},{5,13},{6,14},{7,15},{8,16},{9,17... | collective-permute-start | bytes 24584 | tf_op jit(solution)/shard_map/ppermute | solution.py:597
  35.3 4.1 %collective-permute-start.8 = (f32[48,128]{1,0:T(8,128)S(1)}, f32[48,128]{1,0:T(8,128)S(1)}, u32[]{:S(2)}, u32[]{:S(2)}) collective-permute-start(f32[48,128]{1,0:T(8,128)S(1)} %pad_maximum_fusion), channel_id=1, source_target_pairs={{0,1},{1,0},{2,3},{3,2},{4,5},{5,4},{6,7},{7,6},{8,9},{9,8},{10,11... | collective-permute-start | bytes 73736 | tf_op jit(solution)/shard_map/ppermute | solution.py:594
  39.5 8.2 %collective-permute-start.11 = (f32[32,128]{1,0:T(8,128)S(1)}, f32[32,128]{1,0:T(8,128)S(1)}, u32[]{:S(2)}, u32[]{:S(2)}) collective-permute-start(f32[32,128]{1,0:T(8,128)S(1)} %maximum_add_fusion.pair_rho), channel_id=1, source_target_pairs={{0,6},{1,7},{2,0},{3,1},{4,2},{5,3},{6,4},{7,5},{8,14},{9,15},{10,... | collective-permute-start | bytes 49160 | tf_op jit(solution)/shard_map/ppermute | solution.py:591
  42.1 3.7 %collective-permute-start.9 = (f32[16,128]{1,0:T(8,128)S(1)}, f32[16,128]{1,0:T(8,128)S(1)}, u32[]{:S(2)}, u32[]{:S(2)}) collective-permute-start(f32[16,128]{1,0:T(8,128)S(1)} %slice.65), channel_id=1, source_target_pairs={{0,24},{1,25},{2,26},{3,27},{4,28},{5,29},{6,30},{7,31},{8,0},{9,1... | collective-permute-start | bytes 24584 | tf_op jit(solution)/shard_map/ppermute | solution.py:597
  42.1 5.6 %collective-permute-start.10 = (f32[40,128]{1,0:T(8,128)S(1)}, f32[40,128]{1,0:T(8,128)S(1)}, u32[]{:S(2)}, u32[]{:S(2)}) collective-permute-start(f32[40,128]{1,0:T(8,128)S(1)} %pad_maximum_fusion.1), channel_id=1, source_target_pairs={{0,2},{1,3},{2,4},{3,5},{4,6},{5,7},{6,0},{7,1},{8,10},{9,11},{10,... | collective-permute-start | bytes 61448 | tf_op jit(solution)/shard_map/ppermute | solution.py:591
  54.4 8.5 %collective-permute-start.12 = (f32[3,32,128]{2,1,0:T(8,128)S(1)}, f32[3,32,128]{2,1,0:T(8,128)S(1)}, u32[]{:S(2)}, u32[]{:S(2)}) collective-permute-start(f32[3,32,128]{2,1,0:T(8,128)S(1)} %get-tuple-element.55), channel_id=1, source_target_pairs={{0,6},{1,7},{2,0},{3,1},{4,2},{5,3},{6,4},{7,5},{8,14},{9,15},{10,... | collective-permute-start | bytes 147464 | tf_op jit(solution)/shard_map/ppermute | solution.py:591
  54.4 8.4 %collective-permute-start.13 = (f32[3,32,128]{2,1,0:T(8,128)S(1)}, f32[3,32,128]{2,1,0:T(8,128)S(1)}, u32[]{:S(2)}, u32[]{:S(2)}) collective-permute-start(f32[3,32,128]{2,1,0:T(8,128)S(1)} %get-tuple-element.56), channel_id=1, source_target_pairs={{0,2},{1,3},{2,4},{3,5},{4,6},{5,7},{6,0},{7,1},{8,10},{9,11},{10,... | collective-permute-start | bytes 147464 | tf_op jit(solution)/shard_map/ppermute | solution.py:591
  62.9 2.2 %collective-permute-start.15 = (f32[3,16,128]{2,1,0:T(8,128)S(1)}, f32[3,16,128]{2,1,0:T(8,128)S(1)}, u32[]{:S(2)}, u32[]{:S(2)}) collective-permute-start(f32[3,16,128]{2,1,0:T(8,128)S(1)} %slice.69), channel_id=1, source_target_pairs={{0,1},{1,0},{2,3},{3,2},{4,5},{5,4},{6,7},{7,6},{8,9},{9,8},{10,11... | collective-permute-start | bytes 73736 | tf_op jit(solution)/shard_map/ppermute | solution.py:594
  63.0 12.8 %collective-permute-start.14 = (f32[3,8,128]{2,1,0:T(8,128)S(1)}, f32[3,8,128]{2,1,0:T(8,128)S(1)}, u32[]{:S(2)}, u32[]{:S(2)}) collective-permute-start(f32[3,8,128]{2,1,0:T(8,128)S(1)} %get-tuple-element.58), channel_id=1, source_target_pairs={{0,7},{1,0},{2,1},{3,2},{4,3},{5,4},{6,5},{7,6},{8,15},{9,8},{10,9... | collective-permute-start | bytes 36872 | tf_op jit(solution)/shard_map/ppermute | solution.py:591
  65.1 10.7 %collective-permute-start.16 = (f32[3,16,128]{2,1,0:T(8,128)S(1)}, f32[3,16,128]{2,1,0:T(8,128)S(1)}, u32[]{:S(2)}, u32[]{:S(2)}) collective-permute-start(f32[3,16,128]{2,1,0:T(8,128)S(1)} %slice_add_fusion), channel_id=1, source_target_pairs={{0,24},{1,25},{2,26},{3,27},{4,28},{5,29},{6,30},{7,31},{8,0},{9,1... | collective-permute-start | bytes 73736 | tf_op jit(solution)/shard_map/ppermute | solution.py:597
  65.2 10.6 %copy-start = (f32[3,4096]{1,0:T(4,128)S(1)}, f32[3,4096]{1,0:T(4,128)}, u32[]{:S(2)}) copy-start(f32[3,4096]{1,0:T(4,128)} %pos.1) | copy-start | bytes 147460
  65.2 10.6 %copy-start.1 = (f32[3,4096]{1,0:T(4,128)S(1)}, f32[3,4096]{1,0:T(4,128)}, u32[]{:S(2)}) copy-start(f32[3,4096]{1,0:T(4,128)} %vel.1) | copy-start | bytes 147460
  65.2 10.6 %copy-start.2 = (s32[32]{0:T(128)S(1)}, s32[32]{0:T(128)}, u32[]{:S(2)}) copy-start(s32[32]{0:T(128)} %counts.1) | copy-start | bytes 388
